TPU v7x, 512 devices: a whole 4x4x16 slice. The times are simulated.
512 devices in a mesh: rows: 64 (over y, z), probes: 8 (over x, core).
Axes of the slice: x: 4, y: 4, z: 16, core: 2. Of those that a mesh axis runs over, the one named last changes fastest.
Arguments:
- probes: bfloat16 [128, 64, 256], P('rows', 'probes'), parts along dimension 1, may hold values from -6 to 6
- factor: bfloat16 [128, 4, 256, 256], P('rows'), may hold values from -0.125 to 0.125
- inverses: bfloat16 [128, 256, 256], P('rows')
- pattern: int32 [128, 4], replicated, may hold values from -1 to 95, as said below
- owner: int32 [128], replicated, may hold values from 0 to 127, each once
Outputs:
- solution: bfloat16 [128, 64, 256], P('rows', 'probes'), parts along dimension 1
- selected: bfloat16 [128, 40, 256, 256], P('rows', 'probes'), parts along dimension 1
There are 8 independent parts, one for each index of `probes`. A program takes and returns all parts, laid end to end along the dimension named above; an argument that names none is the same for every part. Nothing has to cross between parts.
Inputs may be any that keep to these rules, and one draw needn't show every extreme that they name: `pattern`: Block-rows of the first level have only -1; every other block-row i names 4 different block-columns, all in levels below the level of i, one of them the block-row just before the first block-row of its own level.
All inputs are finite; a program needn't handle non-finite values.
Results may differ from a plain program's by a relative error of at most 0.012.
Values may be sent and summed in bfloat16 or wider, within the bound.
No kernel may reach another device: no remote copies, remote signals or barrier semaphores. Data moves between devices by JAX's collectives and lax.ppermute only.
A program may use at most 64 MiB of HBM per device.

v0:
```python
import jax
import jax.numpy as jnp
from jax import lax
from jax.sharding import PartitionSpec as P

LEVELS = 4


def body(probes, factor, inverses, pattern, owner):
    f32 = jnp.float32
    bf16 = jnp.bfloat16
    me = lax.axis_index("rows")
    local = probes.shape[0]
    count = probes.shape[1]
    total = owner.shape[0]
    width = total // LEVELS
    iota = jnp.arange(total, dtype=jnp.int32)
    row_of_slot = jnp.sum(jnp.where(owner[None, :] == iota[:, None], iota[None, :], 0), axis=1)
    my_slots = me * local + jnp.arange(local, dtype=jnp.int32)
    my_rows = row_of_slot[my_slots]
    my_level = my_rows // width
    cols = pattern[my_rows]
    valid = cols >= 0
    source = owner[jnp.maximum(cols, 0)]
    picker = jnp.logical_and(source[:, :, None] == iota[None, None, :], valid[:, :, None])
    picker_half = picker.astype(bf16)
    picker_full = picker.astype(f32)
    all_probes = lax.all_gather(probes, "rows", axis=0, tiled=True)
    solved_all = jnp.zeros((total, count, probes.shape[2]), bf16)
    own_solved = jnp.zeros_like(probes)
    for level in range(LEVELS):
        near = jnp.einsum(
            "rkd,dpb->rkpb", picker_half, solved_all, preferred_element_type=f32
        ).astype(bf16)
        partial_value = jnp.einsum("rkpb,rkab->rpa", near, factor, preferred_element_type=f32)
        resid = (probes.astype(f32) - partial_value).astype(bf16)
        value = jnp.einsum("rpb,rab->rpa", resid, inverses, preferred_element_type=f32).astype(bf16)
        own_solved = jnp.where((my_level == level)[:, None, None], value, own_solved)
        if level < LEVELS - 1:
            solved_all = lax.all_gather(own_solved, "rows", axis=0, tiled=True)
    accum = jnp.zeros(probes.shape, f32)
    own_back = jnp.zeros_like(probes)
    for level in range(LEVELS - 1, -1, -1):
        start = (own_solved.astype(f32) - accum).astype(bf16)
        value = jnp.einsum("rpb,rba->rpa", start, inverses, preferred_element_type=f32).astype(bf16)
        active = my_level == level
        own_back = jnp.where(active[:, None, None], value, own_back)
        if level > 0:
            terms = jnp.einsum("rpa,rkab->rkpb", own_back, factor, preferred_element_type=f32)
            terms = terms * active.astype(f32)[:, None, None, None]
            outgoing = jnp.einsum(
                "rkd,rkpb->dpb", picker_full, terms, precision=lax.Precision.HIGHEST
            )
            arrived = lax.all_to_all(outgoing, "rows", split_axis=0, concat_axis=0, tiled=True)
            pieces = arrived.reshape((total // local, local) + arrived.shape[1:])
            accum = accum + jnp.sum(pieces, axis=0)
    near_probes = jnp.einsum(
        "rkd,dpb->rkpb", picker_half, all_probes, preferred_element_type=f32
    ).astype(bf16)
    off = jnp.einsum("rpa,rkpb->rkab", own_back, near_probes, preferred_element_type=f32)
    diag = jnp.einsum("rpa,rpb->rab", own_back, probes, preferred_element_type=f32)
    selected = (jnp.concatenate([off, diag[:, None]], axis=1) / count).astype(bf16)
    return (own_back, selected)


def solution(mesh):
    return jax.shard_map(
        body,
        mesh=mesh,
        in_specs=(
            P("rows", "probes", None),
            P("rows", None, None, None),
            P("rows", None, None),
            P(),
            P(),
        ),
        out_specs=(P("rows", "probes", None), P("rows", "probes", None, None)),
        check_vma=False,
    )
```

profile of v0, /device:TPU:6, one launch (start us, length us, event | category | flops | bytes accessed | tf_op | source)
XLA Modules:
  0.0 554.9 jit_solution(11682396132871699083)
XLA Ops:
  0.6 0.0 copy-start
  0.7 0.8 select_reduce_fusion
  1.5 0.0 copy-start.1
  1.5 0.0 copy-start.2
  1.5 0.6 gather_fusion
  2.2 0.8 copy.38
  3.0 0.6 gather_fusion.1
  3.6 0.1 reshape.131
  3.7 1.3 gather_fusion.2
  5.0 0.1 reshape.130
  5.1 0.1 fusion.55
  5.2 0.1 convolution_convert_fusion.4
  5.3 0.0 copy-done
  5.3 1.5 fusion.12
  6.8 106.7 %all_gather.12 = bf16[128,8,256]{2,1,0:T(8,128)(2,1)S(1)} all-gather(bf16[2,8,256]{2,1,0:T(8,128)(2,1)S(1)} %fusion.12), channel_id=1, replica_groups=mesh['rows'=64,'probes'=8] {'rows'}, dimensions={0}, use_global_device_ids=true | all-gather | bytes 532480 | tf_op jit(solution)/shard_map/all_gather | solution.py:40
  113.4 0.2 convolution_convert_fusion.3
  113.6 0.0 copy-done.1
  113.6 0.0 copy-done.2
  113.6 0.5 fusion.13
  114.1 98.5 %all_gather.13 = bf16[128,8,256]{2,1,0:T(8,128)(2,1)S(1)} all-gather(bf16[2,8,256]{2,1,0:T(8,128)(2,1)S(1)} %fusion.13), channel_id=1, replica_groups=mesh['rows'=64,'probes'=8] {'rows'}, dimensions={0}, use_global_device_ids=true | all-gather | bytes 532480 | tf_op jit(solution)/shard_map/all_gather | solution.py:40
  212.6 0.2 convolution_convert_fusion.2
  212.8 0.5 fusion.14
  213.3 104.4 %all_gather.14 = bf16[128,8,256]{2,1,0:T(8,128)(2,1)S(1)} all-gather(bf16[2,8,256]{2,1,0:T(8,128)(2,1)S(1)} %fusion.14), channel_id=1, replica_groups=mesh['rows'=64,'probes'=8] {'rows'}, dimensions={0}, use_global_device_ids=true | all-gather | bytes 532480 | tf_op jit(solution)/shard_map/all_gather | solution.py:40
  317.7 0.2 convolution_convert_fusion.1
  317.9 0.5 fusion.15
  318.4 0.2 fusion.16
  318.5 0.3 fusion.3
  318.8 0.7 convolution_bitcast_fusion.3
  319.4 0.6 copy.47
  320.0 60.5 %all_to_all.15 = f32[128,8,256]{2,1,0:T(8,128)S(1)} all-to-all(f32[128,8,256]{2,1,0:T(8,128)S(1)} %copy.47), channel_id=1, replica_groups=mesh['rows'=64,'probes'=8] {'rows'}, dimensions={0} | all-to-all | bytes 2097152 | tf_op jit(solution)/shard_map/all_to_all | solution.py:54
  380.5 0.1 reduce_sum.37
  380.6 0.1 fusion.17
  380.8 0.2 fusion.2
  381.0 0.7 convolution_bitcast_fusion.2
  381.7 0.6 copy.51
  382.3 40.6 %all_to_all.16 = f32[128,8,256]{2,1,0:T(8,128)S(1)} all-to-all(f32[128,8,256]{2,1,0:T(8,128)S(1)} %copy.51), channel_id=1, replica_groups=mesh['rows'=64,'probes'=8] {'rows'}, dimensions={0} | all-to-all | bytes 2097152 | tf_op jit(solution)/shard_map/all_to_all | solution.py:54
  422.9 0.1 reduce_sum.38
  423.1 0.1 fusion.18
  423.2 0.2 fusion.1
  423.4 0.7 convolution_bitcast_fusion.1
  424.1 1.6 copy.56
  425.7 6.8 %all-to-all-start.2 = ((f32[128,8,256]{2,1,0:T(8,128)}), f32[128,8,256]{2,1,0:T(8,128)S(1)}, u32[]{:S(2)}, u32[]{:S(2)}) async-start(f32[128,8,256]{2,1,0:T(8,128)} %copy.56), calls=%async_computation.2 | async-start | bytes 2097152 | tf_op jit(solution)/shard_map/all_to_all | solution.py:54
  432.5 119.4 %all_gather.15 = bf16[128,8,256]{2,1,0:T(8,128)(2,1)S(1)} all-gather(bf16[2,8,256]{2,1,0:T(8,128)(2,1)S(1)} %copy-done.2), channel_id=1, replica_groups=mesh['rows'=64,'probes'=8] {'rows'}, dimensions={0}, use_global_device_ids=true | all-gather | bytes 532480 | tf_op jit(solution)/shard_map/all_gather | solution.py:28
  551.9 0.2 convolution_convert_fusion
  552.1 0.0 all-to-all-done.2
  552.1 0.1 reduce_sum.39
  552.2 0.1 fusion.19
  552.4 0.0 copy-start.3
  552.4 0.3 convolution_bitcast_fusion.4
  552.7 0.5 convolution_bitcast_fusion
  553.2 0.3 fusion
  553.4 0.0 copy-done.3
  553.5 1.4 copy.62
  (10 shorter events, 0.1 us)
Async XLA Ops:
  0.6 4.7 copy-start
  1.5 112.1 %copy-start.1 = (bf16[2,256,256]{2,1,0:T(8,128)(2,1)S(1)}, bf16[2,256,256]{2,1,0:T(8,128)(2,1)}, u32[]{:S(2)}) copy-start(bf16[2,256,256]{2,1,0:T(8,128)(2,1)} %param.7) | copy-start | bytes 786436
  1.5 112.1 %copy-start.2 = (bf16[2,8,256]{2,1,0:T(8,128)(2,1)S(1)}, bf16[2,8,256]{2,1,0:T(8,128)(2,1)}, u32[]{:S(2)}) copy-start(bf16[2,8,256]{2,1,0:T(8,128)(2,1)} %param.5) | copy-start | bytes 24580
  425.7 126.4 %all-to-all-start.2 = ((f32[128,8,256]{2,1,0:T(8,128)}), f32[128,8,256]{2,1,0:T(8,128)S(1)}, u32[]{:S(2)}, u32[]{:S(2)}) async-start(f32[128,8,256]{2,1,0:T(8,128)} %copy.56), calls=%async_computation.2 | async-start | bytes 2097152 | tf_op jit(solution)/shard_map/all_to_all | solution.py:54
  552.4 1.1 copy-start.3
where the time goes:
time: 556 us; the launch traced here: 555 us
  blocking collectives  530 us (95%)
  matrix products  7.89 us (1%)
  local copies, waits for them, and re-layouts  7.72 us (1%)
  starting transfers between devices  6.83 us (1%)
    all_gather x3, blocking collectives, body(): solved_all = lax.all_gather(own_solved, 'rows', axis=0, tiled=True)  310 us
    all_gather x1, blocking collectives, body(): all_probes = lax.all_gather(probes, 'rows', axis=0, tiled=True)  119 us
    all_to_all x2, blocking collectives, body(): lax.all_to_all(outgoing, 'rows', split_axis=0, concat_axis=0, tiled=True)  101 us
  transfers between devices with their start and end apart: 1, of which 0 were waited for; matrix products, arithmetic and copies ran while one was open for 0% of the time, Pallas kernels for 0%

commit v1 on v0

v1 whole, which is shorter than its diff:
```python
import jax
import jax.numpy as jnp
from jax import lax
from jax.sharding import Mesh, PartitionSpec as P

LEVELS = 4
Y, Z = 4, 16
ROWS = ("y", "z")


def body(probes, factor, inverses, pattern, owner):
    f32, bf16 = jnp.float32, jnp.bfloat16
    my, mz = lax.axis_index("y"), lax.axis_index("z")
    local, count, block = probes.shape
    total = owner.shape[0]
    width = total // LEVELS
    nbr = pattern.shape[1]
    pair = count // Y
    lanes = pair * block
    held = Y * local
    iota = jnp.arange(total, dtype=jnp.int32)

    def weights(d, l):
        return jnp.einsum("sab,skbc->skac", d, l, preferred_element_type=f32).astype(bf16)

    own_w = weights(inverses, factor)
    w = [own_w] + [
        lax.ppermute(own_w, "y", [(i, (i + d) % Y) for i in range(Y)]) for d in range(1, Y)
    ]
    q_own = jnp.einsum("spb,sab->spa", probes, inverses, preferred_element_type=f32).astype(bf16)

    def pick(keys, values):
        hit = keys[..., None] == iota
        return jnp.sum(jnp.where(hit, values, 0), axis=-1)

    def rows_of(slots):
        return jnp.sum(jnp.where(owner[None, :] == slots[:, None], iota[None, :], 0), axis=1)

    def sources(rows):
        hit = rows[:, None, None] == iota[None, :, None]
        cols = jnp.sum(jnp.where(hit, pattern[None], 0), axis=1)
        return jnp.where(cols >= 0, pick(cols, owner), -1)

    back = jnp.arange(Y, dtype=jnp.int32)
    local_iota = jnp.arange(local, dtype=jnp.int32)
    slots = (local * (((my - back) % Y) * Z + mz))[:, None] + local_iota[None, :]
    slots = slots.reshape(-1)
    rows = rows_of(slots)
    level = rows // width
    src = sources(rows).reshape(-1)
    sel = src[:, None] == iota[None, :]
    dev = src // local
    place = (dev % Z) * held + ((my - dev // Z) % Y) * local + src % local
    place = jnp.where(src >= 0, place, -1)
    sel_z = place[:, None] == iota[None, :]
    hold = slots[:, None] == iota[None, :]

    both = jnp.stack([q_own, probes]).reshape(2, local, Y, lanes)
    both = both.transpose(2, 0, 1, 3).reshape(Y, 1, 2 * local, lanes)
    both = jnp.broadcast_to(both, (Y, Z, 2 * local, lanes)).reshape(Y * Z, 2 * local, lanes)
    got = lax.all_to_all(both, ROWS, 0, 0, tiled=True)
    q_all = got[:, :local].reshape(total, lanes)
    p_all = got[:, local:].reshape(total, lanes)

    def choose(mask, table):
        return jnp.dot(mask.astype(bf16), table, preferred_element_type=f32)

    nat = (local * (back * Z + mz))[:, None] + local_iota[None, :]
    src_nat = sources(rows_of(nat.reshape(-1))).reshape(-1)
    near_p = choose(src_nat[:, None] == iota[None, :], p_all).astype(bf16)
    near_p = lax.all_to_all(near_p.reshape(Y, local * nbr, lanes), "y", 0, 0, tiled=True)
    near_p = near_p.reshape(Y, local, nbr, pair, block).transpose(1, 2, 0, 3, 4)
    near_p = near_p.reshape(local, nbr, count, block)

    q = choose(hold, q_all)
    solved = q.astype(bf16)
    known, mask = q_all, sel
    for lev in range(1, LEVELS):
        near = choose(mask, known).astype(bf16).reshape(Y, local, nbr, pair, block)
        moved = jnp.stack(
            [
                jnp.einsum("skcb,skab->sca", near[d], w[d], preferred_element_type=f32)
                for d in range(Y)
            ]
        ).reshape(held, lanes)
        value = (q - moved).astype(bf16)
        solved = jnp.where((level == lev)[:, None], value, solved)
        if lev < LEVELS - 1:
            send = jnp.broadcast_to(solved[None], (Z, held, lanes))
            known = lax.all_to_all(send, "z", 0, 0, tiled=True).reshape(total, lanes)
            mask = sel_z

    t = solved
    out = jnp.zeros((total, lanes), f32)
    for lev in range(LEVELS - 1, 0, -1):
        live = jnp.where((level == lev)[:, None], t, jnp.zeros((), bf16))
        live = live.reshape(Y, local, pair, block)
        terms = jnp.stack(
            [
                jnp.einsum("sca,skab->skcb", live[d], w[d], preferred_element_type=f32)
                for d in range(Y)
            ]
        ).reshape(held * nbr, lanes)
        m = sel_z if lev > 1 else sel
        if lev > 1:
            out = out + jnp.dot(m.T.astype(f32), terms, precision=lax.Precision.HIGHEST)
            got = lax.all_to_all(out.astype(bf16).reshape(Z, held, lanes), "z", 0, 0, tiled=True)
            acc = jnp.sum(got.astype(f32), axis=0)
            t = jnp.where((level == lev - 1)[:, None], (solved.astype(f32) - acc).astype(bf16), t)
        else:
            nat_out = out.reshape(Z, Y, local, lanes)
            nat_out = jnp.take(nat_out, (my - back) % Y, axis=1).transpose(1, 0, 2, 3)
            nat_out = nat_out.reshape(total, lanes)
            nat_out = nat_out + jnp.dot(m.T.astype(f32), terms, precision=lax.Precision.HIGHEST)
            level_all = rows_of(iota) // width
            nat_out = jnp.where((level_all == 0)[:, None], nat_out, 0.0)
            done = jnp.where((level > 0)[:, None], t, jnp.zeros((), bf16))
            nat_out = nat_out + jnp.dot(hold.T.astype(bf16), done, preferred_element_type=f32)
            got = lax.all_to_all(
                nat_out.astype(bf16).reshape(Y * Z, local, lanes), ROWS, 0, 0, tiled=True
            )
            got = jnp.sum(got.astype(f32).reshape(Y, Z, local, lanes), axis=1)
            got = got.reshape(Y, local, pair, block).transpose(1, 0, 2, 3)
            got = got.reshape(local, count, block)
    me = my * Z + mz
    my_level = rows_of(me * local + local_iota) // width
    first = (my_level == 0)[:, None, None]
    t_own = jnp.where(first, q_own.astype(f32) - got, got).astype(bf16)
    x = jnp.einsum("spa,sab->spb", t_own, inverses, preferred_element_type=f32).astype(bf16)
    near_all = jnp.concatenate([near_p, probes[:, None]], axis=1)
    selected = jnp.einsum("spa,skpb->skab", x, near_all, preferred_element_type=f32)
    return x, (selected / count).astype(bf16)


def solution(mesh):
    fine = Mesh(mesh.devices.reshape(Y, Z, -1), ("y", "z", "p"))
    return jax.shard_map(
        body,
        mesh=fine,
        in_specs=(
            P(ROWS, "p", None),
            P(ROWS, None, None, None),
            P(ROWS, None, None),
            P(),
            P(),
        ),
        out_specs=(P(ROWS, "p", None), P(ROWS, "p", None, None)),
        check_vma=False,
    )
```

time: 556 us -> 224 us (0.40)
  blocking collectives: 530 us -> 0 us
  waiting for transfers between devices: 0.01 us -> 74 us
  starting transfers between devices: 6.83 us -> 75.8 us
  matrix products: 7.89 us -> 31.6 us
  local copies, waits for them, and re-layouts: 7.72 us -> 24.9 us
  other arithmetic: 1.56 us -> 14.4 us
    all_gather x4 -> x0, blocking collectives: 429 us -> none  [the longest x3 310 us: body(): solved_all = lax.all_gather(own_solved, 'rows', axis=0, tiled=True)]
    all_to_all x2 -> x0, blocking collectives: 101 us -> none  [body(): lax.all_to_all(outgoing, 'rows', split_axis=0, concat_axis=0, tiled=True)]
    all_to_all x1 -> x7, waiting for transfers between devices: 0.01 us -> 74 us  [the longest x2 25.9 us: body(): known = lax.all_to_all(send, 'z', 0, 0, tiled=True).reshape(total, lanes)]
    all_to_all x1 -> x7, starting transfers between devices: 6.83 us -> 63.6 us  [the longest x2 19.1 us: body(): known = lax.all_to_all(send, 'z', 0, 0, tiled=True).reshape(total, lanes)]
    dot_general x21 -> x37, matrix products: 7.89 us -> 31.6 us  [the longest x12 11.9 us: body(): jnp.einsum('sca,skab->skcb', live[d], w[d], preferred_element_type=f32)]
    ppermute x0 -> x3, starting transfers between devices: none -> 12.2 us  [body(): lax.ppermute(own_w, 'y', [(i, (i + d) % Y) for i in range(Y)])]
    reshape x0 -> x11, local copies, waits for them, and re-layouts: none -> 6.39 us  [the longest x1 1.83 us: body(): nat_out = nat_out.reshape(total, lanes)]
    select_n x2 -> x10, other arithmetic: 0.01 us -> 5.89 us  [the longest x2 2.43 us: body(): nat_out = jnp.take(nat_out, (my - back) % Y, axis=1).transpose(1, 0, 2, 3)]
  transfers between devices with their start and end apart: 1 -> 10, of which waited for: 0 -> 6; matrix products, arithmetic and copies ran while one was open for 0% -> 18% of each run, Pallas kernels for 0% -> 0%
where the time goes in v1:
time: 224 us; the launch traced here: 222 us
  starting transfers between devices  75.8 us (34%)
  waiting for transfers between devices  74 us (33%)
  matrix products  31.6 us (14%)
  local copies, waits for them, and re-layouts  24.9 us (11%)
  other arithmetic  14.4 us (6%)
    all_to_all x2, waiting for transfers between devices, body(): known = lax.all_to_all(send, 'z', 0, 0, tiled=True).reshape(total, lanes)  25.9 us
    all_to_all x1, waiting for transfers between devices, body(): got = lax.all_to_all(both, ROWS, 0, 0, tiled=True)  20.7 us
    all_to_all x2, starting transfers between devices, body(): known = lax.all_to_all(send, 'z', 0, 0, tiled=True).reshape(total, lanes)  19.1 us
    all_to_all x1, starting transfers between devices, body(): got = lax.all_to_all(both, ROWS, 0, 0, tiled=True)  16.4 us
    all_to_all x1, waiting for transfers between devices, body(): lax.all_to_all(nat_out.astype(bf16).reshape(Y * Z, local, lanes), ROWS, 0...  14.8 us
    all_to_all x1, starting transfers between devices, body(): lax.all_to_all(nat_out.astype(bf16).reshape(Y * Z, local, lanes), ROWS, 0...  14.7 us
    all_to_all x2, waiting for transfers between devices, body(): lax.all_to_all(out.astype(bf16).reshape(Z, held, lanes), 'z', 0, 0, tiled...  12.6 us
    ppermute x3, starting transfers between devices, body(): lax.ppermute(own_w, 'y', [(i, (i + d) % Y) for i in range(Y)])  12.2 us
  transfers between devices with their start and end apart: 10, of which 6 were waited for; matrix products, arithmetic and copies ran while one was open for 18% of the time, Pallas kernels for 0%

profile of v1, /device:TPU:6, one launch (start us, length us, event | category | flops | bytes accessed | tf_op | source)
XLA Modules:
  0.0 221.9 jit_solution(13909544422267869793)
XLA Ops:
  0.7 1.2 copy-done
  1.9 1.5 fusion.1
  3.4 5.1 %collective-permute-start.1 = (bf16[2,4,256,256]{2,3,1,0:T(8,128)(2,1)S(1)}, bf16[2,4,256,256]{2,3,1,0:T(8,128)(2,1)S(1)}, u32[]{:S(2)}, u32[]{:S(2)}) collective-permute-start(bf16[2,4,256,256]{2,3,1,0:T(8,128)(2,1)S(1)} %fusion.1), channel_id=1, source_target_pairs={{0,256},{128,384},{256,0},{384,128},{1,257},{129,385},{257,1},{385... | collective-permute-start | bytes 3145736 | tf_op jit(solution)/shard_map/ppermute | solution.py:28
  8.5 2.6 %collective-permute-start = (bf16[2,4,256,256]{2,3,1,0:T(8,128)(2,1)S(1)}, bf16[2,4,256,256]{2,3,1,0:T(8,128)(2,1)}, u32[]{:S(2)}, u32[]{:S(2)}) collective-permute-start(bf16[2,4,256,256]{2,3,1,0:T(8,128)(2,1)S(1)} %fusion.1), channel_id=1, source_target_pairs={{0,128},{128,256},{256,384},{384,0},{1,129},{129,257},{257,385},{3... | collective-permute-start | bytes 3145736 | tf_op jit(solution)/shard_map/ppermute | solution.py:28
  11.1 4.5 %collective-permute-start.2 = (bf16[2,4,256,256]{2,3,1,0:T(8,128)(2,1)S(1)}, bf16[2,4,256,256]{2,3,1,0:T(8,128)(2,1)}, u32[]{:S(2)}, u32[]{:S(2)}) collective-permute-start(bf16[2,4,256,256]{2,3,1,0:T(8,128)(2,1)S(1)} %fusion.1), channel_id=1, source_target_pairs={{0,384},{128,0},{256,128},{384,256},{1,385},{129,1},{257,129},{385... | collective-permute-start | bytes 3145736 | tf_op jit(solution)/shard_map/ppermute | solution.py:28
  15.8 0.8 broadcast_in_dim.251
  16.6 16.4 %all-to-all-start = ((bf16[64,4,512]{2,1,0:T(4,128)(2,1)}), bf16[64,4,512]{2,1,0:T(4,128)(2,1)}, u32[]{:S(2)}, u32[]{:S(2)}) async-start(bf16[64,4,512]{2,1,0:T(4,128)(2,1)} %bitcast.238), calls=%async_computation | async-start | bytes 524288 | tf_op jit(solution)/shard_map/all_to_all | solution.py:61
  34.5 0.8 select_reduce_fusion.1
  36.1 0.6 broadcast_compare_fusion
  36.7 20.7 %all-to-all-done = bf16[64,4,512]{2,1,0:T(4,128)(2,1)} async-done(((bf16[64,4,512]{2,1,0:T(4,128)(2,1)}), bf16[64,4,512]{2,1,0:T(4,128)(2,1)}, u32[]{:S(2)}, u32[]{:S(2)}) %all-to-all-start) | async-done | bytes 262176 | tf_op jit(solution)/shard_map/all_to_all | solution.py:61
  57.4 2.0 fusion.63
  59.4 1.0 reshape.458
  60.5 0.6 fusion.66
  61.1 1.3 squeeze.74
  62.4 1.3 squeeze.73
  63.7 0.6 squeeze.75
  65.0 0.9 fusion.33
  65.8 0.9 convolution_bitcast_fusion.23
  66.8 1.0 convolution_bitcast_fusion.21
  67.8 1.5 convolution_bitcast_fusion.22
  69.2 1.5 convolution_bitcast_fusion.20
  71.4 0.7 broadcast_in_dim.254
  72.1 15.2 %all-to-all-start.1 = ((bf16[16,8,512]{2,1,0:T(8,128)(2,1)}), bf16[16,8,512]{2,1,0:T(8,128)(2,1)S(1)}, u32[]{:S(2)}, u32[]{:S(2)}) async-start(bf16[16,8,512]{2,1,0:T(8,128)(2,1)} %broadcast_in_dim.254), calls=%async_computation.1 | async-start | bytes 262144 | tf_op jit(solution)/shard_map/all_to_all | solution.py:90
  87.3 1.1 compare_select_fusion.9
  88.5 13.2 %all-to-all-done.1 = bf16[16,8,512]{2,1,0:T(8,128)(2,1)S(1)} async-done(((bf16[16,8,512]{2,1,0:T(8,128)(2,1)}), bf16[16,8,512]{2,1,0:T(8,128)(2,1)S(1)}, u32[]{:S(2)}, u32[]{:S(2)}) %all-to-all-start.1) | async-done | bytes 131104 | tf_op jit(solution)/shard_map/all_to_all | solution.py:90
  101.7 0.8 convolution_convert_fusion.3
  102.8 1.5 convolution_bitcast_fusion.18
  104.5 1.5 convolution_bitcast_fusion.16
  106.7 0.7 broadcast_in_dim.255
  107.4 3.9 %all-to-all-start.2 = ((bf16[16,8,512]{2,1,0:T(8,128)(2,1)}), bf16[16,8,512]{2,1,0:T(8,128)(2,1)S(1)}, u32[]{:S(2)}, u32[]{:S(2)}) async-start(bf16[16,8,512]{2,1,0:T(8,128)(2,1)} %broadcast_in_dim.255), calls=%async_computation.2 | async-start | bytes 262144 | tf_op jit(solution)/shard_map/all_to_all | solution.py:90
  111.3 1.3 select_reduce_fusion
  112.7 12.7 %all-to-all-done.2 = bf16[16,8,512]{2,1,0:T(8,128)(2,1)S(1)} async-done(((bf16[16,8,512]{2,1,0:T(8,128)(2,1)}), bf16[16,8,512]{2,1,0:T(8,128)(2,1)S(1)}, u32[]{:S(2)}, u32[]{:S(2)}) %all-to-all-start.2) | async-done | bytes 131104 | tf_op jit(solution)/shard_map/all_to_all | solution.py:90
  125.3 0.8 convolution_convert_fusion.2
  126.4 1.5 convolution_bitcast_fusion.14
  128.1 1.5 convolution_bitcast_fusion.12
  129.7 0.7 broadcast_select_fusion.3
  130.8 1.6 convolution_bitcast_fusion.10
  132.8 1.6 convolution_bitcast_fusion.8
  134.9 0.7 copy-done.2
  135.6 0.7 convert_bitcast_fusion.1
  136.2 3.6 %all-to-all-start.3 = ((bf16[16,8,512]{2,1,0:T(8,128)(2,1)}), bf16[16,8,512]{2,1,0:T(8,128)(2,1)S(1)}, u32[]{:S(2)}, u32[]{:S(2)}) async-start(bf16[16,8,512]{2,1,0:T(8,128)(2,1)} %convert_bitcast_fusion.1), calls=%async_computation.3 | async-start | bytes 262144 | tf_op jit(solution)/shard_map/all_to_all | solution.py:107
  141.5 11.7 %all-to-all-done.3 = bf16[16,8,512]{2,1,0:T(8,128)(2,1)S(1)} async-done(((bf16[16,8,512]{2,1,0:T(8,128)(2,1)}), bf16[16,8,512]{2,1,0:T(8,128)(2,1)S(1)}, u32[]{:S(2)}, u32[]{:S(2)}) %all-to-all-start.3) | async-done | bytes 131104 | tf_op jit(solution)/shard_map/all_to_all | solution.py:107
  153.3 0.8 broadcast_select_fusion.2
  154.6 1.6 convolution_bitcast_fusion.6
  156.6 1.6 convolution_bitcast_fusion.4
  158.7 0.7 copy-done.4
  159.4 0.7 convert_bitcast_fusion
  160.0 4.2 %all-to-all-start.4 = ((bf16[16,8,512]{2,1,0:T(8,128)(2,1)}), bf16[16,8,512]{2,1,0:T(8,128)(2,1)}, u32[]{:S(2)}, u32[]{:S(2)}) async-start(bf16[16,8,512]{2,1,0:T(8,128)(2,1)} %convert_bitcast_fusion), calls=%async_computation.4 | async-start | bytes 262144 | tf_op jit(solution)/shard_map/all_to_all | solution.py:107
  164.8 0.7 select_n.261
  166.1 1.0 reshape.476
  167.0 1.5 fusion.4
  168.5 1.8 reshape.467
  170.3 2.6 %gather_fusion = f32[4,16,2,512]{3,2,1,0:T(2,128)} fusion(f32[16,4,2,512]{3,2,1,0:T(2,128)} %reshape.467, s32[1024]{0:T(1024)} %pad_clamp_fusion), kind=kCustom, calls=%fused_computation | custom fusion | bytes 524304 | tf_op jit(solution)/shard_map/jit(_take)/gather | solution.py:112
  172.9 1.8 broadcast_select_fusion
  174.7 1.8 reshape.468
  176.6 0.8 all-to-all-done.4
  177.4 5.7 %all-to-all-start.6 = ((bf16[4,8,512]{2,1,0:T(8,128)(2,1)}), bf16[4,8,512]{2,1,0:T(8,128)(2,1)S(1)}, u32[]{:S(2)}, u32[]{:S(2)}) async-start(bf16[4,8,512]{2,1,0:T(8,128)(2,1)} %fusion.4), calls=%async_computation.6 | async-start | bytes 65536 | tf_op jit(solution)/shard_map/all_to_all | solution.py:71
  183.1 0.9 convert_reduce_fusion.1
  184.5 1.6 convolution_bitcast_fusion.2
  186.6 1.6 convolution_bitcast_fusion
  189.0 0.7 reshape.471
  189.7 14.7 %all-to-all-start.5 = ((bf16[64,2,512]{2,1,0:T(2,128)(2,1)}), bf16[64,2,512]{2,1,0:T(2,128)(2,1)S(1)}, u32[]{:S(2)}, u32[]{:S(2)}) async-start(bf16[64,2,512]{2,1,0:T(2,128)(2,1)} %reshape.471), calls=%async_computation.5 | async-start | bytes 262144 | tf_op jit(solution)/shard_map/all_to_all | solution.py:119
  204.8 14.8 %all-to-all-done.5 = bf16[64,2,512]{2,1,0:T(2,128)(2,1)S(1)} async-done(((bf16[64,2,512]{2,1,0:T(2,128)(2,1)}), bf16[64,2,512]{2,1,0:T(2,128)(2,1)S(1)}, u32[]{:S(2)}, u32[]{:S(2)}) %all-to-all-start.5) | async-done | bytes 131104 | tf_op jit(solution)/shard_map/all_to_all | solution.py:119
  220.5 1.4 copy.125
  (174 shorter events, 14.1 us)
Async XLA Ops:
  0.6 1.2 copy-start
  0.6 14.9 %copy-start.1 = (bf16[2,256,256]{2,1,0:T(8,128)(2,1)S(1)}, bf16[2,256,256]{2,1,0:T(8,128)(2,1)}, u32[]{:S(2)}) copy-start(bf16[2,256,256]{2,1,0:T(8,128)(2,1)} %param.7) | copy-start | bytes 786436
  0.7 14.9 %copy-start.6 = (bf16[2,8,256]{2,1,0:T(8,128)(2,1)S(1)}, bf16[2,8,256]{2,1,0:T(8,128)(2,1)}, u32[]{:S(2)}) copy-start(bf16[2,8,256]{2,1,0:T(8,128)(2,1)} %param.5) | copy-start | bytes 24580
  0.7 32.7 %copy-start.33 = (s32[128]{0:T(128)S(1)}, s32[128]{0:T(128)}, u32[]{:S(2)}) copy-start(s32[128]{0:T(128)} %param.9) | copy-start | bytes 1540
  1.9 31.8 %copy-start.35 = (s32[128,4]{0,1:T(4,128)S(1)}, s32[128,4]{0,1:T(4,128)}, u32[]{:S(2)}) copy-start(s32[128,4]{0,1:T(4,128)} %param.8) | copy-start | bytes 6148
  3.4 63.4 %collective-permute-start.1 = (bf16[2,4,256,256]{2,3,1,0:T(8,128)(2,1)S(1)}, bf16[2,4,256,256]{2,3,1,0:T(8,128)(2,1)S(1)}, u32[]{:S(2)}, u32[]{:S(2)}) collective-permute-start(bf16[2,4,256,256]{2,3,1,0:T(8,128)(2,1)S(1)} %fusion.1), channel_id=1, source_target_pairs={{0,256},{128,384},{256,0},{384,128},{1,257},{129,385},{257,1},{385... | collective-permute-start | bytes 3145736 | tf_op jit(solution)/shard_map/ppermute | solution.py:28
  8.5 59.3 %collective-permute-start = (bf16[2,4,256,256]{2,3,1,0:T(8,128)(2,1)S(1)}, bf16[2,4,256,256]{2,3,1,0:T(8,128)(2,1)}, u32[]{:S(2)}, u32[]{:S(2)}) collective-permute-start(bf16[2,4,256,256]{2,3,1,0:T(8,128)(2,1)S(1)} %fusion.1), channel_id=1, source_target_pairs={{0,128},{128,256},{256,384},{384,0},{1,129},{129,257},{257,385},{3... | collective-permute-start | bytes 3145736 | tf_op jit(solution)/shard_map/ppermute | solution.py:28
  11.1 58.1 %collective-permute-start.2 = (bf16[2,4,256,256]{2,3,1,0:T(8,128)(2,1)S(1)}, bf16[2,4,256,256]{2,3,1,0:T(8,128)(2,1)}, u32[]{:S(2)}, u32[]{:S(2)}) collective-permute-start(bf16[2,4,256,256]{2,3,1,0:T(8,128)(2,1)S(1)} %fusion.1), channel_id=1, source_target_pairs={{0,384},{128,0},{256,128},{384,256},{1,385},{129,1},{257,129},{385... | collective-permute-start | bytes 3145736 | tf_op jit(solution)/shard_map/ppermute | solution.py:28
  15.7 43.6 %copy-start.10 = (bf16[2,8,256]{2,1,0:T(8,128)(2,1)}, bf16[2,8,256]{2,1,0:T(8,128)(2,1)S(1)}, u32[]{:S(2)}) copy-start(bf16[2,8,256]{2,1,0:T(8,128)(2,1)S(1)} %convolution_convert_fusion.6) | copy-start | bytes 24580
  16.6 40.8 %all-to-all-start = ((bf16[64,4,512]{2,1,0:T(4,128)(2,1)}), bf16[64,4,512]{2,1,0:T(4,128)(2,1)}, u32[]{:S(2)}, u32[]{:S(2)}) async-start(bf16[64,4,512]{2,1,0:T(4,128)(2,1)} %bitcast.238), calls=%async_computation | async-start | bytes 524288 | tf_op jit(solution)/shard_map/all_to_all | solution.py:61
  33.2 2.1 copy-start.28
  33.9 0.6 copy-start.18
  35.5 24.9 %copy-start.26 = (s32[32]{0:T(128)}, s32[32]{0:T(128)S(1)}, u32[]{:S(2)}) copy-start(s32[32]{0:T(128)S(1)} %select_n.234) | copy-start | bytes 388
  65.0 2.8 %copy-start.17 = (bf16[2,4,2,256]{3,2,1,0:T(2,128)(2,1)S(1)}, bf16[2,4,2,256]{3,2,1,0:T(2,128)(2,1)}, u32[]{:S(2)}) copy-start(bf16[2,4,2,256]{3,2,1,0:T(2,128)(2,1)} %squeeze.73) | copy-start | bytes 24580
  66.8 2.5 %copy-start.16 = (bf16[2,4,2,256]{3,2,1,0:T(2,128)(2,1)S(1)}, bf16[2,4,2,256]{3,2,1,0:T(2,128)(2,1)}, u32[]{:S(2)}) copy-start(bf16[2,4,2,256]{3,2,1,0:T(2,128)(2,1)} %squeeze.75) | copy-start | bytes 24580
  67.7 3.0 %copy-start.30 = (pred[8]{0:T(512)(128)(4,1)S(1)}, pred[8]{0:T(512)(128)(4,1)}, u32[]{:S(2)}) copy-start(pred[8]{0:T(512)(128)(4,1)} %get-tuple-element.49) | copy-start | bytes 28
  70.8 0.6 copy-start.13
  72.1 29.6 %all-to-all-start.1 = ((bf16[16,8,512]{2,1,0:T(8,128)(2,1)}), bf16[16,8,512]{2,1,0:T(8,128)(2,1)S(1)}, u32[]{:S(2)}, u32[]{:S(2)}) async-start(bf16[16,8,512]{2,1,0:T(8,128)(2,1)} %broadcast_in_dim.254), calls=%async_computation.1 | async-start | bytes 262144 | tf_op jit(solution)/shard_map/all_to_all | solution.py:90
  104.3 1.8 copy-start.14
  104.3 1.8 copy-start.20
  106.1 0.6 copy-start.8
  107.4 17.9 %all-to-all-start.2 = ((bf16[16,8,512]{2,1,0:T(8,128)(2,1)}), bf16[16,8,512]{2,1,0:T(8,128)(2,1)S(1)}, u32[]{:S(2)}, u32[]{:S(2)}) async-start(bf16[16,8,512]{2,1,0:T(8,128)(2,1)} %broadcast_in_dim.255), calls=%async_computation.2 | async-start | bytes 262144 | tf_op jit(solution)/shard_map/all_to_all | solution.py:90
  127.9 1.8 copy-start.9
  127.9 1.8 copy-start.32
  132.4 2.1 copy-start.24
  132.8 7.6 %copy-start.39 = (s32[128]{0:T(128)S(1)}, s32[128]{0:T(128)}, u32[]{:S(2)}) copy-start(s32[128]{0:T(128)} %select_reduce_fusion) | copy-start | bytes 1540
  132.8 8.2 %copy-start.19 = (s32[8,4]{0,1:T(4,128)S(1)}, s32[8,4]{0,1:T(4,128)}, u32[]{:S(2)}) copy-start(s32[8,4]{0,1:T(4,128)} %copy-done.18) | copy-start | bytes 388
  132.8 8.2 %copy-start.22 = (s32[8,4]{0,1:T(4,128)S(1)}, s32[8,4]{0,1:T(4,128)}, u32[]{:S(2)}) copy-start(s32[8,4]{0,1:T(4,128)} %get-tuple-element.12) | copy-start | bytes 388
  134.9 0.7 copy-start.2
  136.2 17.0 %all-to-all-start.3 = ((bf16[16,8,512]{2,1,0:T(8,128)(2,1)}), bf16[16,8,512]{2,1,0:T(8,128)(2,1)S(1)}, u32[]{:S(2)}, u32[]{:S(2)}) async-start(bf16[16,8,512]{2,1,0:T(8,128)(2,1)} %convert_bitcast_fusion.1), calls=%async_computation.3 | async-start | bytes 262144 | tf_op jit(solution)/shard_map/all_to_all | solution.py:107
  156.2 2.1 copy-start.3
  156.2 2.1 copy-start.25
  156.6 8.2 %copy-start.23 = (s32[8,4]{0,1:T(4,128)S(1)}, s32[8,4]{0,1:T(4,128)}, u32[]{:S(2)}) copy-start(s32[8,4]{0,1:T(4,128)} %compare_select_fusion.8) | copy-start | bytes 388
  156.6 8.9 %copy-start.38 = (s32[4]{0:T(128)S(1)}, s32[4]{0:T(128)}, u32[]{:S(2)}) copy-start(s32[4]{0:T(128)} %fusion.56) | copy-start | bytes 52
  158.7 0.7 copy-start.4
  160.0 17.4 %all-to-all-start.4 = ((bf16[16,8,512]{2,1,0:T(8,128)(2,1)}), bf16[16,8,512]{2,1,0:T(8,128)(2,1)}, u32[]{:S(2)}, u32[]{:S(2)}) async-start(bf16[16,8,512]{2,1,0:T(8,128)(2,1)} %convert_bitcast_fusion), calls=%async_computation.4 | async-start | bytes 262144 | tf_op jit(solution)/shard_map/all_to_all | solution.py:107
  168.5 15.5 %copy-start.12 = (bf16[8,512]{1,0:T(8,128)(2,1)S(1)}, bf16[8,512]{1,0:T(8,128)(2,1)}, u32[]{:S(2)}) copy-start(bf16[8,512]{1,0:T(8,128)(2,1)} %get-tuple-element.21) | copy-start | bytes 24580
  168.5 15.5 %copy-start.21 = (pred[8]{0:T(512)(128)(4,1)S(1)}, pred[8]{0:T(512)(128)(4,1)}, u32[]{:S(2)}) copy-start(pred[8]{0:T(512)(128)(4,1)} %get-tuple-element.48) | copy-start | bytes 28
  168.5 15.5 %copy-start.31 = (pred[8]{0:T(512)(128)(4,1)S(1)}, pred[8]{0:T(512)(128)(4,1)}, u32[]{:S(2)}) copy-start(pred[8]{0:T(512)(128)(4,1)} %get-tuple-element.49) | copy-start | bytes 28
  177.4 12.3 %all-to-all-start.6 = ((bf16[4,8,512]{2,1,0:T(8,128)(2,1)}), bf16[4,8,512]{2,1,0:T(8,128)(2,1)S(1)}, u32[]{:S(2)}, u32[]{:S(2)}) async-start(bf16[4,8,512]{2,1,0:T(8,128)(2,1)} %fusion.4), calls=%async_computation.6 | async-start | bytes 65536 | tf_op jit(solution)/shard_map/all_to_all | solution.py:71
  186.1 2.1 copy-start.5
  186.1 2.1 copy-start.27
  186.1 2.1 copy-start.37
  186.1 2.5 %copy-start.29 = (s32[8]{0:T(128)S(1)}, s32[8]{0:T(128)}, u32[]{:S(2)}) copy-start(s32[8]{0:T(128)} %copy-done.28) | copy-start | bytes 100
  186.2 2.5 %copy-start.36 = (pred[8]{0:T(512)(128)(4,1)S(1)}, pred[8]{0:T(512)(128)(4,1)}, u32[]{:S(2)}) copy-start(pred[8]{0:T(512)(128)(4,1)} %get-tuple-element.16) | copy-start | bytes 28
  186.6 17.9 %copy-start.34 = (s32[128]{0:T(128)S(1)}, s32[128]{0:T(128)}, u32[]{:S(2)}) copy-start(s32[128]{0:T(128)} %param.9) | copy-start | bytes 1540
  188.2 31.6 %copy-start.11 = (bf16[2,8,256]{2,1,0:T(8,128)(2,1)S(1)}, bf16[2,8,256]{2,1,0:T(8,128)(2,1)}, u32[]{:S(2)}) copy-start(bf16[2,8,256]{2,1,0:T(8,128)(2,1)} %copy-done.10) | copy-start | bytes 24580
  188.2 31.7 %copy-start.7 = (bf16[2,8,256]{2,1,0:T(8,128)(2,1)S(1)}, bf16[2,8,256]{2,1,0:T(8,128)(2,1)}, u32[]{:S(2)}) copy-start(bf16[2,8,256]{2,1,0:T(8,128)(2,1)} %param.5) | copy-start | bytes 24580
  189.7 29.8 %all-to-all-start.5 = ((bf16[64,2,512]{2,1,0:T(2,128)(2,1)}), bf16[64,2,512]{2,1,0:T(2,128)(2,1)S(1)}, u32[]{:S(2)}, u32[]{:S(2)}) async-start(bf16[64,2,512]{2,1,0:T(2,128)(2,1)} %reshape.471), calls=%async_computation.5 | async-start | bytes 262144 | tf_op jit(solution)/shard_map/all_to_all | solution.py:119
  219.9 2.0 copy-start.15

commit v2 on v0

v2 whole, which is shorter than its diff:
```python
import functools

import jax
import jax.numpy as jnp
from jax import lax
from jax.experimental import pallas as pl
from jax.experimental.pallas import tpu as pltpu
from jax.sharding import Mesh, PartitionSpec as P

LEVELS = 4
Y, Z = 4, 16
LOCAL, COUNT, BLOCK, NBR = 2, 8, 256, 4
PAIR = COUNT // Y
HELD = Y * LOCAL
PAD = 8
WIDE = HELD * NBR * PAD
ROWS = ("y", "z")
F32, BF16 = jnp.float32, jnp.bfloat16
NT = (((1,), (1,)), ((), ()))
TN = (((0,), (0,)), ((), ()))
VMEM = pl.BlockSpec(memory_space=pltpu.VMEM)
SMEM = pl.BlockSpec(memory_space=pltpu.SMEM)


def call(kernel, out_shape, places, scratch=(), flops=0, moved=0):
    kinds = {"s": SMEM, "v": VMEM, "h": pl.BlockSpec(memory_space=pl.ANY)}
    return pl.pallas_call(
        kernel,
        out_shape=out_shape,
        in_specs=[kinds[p] for p in places],
        out_specs=jax.tree.map(lambda _: VMEM, out_shape),
        scratch_shapes=list(scratch),
        compiler_params=pltpu.CompilerParams(vmem_limit_bytes=52 * 2**20),
        cost_estimate=pl.CostEstimate(flops=flops, bytes_accessed=moved, transcendentals=0),
    )


def shape(*dims, dtype=BF16):
    return jax.ShapeDtypeStruct(dims, dtype)


def dot(a, b, dims=None):
    if dims is None:
        return jnp.dot(a, b, preferred_element_type=F32)
    return lax.dot_general(a, b, dims, preferred_element_type=F32)


def start_kernel(core_ref, probes_ref, inv_ref, factor_ref, q_ref, msg_ref, w_ref, d_ref, l_ref, sems):
    load_d = pltpu.make_async_copy(inv_ref, d_ref, sems.at[0])
    load_l = pltpu.make_async_copy(factor_ref.at[core_ref[0]], l_ref, sems.at[1])
    load_d.start()
    load_l.start()
    load_d.wait()
    parts = []
    for s in range(LOCAL):
        q = dot(probes_ref[s], d_ref[s], NT).astype(BF16)
        q_ref[s] = q
        parts.append(q.astype(F32))
    for s in range(LOCAL):
        parts.append(probes_ref[s].astype(F32))
    for y in range(Y):
        msg = jnp.concatenate([p[y * PAIR : (y + 1) * PAIR] for p in parts], axis=0).astype(BF16)
        for z in range(Z):
            msg_ref[y * Z + z] = msg
    load_l.wait()
    core = core_ref[0]
    d = d_ref[core]
    for k in range(NBR):
        w_ref[k] = dot(d, l_ref[k]).astype(BF16)


def load_rows(level_ref, lev, w_ref, held_ref, sems):
    waits = []
    for r in range(HELD):
        copy = pltpu.make_async_copy(w_ref.at[r], held_ref.at[r], sems.at[r])

        @pl.when(level_ref[r] == lev)
        def _():
            copy.start()

        waits.append(copy.wait)
    return waits


def forward_rows(level_ref, lev, waits, near_ref, q_ref, w_ref, solved_ref):
    for r in range(HELD):

        @pl.when(level_ref[r] == lev)
        def _():
            waits[r]()
            moved = jnp.zeros((PAD, BLOCK), F32)
            for k in range(NBR):
                at = (r * NBR + k) * PAD
                moved += dot(near_ref[at : at + PAD].astype(BF16), w_ref[r, k], NT)
            value = (q_ref[r * PAD : (r + 1) * PAD] - moved).astype(BF16).astype(F32)
            solved_ref[r * PAIR : (r + 1) * PAIR] = value[:PAIR]


def backward_rows(level_ref, lev, waits, t_ref, pad_ref, w_ref, terms_ref):
    terms_ref[...] = jnp.zeros_like(terms_ref)
    for r in range(HELD):

        @pl.when(level_ref[r] == lev)
        def _():
            if waits is not None:
                waits[r]()
            pad_ref[...] = jnp.zeros_like(pad_ref)
            pad_ref[:PAIR] = t_ref[r * PAIR : (r + 1) * PAIR]
            t = pad_ref[...].astype(BF16)
            for k in range(NBR):
                at = (r * NBR + k) * PAD
                terms_ref[at : at + PAD] = dot(t, w_ref[r, k])


def scatter(place, terms):
    high = terms.astype(BF16)
    low = (terms - high.astype(F32)).astype(BF16)
    return dot(place, high) + dot(place, low)


def broadcast_to_z(value, msg_ref):
    for z in range(Z):
        msg_ref[z] = value


def level1_kernel(level_ref, got_ref, pick_ref, w_ref, msg_ref, solved_ref, q_ref, near_p_ref, near_ref, held_ref, sems):
    waits = load_rows(level_ref, 1, w_ref, held_ref, sems)
    got = got_ref[...].reshape(Y * Z * 4 * PAIR, BLOCK)
    near_ref[...] = dot(pick_ref[:WIDE], got)
    q_ref[...] = dot(pick_ref[WIDE : WIDE + HELD * PAD], got)
    near_p = dot(pick_ref[WIDE + HELD * PAD :], got).astype(BF16)
    near_p_ref[...] = near_p.reshape(near_p_ref.shape)
    for r in range(HELD):
        solved_ref[r * PAIR : (r + 1) * PAIR] = q_ref[r * PAD : r * PAD + PAIR]
    forward_rows(level_ref, 1, waits, near_ref, q_ref, held_ref, solved_ref)
    broadcast_to_z(solved_ref[...].astype(BF16), msg_ref)


def level2_kernel(level_ref, got_ref, pick_ref, w_ref, q_ref, old_ref, msg_ref, solved_ref, near_ref, held_ref, sems):
    waits = load_rows(level_ref, 2, w_ref, held_ref, sems)
    near_ref[...] = dot(pick_ref[...], got_ref[...].reshape(Z * HELD * PAIR, BLOCK))
    solved_ref[...] = old_ref[...]
    forward_rows(level_ref, 2, waits, near_ref, q_ref, held_ref, solved_ref)
    broadcast_to_z(solved_ref[...].astype(BF16), msg_ref)


def level3_kernel(
    level_ref, got_ref, pick_ref, w_ref, q_ref, old_ref, put_ref,
    msg_ref, solved_ref, terms_ref, near_ref, pad_ref, held_ref, sems):
    waits = load_rows(level_ref, 3, w_ref, held_ref, sems)
    near_ref[...] = dot(pick_ref[...], got_ref[...].reshape(Z * HELD * PAIR, BLOCK))
    solved_ref[...] = old_ref[...]
    forward_rows(level_ref, 3, waits, near_ref, q_ref, held_ref, solved_ref)
    backward_rows(level_ref, 3, None, solved_ref, pad_ref, held_ref, terms_ref)
    out = scatter(put_ref[...], terms_ref[...])
    msg_ref[...] = out.astype(BF16).reshape(msg_ref.shape)


def finish_rows(level_ref, lev, got_ref, old_ref, t_ref):
    acc = jnp.sum(got_ref[...].astype(F32), axis=0)
    t_ref[...] = old_ref[...]
    for r in range(HELD):

        @pl.when(level_ref[r] == lev)
        def _():
            rows = slice(r * PAIR, (r + 1) * PAIR)
            t_ref[rows] = (old_ref[rows] - acc[rows]).astype(BF16).astype(F32)


def back2_kernel(
    level_ref, got_ref, w_ref, old_ref, before_ref, put_ref,
    msg_ref, t_ref, sums_ref, terms_ref, pad_ref, held_ref, sems):
    waits = load_rows(level_ref, 2, w_ref, held_ref, sems)
    finish_rows(level_ref, 2, got_ref, old_ref, t_ref)
    backward_rows(level_ref, 2, waits, t_ref, pad_ref, held_ref, terms_ref)
    sums_ref[...] = before_ref[...] + terms_ref[...]
    out = scatter(put_ref[...], sums_ref[...])
    msg_ref[...] = out.astype(BF16).reshape(msg_ref.shape)


def back1_kernel(
    level_ref, got_ref, w_ref, old_ref, before_ref, put_ref, own_ref, msg_ref, t_ref, terms_ref, pad_ref, held_ref, sems):
    waits = load_rows(level_ref, 1, w_ref, held_ref, sems)
    finish_rows(level_ref, 1, got_ref, old_ref, t_ref)
    backward_rows(level_ref, 1, waits, t_ref, pad_ref, held_ref, terms_ref)
    sums = before_ref[...] + terms_ref[...]
    t = t_ref[...].astype(BF16)
    half = BLOCK // 2
    left = scatter(put_ref[0], sums[:, :half]) + dot(own_ref[0], t[:, :half])
    right = scatter(put_ref[1], sums[:, half:]) + dot(own_ref[1], t[:, half:])
    msg_ref[...] = (left + right).astype(BF16).reshape(msg_ref.shape)


def final_kernel(first_ref, got_ref, q_ref, probes_ref, inv_ref, near_ref, x_ref, sel_ref):
    group = LOCAL * PAIR
    sums = []
    for y in range(Y):
        v = jnp.sum(got_ref[y * Z : (y + 1) * Z].astype(F32), axis=0)
        sums.append(jnp.concatenate([v[:group], v[group:]], axis=1))
    for s in range(LOCAL):
        acc = jnp.concatenate([v[s * PAIR : (s + 1) * PAIR] for v in sums], axis=0)
        base = jnp.where(first_ref[s] == 1, q_ref[s].astype(F32) - acc, acc)
        x = dot(base.astype(BF16), inv_ref[s]).astype(BF16)
        x_ref[s] = x
        for k in range(NBR):
            at = (s * NBR + k) * PAIR
            near = jnp.concatenate(
                [near_ref[y, at : at + PAIR].astype(F32) for y in range(Y)], axis=0
            ).astype(BF16)
            sel_ref[s, k] = (dot(x, near, TN) * (1.0 / COUNT)).astype(BF16)
        sel_ref[s, NBR] = (dot(x, probes_ref[s], TN) * (1.0 / COUNT)).astype(BF16)


def body(probes, factor, inverses, pattern, owner):
    my, mz = lax.axis_index("y"), lax.axis_index("z")
    total = owner.shape[0]
    width = total // LEVELS
    iota = jnp.arange(total, dtype=jnp.int32)

    core = lax.axis_index("c").reshape(1)
    w_shape = shape(NBR, BLOCK, BLOCK)
    out = (shape(LOCAL, COUNT, BLOCK), shape(Y * Z, 4 * PAIR, BLOCK), w_shape)
    scratch = [
        pltpu.VMEM((LOCAL, BLOCK, BLOCK), BF16),
        pltpu.VMEM((NBR, BLOCK, BLOCK), BF16),
        pltpu.SemaphoreType.DMA((2,)),
    ]
    q_own, msg, w_send = call(start_kernel, out, "svhh", scratch)(
        core, probes, inverses, factor
    )
    got = lax.all_to_all(msg, ROWS, 0, 0, tiled=True)
    w = lax.all_gather(w_send, ("y", "c"), axis=0, tiled=False)

    def rows_of(slots):
        return jnp.sum(jnp.where(owner[None, :] == slots[:, None], iota[None, :], 0), axis=1)

    local_iota = jnp.arange(LOCAL, dtype=jnp.int32)
    held_y = jnp.arange(Y, dtype=jnp.int32)
    slots = (LOCAL * (held_y * Z + mz))[:, None] + local_iota[None, :]
    slots = slots.reshape(-1)
    rows = rows_of(slots)
    level = rows // width
    hit = rows[:, None, None] == iota[None, :, None]
    cols = jnp.sum(jnp.where(hit, pattern[None], 0), axis=1)
    src = jnp.sum(jnp.where(cols[..., None] == iota, owner, 0), axis=-1)
    src = jnp.where(cols >= 0, src, -1).reshape(-1)
    dev = src // LOCAL
    bad = -(2**20)
    place_z = jnp.where(src >= 0, (dev % Z) * HELD + (dev // Z) * LOCAL + src % LOCAL, bad)

    def rows_at(place, pad, stride=PAIR):
        col = jnp.arange(pad, dtype=jnp.int32)
        at = jnp.where(col[None, :] < PAIR, place[:, None] * stride + col[None, :], bad)
        return at.reshape(-1)

    def hot(at, size):
        return (at[:, None] == jnp.arange(size, dtype=jnp.int32)[None, :]).astype(BF16)

    def first_at(slot, kind):
        return jnp.where(slot >= 0, (slot // LOCAL) * 4 + kind * LOCAL + slot % LOCAL, bad)

    pick1 = jnp.concatenate(
        [
            rows_at(first_at(src, 0), PAD),
            rows_at(first_at(slots, 0), PAD),
            rows_at(first_at(src, 1), PAIR),
        ]
    )
    pick1 = hot(pick1, Y * Z * 4 * PAIR)
    at_z = rows_at(place_z, PAD)
    pick_z = hot(at_z, Z * HELD * PAIR)
    put_z = (jnp.arange(Z * HELD * PAIR, dtype=jnp.int32)[:, None] == at_z[None, :]).astype(BF16)
    level_of_src = jnp.where(cols >= 0, cols // width, LEVELS).reshape(-1)
    group = LOCAL * PAIR

    def last_at(slot, good):
        return jnp.where(good, (slot // LOCAL) * (2 * LOCAL) + slot % LOCAL, bad)

    size = Y * Z * 2 * group
    last_rows = jnp.arange(size, dtype=jnp.int32)
    put_at = rows_at(last_at(src, level_of_src == 0), PAD)
    own_at = rows_at(last_at(slots, level > 0), PAIR)
    put_last = jnp.stack(
        [(last_rows[:, None] == (put_at + h * group)[None, :]) for h in range(2)]
    ).astype(BF16)
    own_last = jnp.stack(
        [(last_rows[:, None] == (own_at + h * group)[None, :]) for h in range(2)]
    ).astype(BF16)

    near_scratch = pltpu.VMEM((WIDE, BLOCK), F32)
    held_scratch = [
        pltpu.VMEM((HELD, NBR, BLOCK, BLOCK), BF16),
        pltpu.SemaphoreType.DMA((HELD,)),
    ]
    pad_scratch = pltpu.VMEM((PAD, BLOCK), F32)
    msg_z = shape(Z, HELD * PAIR, BLOCK)
    held = shape(HELD * PAIR, BLOCK, dtype=F32)
    sums = shape(WIDE, BLOCK, dtype=F32)
    out = (msg_z, held, shape(HELD * PAD, BLOCK, dtype=F32), shape(Y, LOCAL * NBR * PAIR, BLOCK))
    msg, solved, q, near_p = call(
        level1_kernel, out, "svv" + "h", [near_scratch] + held_scratch
    )(level, got, pick1, w)
    got = lax.all_to_all(msg, "z", 0, 0, tiled=True)
    near_p = lax.all_to_all(near_p, "y", 0, 0, tiled=True)
    msg, solved = call(
        level2_kernel, (msg_z, held), "svv" + "h" + "vv", [near_scratch] + held_scratch
    )(level, got, pick_z, w, q, solved)
    got = lax.all_to_all(msg, "z", 0, 0, tiled=True)
    msg, solved, before = call(
        level3_kernel,
        (msg_z, held, sums),
        "svv" + "h" + "vvv",
        [near_scratch, pad_scratch] + held_scratch,
    )(level, got, pick_z, w, q, solved, put_z)
    got = lax.all_to_all(msg, "z", 0, 0, tiled=True)
    msg, t, before = call(
        back2_kernel,
        (msg_z, held, sums),
        "sv" + "h" + "vvv",
        [near_scratch, pad_scratch] + held_scratch,
    )(level, got, w, solved, before, put_z)
    got = lax.all_to_all(msg, "z", 0, 0, tiled=True)
    msg, t = call(
        back1_kernel,
        (shape(Y * Z, 2 * group, BLOCK // 2), held),
        "sv" + "h" + "vvvv",
        [near_scratch, pad_scratch] + held_scratch,
    )(level, got, w, t, before, put_last, own_last)
    got = lax.all_to_all(msg, ROWS, 0, 0, tiled=True)
    mine = (my * Z + mz) * LOCAL + local_iota
    first = (rows_of(mine) < width).astype(jnp.int32)
    out = (shape(LOCAL, COUNT, BLOCK), shape(LOCAL, NBR + 1, BLOCK, BLOCK))
    return call(final_kernel, out, "svvvvv")(first, got, q_own, probes, inverses, near_p)


def solution(mesh):
    fine = Mesh(mesh.devices.reshape(Y, Z, -1, 2), ("y", "z", "x", "c"))
    parts = ("x", "c")
    return jax.shard_map(
        body,
        mesh=fine,
        in_specs=(
            P(ROWS, parts, None),
            P(ROWS, None, None, None),
            P(ROWS, None, None),
            P(),
            P(),
        ),
        out_specs=(P(ROWS, parts, None), P(ROWS, parts, None, None)),
        check_vma=False,
    )
```

time: 556 us -> 191 us (0.34)
  blocking collectives: 530 us -> 0 us
  waiting for transfers between devices: 0.01 us -> 97.5 us
  starting transfers between devices: 6.83 us -> 53.5 us
  Pallas kernels: 0 us -> 17.9 us
  between operations: 0.81 us -> 14.3 us
  matrix products: 7.89 us -> 0 us
    all_gather x4 -> x0, blocking collectives: 429 us -> none  [the longest x3 310 us: body(): solved_all = lax.all_gather(own_solved, 'rows', axis=0, tiled=True)]
    all_to_all x2 -> x0, blocking collectives: 101 us -> none  [body(): lax.all_to_all(outgoing, 'rows', split_axis=0, concat_axis=0, tiled=True)]
    all_to_all x1 -> x7, waiting for transfers between devices: 0.01 us -> 90.5 us  [the longest x4 55.2 us: body(): got = lax.all_to_all(msg, 'z', 0, 0, tiled=True)]
    all_to_all x1 -> x7, starting transfers between devices: 6.83 us -> 53.5 us  [the longest x4 25.6 us: body(): got = lax.all_to_all(msg, 'z', 0, 0, tiled=True)]
    pallas_call x0 -> x7, Pallas kernels: none -> 17.9 us  [the longest x1 3.36 us: body(): call(level2_kernel, (msg_z, held), 'svv' + 'h' + 'vv', [near_scratch] + h...]
    dot_general x21 -> x0, matrix products: 7.89 us -> none  [the longest x4 2.92 us: body(): jnp.einsum('rpb,rab->rpa', resid, inverses, preferred_element_type=f32)]
    all_gather x0 -> x1, waiting for transfers between devices: none -> 6.97 us  [body(): w = lax.all_gather(w_send, ('y', 'c'), axis=0, tiled=False)]
  transfers between devices with their start and end apart: 1 -> 8, of which waited for: 0 -> 8; matrix products, arithmetic and copies ran while one was open for 0% -> 3% of each run, Pallas kernels for 0% -> 1%
where the time goes in v2:
time: 191 us; the launch traced here: 190 us
  waiting for transfers between devices  97.5 us (51%)
  starting transfers between devices  53.5 us (28%)
  Pallas kernels  17.9 us (9%)
  between operations  14.3 us (7%)
  other arithmetic  3.92 us (2%)
  local copies, waits for them, and re-layouts  2.76 us (1%)
    all_to_all x4, waiting for transfers between devices, body(): got = lax.all_to_all(msg, 'z', 0, 0, tiled=True)  55.2 us
    all_to_all x2, waiting for transfers between devices, body(): got = lax.all_to_all(msg, ROWS, 0, 0, tiled=True)  32 us
    all_to_all x4, starting transfers between devices, body(): got = lax.all_to_all(msg, 'z', 0, 0, tiled=True)  25.6 us
    all_to_all x2, starting transfers between devices, body(): got = lax.all_to_all(msg, ROWS, 0, 0, tiled=True)  24.7 us
    all_gather x1, waiting for transfers between devices, body(): w = lax.all_gather(w_send, ('y', 'c'), axis=0, tiled=False)  6.97 us
  transfers between devices with their start and end apart: 8, of which 8 were waited for; matrix products, arithmetic and copies ran while one was open for 3% of the time, Pallas kernels for 1%

profile of v2, /device:TPU:6, one launch (start us, length us, event | category | flops | bytes accessed | tf_op | source)
XLA Modules:
  0.0 189.9 jit_solution(11228753826935454172)
XLA Ops:
  7.2 0.0 all-gather.3.cloned.1.call-start
  7.2 0.0 copy-start
  7.2 0.9 copy-done
  8.2 0.0 copy-start.2
  8.2 0.7 copy-done.2
  8.9 2.2 %shard_map.68 = (bf16[2,8,256]{2,1,0:T(8,128)(2,1)S(1)}, bf16[64,8,256]{2,1,0:T(8,128)(2,1)}, bf16[4,256,256]{2,1,0:T(8,128)(2,1)}) custom-call(s32[1]{0:T(128)} %bitcast.core_ref, bf16[2,8,256]{2,1,0:T(8,128)(2,1)S(1)} %copy-done.2, bf16[2,256,256]{2,1,0:T(8,128)(2,1)S(1)} %copy-done, bf16[2,4,256,256]{3,2,1,0:T(8,128)(2,1)} %factor_ref.1), custom_call_target="tpu_custom_call" | custom-call | tf_op jit(solution)/shard_map/pallas_call | solution.py:228
  11.0 0.0 all-gather.3.cloned.1.call-update
  11.1 18.7 %all-to-all-start = ((bf16[64,8,256]{2,1,0:T(8,128)(2,1)}), bf16[64,8,256]{2,1,0:T(8,128)(2,1)S(1)}, u32[]{:S(2)}, u32[]{:S(2)}) async-start(bf16[64,8,256]{2,1,0:T(8,128)(2,1)} %get-tuple-element.18), calls=%async_computation | async-start | bytes 524288 | tf_op jit(solution)/shard_map/all_to_all | solution.py:231
  29.8 0.1 iota_add_fusion
  29.9 0.1 add.322
  30.0 0.8 select_reduce_fusion.2
  30.8 0.1 iota_compare_fusion.8
  30.9 0.8 select_reduce_fusion.1
  31.7 0.1 copy.14
  31.8 0.1 reduce_sum.43
  31.9 0.9 select_reduce_fusion
  32.8 0.1 copy.15
  32.9 0.1 reduce_sum.45
  33.0 0.1 add_select_fusion.2
  33.1 0.1 select_n.274
  33.2 0.1 add_select_fusion.5
  33.3 0.1 select_n.271
  33.4 0.1 add_select_fusion
  33.5 0.1 select_n.266
  33.6 0.1 pad_add_fusion
  33.6 0.1 fusion.pick_ref
  33.8 17.0 %all-to-all-done.got_ref = bf16[64,8,256]{2,1,0:T(8,128)(2,1)S(1)} async-done(((bf16[64,8,256]{2,1,0:T(8,128)(2,1)}), bf16[64,8,256]{2,1,0:T(8,128)(2,1)S(1)}, u32[]{:S(2)}, u32[]{:S(2)}) %all-to-all-start) | async-done | bytes 262176 | tf_op jit(solution)/shard_map/all_to_all | solution.py:231
  50.8 7.0 %all-gather.3.cloned.1.call-done = bf16[32,256,256]{2,1,0:T(8,128)(2,1)} async-done(((bf16[4,256,256]{2,1,0:T(8,128)(2,1)}), bf16[32,256,256]{2,1,0:T(8,128)(2,1)}) %all-gather.3.cloned.1.call-update) | async-done | bytes 4194320 | tf_op jit(solution)/shard_map/all_gather | solution.py:232
  57.8 1.6 shard_map.69
  59.4 12.7 %all-to-all-start.1 = ((bf16[16,16,256]{2,1,0:T(8,128)(2,1)}), bf16[16,16,256]{2,1,0:T(8,128)(2,1)S(1)}, u32[]{:S(2)}, u32[]{:S(2)}) async-start(bf16[16,16,256]{2,1,0:T(8,128)(2,1)} %get-tuple-element.20), calls=%async_computation.1 | async-start | bytes 262144 | tf_op jit(solution)/shard_map/all_to_all | solution.py:303
  72.1 0.1 select_n.279
  72.2 0.1 fusion.2
  72.3 14.6 %all-to-all-done.1.got_ref = bf16[16,16,256]{2,1,0:T(8,128)(2,1)S(1)} async-done(((bf16[16,16,256]{2,1,0:T(8,128)(2,1)}), bf16[16,16,256]{2,1,0:T(8,128)(2,1)S(1)}, u32[]{:S(2)}, u32[]{:S(2)}) %all-to-all-start.1) | async-done | bytes 131104 | tf_op jit(solution)/shard_map/all_to_all | solution.py:303
  86.9 3.4 %shard_map.70 = (bf16[16,16,256]{2,1,0:T(8,128)(2,1)}, f32[16,256]{1,0:T(8,128)S(1)}) custom-call(s32[8]{0:T(128)S(1)} %get-tuple-element.36.level_ref, bf16[16,16,256]{2,1,0:T(8,128)(2,1)S(1)} %all-to-all-done.1.got_ref, bf16[256,256]{1,0:T(8,128)(2,1)S(1)} %get-tuple-element.45.pick_ref, bf16[8,4,256,256]{3,2,1,0:T(8,128)(2,1)} %bitcast.3, ...), custom_call_target="tpu_custom_call" | custom-call | tf_op jit(solution)/shard_map/pallas_call | solution.py:305
  90.3 4.2 %all-to-all-start.2 = ((bf16[16,16,256]{2,1,0:T(8,128)(2,1)}), bf16[16,16,256]{2,1,0:T(8,128)(2,1)S(1)}, u32[]{:S(2)}, u32[]{:S(2)}) async-start(bf16[16,16,256]{2,1,0:T(8,128)(2,1)} %get-tuple-element.23), calls=%async_computation.2 | async-start | bytes 262144 | tf_op jit(solution)/shard_map/all_to_all | solution.py:308
  94.4 0.1 select_n.284
  94.5 14.3 %all-to-all-done.2.got_ref = bf16[16,16,256]{2,1,0:T(8,128)(2,1)S(1)} async-done(((bf16[16,16,256]{2,1,0:T(8,128)(2,1)}), bf16[16,16,256]{2,1,0:T(8,128)(2,1)S(1)}, u32[]{:S(2)}, u32[]{:S(2)}) %all-to-all-start.2) | async-done | bytes 131104 | tf_op jit(solution)/shard_map/all_to_all | solution.py:308
  108.9 3.0 %shard_map.71 = (bf16[16,16,256]{2,1,0:T(8,128)(2,1)}, f32[16,256]{1,0:T(8,128)S(1)}, f32[256,256]{1,0:T(8,128)S(1)}) custom-call(s32[8]{0:T(128)S(1)} %get-tuple-element.36.level_ref, bf16[16,16,256]{2,1,0:T(8,128)(2,1)S(1)} %all-to-all-done.2.got_ref, bf16[256,256]{1,0:T(8,128)(2,1)S(1)} %get-tuple-element.45.pick_ref, bf16[8,4,256,256]{3,2,1,0:T(8,128)(2,1)} %bitcast.4, ...), custom_call_target="tpu_custom_call" | custom-call | tf_op jit(solution)/shard_map/pallas_call | solution.py:309
  111.9 5.0 %all-to-all-start.3 = ((bf16[16,16,256]{2,1,0:T(8,128)(2,1)}), bf16[16,16,256]{2,1,0:T(8,128)(2,1)S(1)}, u32[]{:S(2)}, u32[]{:S(2)}) async-start(bf16[16,16,256]{2,1,0:T(8,128)(2,1)} %get-tuple-element.25), calls=%async_computation.3 | async-start | bytes 262144 | tf_op jit(solution)/shard_map/all_to_all | solution.py:315
  116.9 0.1 add_select_fusion.4
  117.0 0.2 iota_compare_fusion.1
  117.1 13.3 %all-to-all-done.3.got_ref = bf16[16,16,256]{2,1,0:T(8,128)(2,1)S(1)} async-done(((bf16[16,16,256]{2,1,0:T(8,128)(2,1)}), bf16[16,16,256]{2,1,0:T(8,128)(2,1)S(1)}, u32[]{:S(2)}, u32[]{:S(2)}) %all-to-all-start.3) | async-done | bytes 131104 | tf_op jit(solution)/shard_map/all_to_all | solution.py:315
  130.5 3.3 %shard_map.72 = (bf16[16,16,256]{2,1,0:T(8,128)(2,1)}, f32[16,256]{1,0:T(8,128)S(1)}, f32[256,256]{1,0:T(8,128)S(1)}) custom-call(s32[8]{0:T(128)S(1)} %get-tuple-element.36.level_ref, bf16[16,16,256]{2,1,0:T(8,128)(2,1)S(1)} %all-to-all-done.3.got_ref, bf16[8,4,256,256]{3,2,1,0:T(8,128)(2,1)} %bitcast.5, f32[16,256]{1,0:T(8,128)S(1)} %get-tuple-element.26.old_ref, ...), custom_call_target="tpu_custom_call" | custom-call | tf_op jit(solution)/shard_map/pallas_call | solution.py:316
  133.8 0.0 copy-start.4
  133.8 0.0 copy-start.1
  133.8 0.0 copy-start.3
  133.8 3.7 %all-to-all-start.4 = ((bf16[16,16,256]{2,1,0:T(8,128)(2,1)}), bf16[16,16,256]{2,1,0:T(8,128)(2,1)S(1)}, u32[]{:S(2)}, u32[]{:S(2)}) async-start(bf16[16,16,256]{2,1,0:T(8,128)(2,1)} %get-tuple-element.28), calls=%async_computation.4 | async-start | bytes 262144 | tf_op jit(solution)/shard_map/all_to_all | solution.py:322
  137.5 0.1 add_convert_fusion.put_ref
  137.6 0.1 select_n.287
  137.7 0.1 iota_compare_fusion.5
  137.8 12.9 %all-to-all-done.4.got_ref = bf16[16,16,256]{2,1,0:T(8,128)(2,1)S(1)} async-done(((bf16[16,16,256]{2,1,0:T(8,128)(2,1)}), bf16[16,16,256]{2,1,0:T(8,128)(2,1)S(1)}, u32[]{:S(2)}, u32[]{:S(2)}) %all-to-all-start.4) | async-done | bytes 131104 | tf_op jit(solution)/shard_map/all_to_all | solution.py:322
  150.8 3.3 %all-to-all-start.6 = ((bf16[4,16,256]{2,1,0:T(8,128)(2,1)}), bf16[4,16,256]{2,1,0:T(8,128)(2,1)S(1)}, u32[]{:S(2)}, u32[]{:S(2)}) async-start(bf16[4,16,256]{2,1,0:T(8,128)(2,1)} %get-tuple-element.33), calls=%async_computation.6 | async-start | bytes 65536 | tf_op jit(solution)/shard_map/all_to_all | solution.py:304
  154.0 0.2 copy.16.own_ref
  154.2 1.9 %shard_map.73 = (bf16[64,8,128]{2,1,0:T(8,128)(2,1)}, f32[16,256]{1,0:T(8,128)}) custom-call(s32[8]{0:T(128)S(1)} %get-tuple-element.36.level_ref, bf16[16,16,256]{2,1,0:T(8,128)(2,1)S(1)} %all-to-all-done.4.got_ref, bf16[8,4,256,256]{3,2,1,0:T(8,128)(2,1)} %bitcast.6, f32[16,256]{1,0:T(8,128)S(1)} %get-tuple-element.29.old_ref, ...), custom_call_target="tpu_custom_call" | custom-call | tf_op jit(solution)/shard_map/pallas_call | solution.py:323
  156.1 3.3 %all-to-all-done.6.near_ref = bf16[4,16,256]{2,1,0:T(8,128)(2,1)S(1)} async-done(((bf16[4,16,256]{2,1,0:T(8,128)(2,1)}), bf16[4,16,256]{2,1,0:T(8,128)(2,1)S(1)}, u32[]{:S(2)}, u32[]{:S(2)}) %all-to-all-start.6) | async-done | bytes 32800 | tf_op jit(solution)/shard_map/all_to_all | solution.py:304
  159.4 5.9 %all-to-all-start.5 = ((bf16[64,8,128]{2,1,0:T(8,128)(2,1)}), bf16[64,8,128]{2,1,0:T(8,128)(2,1)S(1)}, u32[]{:S(2)}, u32[]{:S(2)}) async-start(bf16[64,8,128]{2,1,0:T(8,128)(2,1)} %get-tuple-element.31), calls=%async_computation.5 | async-start | bytes 262144 | tf_op jit(solution)/shard_map/all_to_all | solution.py:329
  165.4 0.0 copy-done.4
  165.4 0.2 fusion.3
  165.6 14.9 %all-to-all-done.5.got_ref = bf16[64,8,128]{2,1,0:T(8,128)(2,1)S(1)} async-done(((bf16[64,8,128]{2,1,0:T(8,128)(2,1)}), bf16[64,8,128]{2,1,0:T(8,128)(2,1)S(1)}, u32[]{:S(2)}, u32[]{:S(2)}) %all-to-all-start.5) | async-done | bytes 131104 | tf_op jit(solution)/shard_map/all_to_all | solution.py:329
  180.5 0.0 copy-done.1
  180.5 0.0 copy-done.3
  180.5 2.5 %shard_map.74 = (bf16[2,8,256]{2,1,0:T(8,128)(2,1)}, bf16[2,5,256,256]{3,2,1,0:T(8,128)(2,1)}) custom-call(s32[2]{0:T(128)S(1)} %compare_convert_fusion.first_ref, bf16[64,8,128]{2,1,0:T(8,128)(2,1)S(1)} %all-to-all-done.5.got_ref, bf16[2,8,256]{2,1,0:T(8,128)(2,1)S(1)} %get-tuple-element.32.q_ref, bf16[2,8,256]{2,1,0:T(8,128)(2,1)S(1)} %copy-done.3, ...), custom_call_target="tpu_custom_call" | custom-call | tf_op jit(solution)/shard_map/pallas_call | solution.py:333
  (12 shorter events, 0.1 us)
Async XLA Ops:
  7.2 50.6 %all-gather.3.cloned.1.call-start = ((), (), s32[]{:S(2)}) async-start(), calls=%async_computation.7 | async-start | bytes 4718592 | tf_op jit(solution)/shard_map/all_gather | solution.py:232
  7.2 1.0 copy-start
  8.2 0.7 copy-start.2
  11.1 39.7 %all-to-all-start = ((bf16[64,8,256]{2,1,0:T(8,128)(2,1)}), bf16[64,8,256]{2,1,0:T(8,128)(2,1)S(1)}, u32[]{:S(2)}, u32[]{:S(2)}) async-start(bf16[64,8,256]{2,1,0:T(8,128)(2,1)} %get-tuple-element.18), calls=%async_computation | async-start | bytes 524288 | tf_op jit(solution)/shard_map/all_to_all | solution.py:231
  59.4 27.5 %all-to-all-start.1 = ((bf16[16,16,256]{2,1,0:T(8,128)(2,1)}), bf16[16,16,256]{2,1,0:T(8,128)(2,1)S(1)}, u32[]{:S(2)}, u32[]{:S(2)}) async-start(bf16[16,16,256]{2,1,0:T(8,128)(2,1)} %get-tuple-element.20), calls=%async_computation.1 | async-start | bytes 262144 | tf_op jit(solution)/shard_map/all_to_all | solution.py:303
  90.3 18.6 %all-to-all-start.2 = ((bf16[16,16,256]{2,1,0:T(8,128)(2,1)}), bf16[16,16,256]{2,1,0:T(8,128)(2,1)S(1)}, u32[]{:S(2)}, u32[]{:S(2)}) async-start(bf16[16,16,256]{2,1,0:T(8,128)(2,1)} %get-tuple-element.23), calls=%async_computation.2 | async-start | bytes 262144 | tf_op jit(solution)/shard_map/all_to_all | solution.py:308
  111.9 18.6 %all-to-all-start.3 = ((bf16[16,16,256]{2,1,0:T(8,128)(2,1)}), bf16[16,16,256]{2,1,0:T(8,128)(2,1)S(1)}, u32[]{:S(2)}, u32[]{:S(2)}) async-start(bf16[16,16,256]{2,1,0:T(8,128)(2,1)} %get-tuple-element.25), calls=%async_computation.3 | async-start | bytes 262144 | tf_op jit(solution)/shard_map/all_to_all | solution.py:315
  133.8 31.6 %copy-start.4 = (s32[128]{0:T(128)S(1)}, s32[128]{0:T(128)}, u32[]{:S(2)}) copy-start(s32[128]{0:T(128)} %param.9) | copy-start | bytes 1540
  133.8 46.8 %copy-start.1 = (bf16[2,256,256]{2,1,0:T(8,128)(2,1)S(1)}, bf16[2,256,256]{2,1,0:T(8,128)(2,1)}, u32[]{:S(2)}) copy-start(bf16[2,256,256]{2,1,0:T(8,128)(2,1)} %inv_ref.3) | copy-start | bytes 786436
  133.8 46.7 %copy-start.3 = (bf16[2,8,256]{2,1,0:T(8,128)(2,1)S(1)}, bf16[2,8,256]{2,1,0:T(8,128)(2,1)}, u32[]{:S(2)}) copy-start(bf16[2,8,256]{2,1,0:T(8,128)(2,1)} %probes_ref.3) | copy-start | bytes 24580
  133.8 17.0 %all-to-all-start.4 = ((bf16[16,16,256]{2,1,0:T(8,128)(2,1)}), bf16[16,16,256]{2,1,0:T(8,128)(2,1)S(1)}, u32[]{:S(2)}, u32[]{:S(2)}) async-start(bf16[16,16,256]{2,1,0:T(8,128)(2,1)} %get-tuple-element.28), calls=%async_computation.4 | async-start | bytes 262144 | tf_op jit(solution)/shard_map/all_to_all | solution.py:322
  150.8 8.7 %all-to-all-start.6 = ((bf16[4,16,256]{2,1,0:T(8,128)(2,1)}), bf16[4,16,256]{2,1,0:T(8,128)(2,1)S(1)}, u32[]{:S(2)}, u32[]{:S(2)}) async-start(bf16[4,16,256]{2,1,0:T(8,128)(2,1)} %get-tuple-element.33), calls=%async_computation.6 | async-start | bytes 65536 | tf_op jit(solution)/shard_map/all_to_all | solution.py:304
  159.4 21.1 %all-to-all-start.5 = ((bf16[64,8,128]{2,1,0:T(8,128)(2,1)}), bf16[64,8,128]{2,1,0:T(8,128)(2,1)S(1)}, u32[]{:S(2)}, u32[]{:S(2)}) async-start(bf16[64,8,128]{2,1,0:T(8,128)(2,1)} %get-tuple-element.31), calls=%async_computation.5 | async-start | bytes 262144 | tf_op jit(solution)/shard_map/all_to_all | solution.py:329
Sparse Core Ops, SparseCore 0:
  11.2 46.5 all-gather.2

commit v3 on v2

--- a/solution.py
+++ b/solution.py
@@ -22,7 +22,7 @@
 SMEM = pl.BlockSpec(memory_space=pltpu.SMEM)
 
 
-def call(kernel, out_shape, places, scratch=(), flops=0, moved=0):
+def call(kernel, out_shape, places, scratch=(), room=52):
     kinds = {"s": SMEM, "v": VMEM, "h": pl.BlockSpec(memory_space=pl.ANY)}
     return pl.pallas_call(
         kernel,
@@ -30,8 +30,7 @@
         in_specs=[kinds[p] for p in places],
         out_specs=jax.tree.map(lambda _: VMEM, out_shape),
         scratch_shapes=list(scratch),
-        compiler_params=pltpu.CompilerParams(vmem_limit_bytes=52 * 2**20),
-        cost_estimate=pl.CostEstimate(flops=flops, bytes_accessed=moved, transcendentals=0),
+        compiler_params=pltpu.CompilerParams(vmem_limit_bytes=room * 2**20),
     )
 
 
@@ -45,34 +44,45 @@
     return lax.dot_general(a, b, dims, preferred_element_type=F32)
 
 
-def start_kernel(core_ref, probes_ref, inv_ref, factor_ref, q_ref, msg_ref, w_ref, d_ref, l_ref, sems):
+def start_kernel(core_ref, probes_ref, inv_ref, factor_ref, q_ref, msg_ref, w_ref, send_ref, p_ref, d_ref, l_ref, sems):
+    load_p = pltpu.make_async_copy(probes_ref, p_ref, sems.at[2])
     load_d = pltpu.make_async_copy(inv_ref, d_ref, sems.at[0])
-    load_l = pltpu.make_async_copy(factor_ref.at[core_ref[0]], l_ref, sems.at[1])
+    load_l = pltpu.make_async_copy(factor_ref, l_ref, sems.at[1])
+    load_p.start()
     load_d.start()
     load_l.start()
+    load_p.wait()
     load_d.wait()
     parts = []
     for s in range(LOCAL):
-        q = dot(probes_ref[s], d_ref[s], NT).astype(BF16)
+        q = dot(p_ref[s], d_ref[s], NT).astype(BF16)
         q_ref[s] = q
         parts.append(q.astype(F32))
     for s in range(LOCAL):
-        parts.append(probes_ref[s].astype(F32))
+        parts.append(p_ref[s].astype(F32))
     for y in range(Y):
         msg = jnp.concatenate([p[y * PAIR : (y + 1) * PAIR] for p in parts], axis=0).astype(BF16)
         for z in range(Z):
             msg_ref[y * Z + z] = msg
     load_l.wait()
-    core = core_ref[0]
-    d = d_ref[core]
-    for k in range(NBR):
-        w_ref[k] = dot(d, l_ref[k]).astype(BF16)
-
-
-def load_rows(level_ref, lev, w_ref, held_ref, sems):
+    for i in range(LOCAL):
+        slot = (core_ref[0] + i) % LOCAL
+        for k in range(NBR):
+            w = dot(d_ref[slot], l_ref[slot, k]).astype(BF16)
+            w_ref[i, k] = w
+            if i == 0:
+                send_ref[k] = w
+
+
+def load_rows(level_ref, lev, w_refs, held_ref, sems):
     waits = []
     for r in range(HELD):
-        copy = pltpu.make_async_copy(w_ref.at[r], held_ref.at[r], sems.at[r])
+        d, slot = r // LOCAL, r % LOCAL
+        if d == 0:
+            source = w_refs[0].at[slot]
+        else:
+            source = w_refs[slot * (Y - 1) + d]
+        copy = pltpu.make_async_copy(source, held_ref.at[r], sems.at[r])
 
         @pl.when(level_ref[r] == lev)
         def _():
@@ -123,21 +133,24 @@
         msg_ref[z] = value
 
 
-def level1_kernel(level_ref, got_ref, pick_ref, w_ref, msg_ref, solved_ref, q_ref, near_p_ref, near_ref, held_ref, sems):
-    waits = load_rows(level_ref, 1, w_ref, held_ref, sems)
+def neighbour_kernel(got_ref, pick_ref, near_ref):
+    got = got_ref[...].reshape(Y * Z * 4 * PAIR, BLOCK)
+    near_ref[...] = dot(pick_ref[...], got).astype(BF16).reshape(near_ref.shape)
+
+
+def level1_kernel(level_ref, got_ref, pick_ref, w0_ref, w1_ref, w2_ref, w3_ref, w4_ref, w5_ref, w6_ref, msg_ref, solved_ref, q_ref, near_ref, held_ref, sems):
+    waits = load_rows(level_ref, 1, (w0_ref, w1_ref, w2_ref, w3_ref, w4_ref, w5_ref, w6_ref), held_ref, sems)
     got = got_ref[...].reshape(Y * Z * 4 * PAIR, BLOCK)
     near_ref[...] = dot(pick_ref[:WIDE], got)
     q_ref[...] = dot(pick_ref[WIDE : WIDE + HELD * PAD], got)
-    near_p = dot(pick_ref[WIDE + HELD * PAD :], got).astype(BF16)
-    near_p_ref[...] = near_p.reshape(near_p_ref.shape)
     for r in range(HELD):
         solved_ref[r * PAIR : (r + 1) * PAIR] = q_ref[r * PAD : r * PAD + PAIR]
     forward_rows(level_ref, 1, waits, near_ref, q_ref, held_ref, solved_ref)
     broadcast_to_z(solved_ref[...].astype(BF16), msg_ref)
 
 
-def level2_kernel(level_ref, got_ref, pick_ref, w_ref, q_ref, old_ref, msg_ref, solved_ref, near_ref, held_ref, sems):
-    waits = load_rows(level_ref, 2, w_ref, held_ref, sems)
+def level2_kernel(level_ref, got_ref, pick_ref, w0_ref, w1_ref, w2_ref, w3_ref, w4_ref, w5_ref, w6_ref, q_ref, old_ref, msg_ref, solved_ref, near_ref, held_ref, sems):
+    waits = load_rows(level_ref, 2, (w0_ref, w1_ref, w2_ref, w3_ref, w4_ref, w5_ref, w6_ref), held_ref, sems)
     near_ref[...] = dot(pick_ref[...], got_ref[...].reshape(Z * HELD * PAIR, BLOCK))
     solved_ref[...] = old_ref[...]
     forward_rows(level_ref, 2, waits, near_ref, q_ref, held_ref, solved_ref)
@@ -145,9 +158,9 @@
 
 
 def level3_kernel(
-    level_ref, got_ref, pick_ref, w_ref, q_ref, old_ref, put_ref,
+    level_ref, got_ref, pick_ref, w0_ref, w1_ref, w2_ref, w3_ref, w4_ref, w5_ref, w6_ref, q_ref, old_ref, put_ref,
     msg_ref, solved_ref, terms_ref, near_ref, pad_ref, held_ref, sems):
-    waits = load_rows(level_ref, 3, w_ref, held_ref, sems)
+    waits = load_rows(level_ref, 3, (w0_ref, w1_ref, w2_ref, w3_ref, w4_ref, w5_ref, w6_ref), held_ref, sems)
     near_ref[...] = dot(pick_ref[...], got_ref[...].reshape(Z * HELD * PAIR, BLOCK))
     solved_ref[...] = old_ref[...]
     forward_rows(level_ref, 3, waits, near_ref, q_ref, held_ref, solved_ref)
@@ -168,9 +181,9 @@
 
 
 def back2_kernel(
-    level_ref, got_ref, w_ref, old_ref, before_ref, put_ref,
+    level_ref, got_ref, w0_ref, w1_ref, w2_ref, w3_ref, w4_ref, w5_ref, w6_ref, old_ref, before_ref, put_ref,
     msg_ref, t_ref, sums_ref, terms_ref, pad_ref, held_ref, sems):
-    waits = load_rows(level_ref, 2, w_ref, held_ref, sems)
+    waits = load_rows(level_ref, 2, (w0_ref, w1_ref, w2_ref, w3_ref, w4_ref, w5_ref, w6_ref), held_ref, sems)
     finish_rows(level_ref, 2, got_ref, old_ref, t_ref)
     backward_rows(level_ref, 2, waits, t_ref, pad_ref, held_ref, terms_ref)
     sums_ref[...] = before_ref[...] + terms_ref[...]
@@ -179,8 +192,8 @@
 
 
 def back1_kernel(
-    level_ref, got_ref, w_ref, old_ref, before_ref, put_ref, own_ref, msg_ref, t_ref, terms_ref, pad_ref, held_ref, sems):
-    waits = load_rows(level_ref, 1, w_ref, held_ref, sems)
+    level_ref, got_ref, w0_ref, w1_ref, w2_ref, w3_ref, w4_ref, w5_ref, w6_ref, old_ref, before_ref, put_ref, own_ref, msg_ref, t_ref, terms_ref, pad_ref, held_ref, sems):
+    waits = load_rows(level_ref, 1, (w0_ref, w1_ref, w2_ref, w3_ref, w4_ref, w5_ref, w6_ref), held_ref, sems)
     finish_rows(level_ref, 1, got_ref, old_ref, t_ref)
     backward_rows(level_ref, 1, waits, t_ref, pad_ref, held_ref, terms_ref)
     sums = before_ref[...] + terms_ref[...]
@@ -191,7 +204,8 @@
     msg_ref[...] = (left + right).astype(BF16).reshape(msg_ref.shape)
 
 
-def final_kernel(first_ref, got_ref, q_ref, probes_ref, inv_ref, near_ref, x_ref, sel_ref):
+def final_kernel(first_ref, got_ref, q_ref, probes_ref, inv_ref, turn_ref, near0_ref, near1_ref, near2_ref, near3_ref, x_ref, sel_ref):
+    near_refs = (near0_ref, near1_ref, near2_ref, near3_ref)
     group = LOCAL * PAIR
     sums = []
     for y in range(Y):
@@ -202,12 +216,13 @@
         base = jnp.where(first_ref[s] == 1, q_ref[s].astype(F32) - acc, acc)
         x = dot(base.astype(BF16), inv_ref[s]).astype(BF16)
         x_ref[s] = x
+        turned = dot(turn_ref[...], x).astype(BF16)
         for k in range(NBR):
             at = (s * NBR + k) * PAIR
             near = jnp.concatenate(
-                [near_ref[y, at : at + PAIR].astype(F32) for y in range(Y)], axis=0
+                [ref[at : at + PAIR].astype(F32) for ref in near_refs], axis=0
             ).astype(BF16)
-            sel_ref[s, k] = (dot(x, near, TN) * (1.0 / COUNT)).astype(BF16)
+            sel_ref[s, k] = (dot(turned, near, TN) * (1.0 / COUNT)).astype(BF16)
         sel_ref[s, NBR] = (dot(x, probes_ref[s], TN) * (1.0 / COUNT)).astype(BF16)
 
 
@@ -219,24 +234,32 @@
 
     core = lax.axis_index("c").reshape(1)
     w_shape = shape(NBR, BLOCK, BLOCK)
-    out = (shape(LOCAL, COUNT, BLOCK), shape(Y * Z, 4 * PAIR, BLOCK), w_shape)
+    w_pair = shape(LOCAL, NBR, BLOCK, BLOCK)
+    out = (shape(LOCAL, COUNT, BLOCK), shape(Y * Z, 4 * PAIR, BLOCK), w_pair, w_shape)
     scratch = [
+        pltpu.VMEM((LOCAL, COUNT, BLOCK), BF16),
         pltpu.VMEM((LOCAL, BLOCK, BLOCK), BF16),
-        pltpu.VMEM((NBR, BLOCK, BLOCK), BF16),
-        pltpu.SemaphoreType.DMA((2,)),
+        pltpu.VMEM((LOCAL, NBR, BLOCK, BLOCK), BF16),
+        pltpu.SemaphoreType.DMA((3,)),
     ]
-    q_own, msg, w_send = call(start_kernel, out, "svhh", scratch)(
+    q_own, msg, w_own, w_send = call(start_kernel, out, "shhh", scratch, room=60)(
         core, probes, inverses, factor
     )
+    def along(step):
+        return lax.ppermute(w_send, "y", [(i, (i + step) % Y) for i in range(Y)])
+
+    w_mine = [along(step) for step in (1, 2, 3)]
     got = lax.all_to_all(msg, ROWS, 0, 0, tiled=True)
-    w = lax.all_gather(w_send, ("y", "c"), axis=0, tiled=False)
+    w_other = [lax.ppermute(v, "c", [(0, 1), (1, 0)]) for v in w_mine]
+    ws = [w_own, *w_mine, *w_other]
 
     def rows_of(slots):
         return jnp.sum(jnp.where(owner[None, :] == slots[:, None], iota[None, :], 0), axis=1)
 
     local_iota = jnp.arange(LOCAL, dtype=jnp.int32)
-    held_y = jnp.arange(Y, dtype=jnp.int32)
-    slots = (LOCAL * (held_y * Z + mz))[:, None] + local_iota[None, :]
+    held_y = (my - jnp.arange(Y, dtype=jnp.int32)) % Y
+    core = lax.axis_index("c")
+    slots = (LOCAL * (held_y * Z + mz))[:, None] + (core + local_iota[None, :]) % LOCAL
     slots = slots.reshape(-1)
     rows = rows_of(slots)
     level = rows // width
@@ -246,7 +269,8 @@
     src = jnp.where(cols >= 0, src, -1).reshape(-1)
     dev = src // LOCAL
     bad = -(2**20)
-    place_z = jnp.where(src >= 0, (dev % Z) * HELD + (dev // Z) * LOCAL + src % LOCAL, bad)
+    turn = (my - dev // Z) % Y
+    place_z = jnp.where(src >= 0, (dev % Z) * HELD + turn * LOCAL + (src - core) % LOCAL, bad)
 
     def rows_at(place, pad, stride=PAIR):
         col = jnp.arange(pad, dtype=jnp.int32)
@@ -259,14 +283,23 @@
     def first_at(slot, kind):
         return jnp.where(slot >= 0, (slot // LOCAL) * 4 + kind * LOCAL + slot % LOCAL, bad)
 
+    natural = (held_y[:, None] * Z + mz) * LOCAL + local_iota[None, :]
+    nat_rows = rows_of(natural.reshape(-1))
+    nat_cols = jnp.sum(jnp.where(nat_rows[:, None, None] == iota[None, :, None], pattern[None], 0), axis=1)
+    nat_src = jnp.sum(jnp.where(nat_cols[..., None] == iota, owner, 0), axis=-1)
+    nat_src = jnp.where(nat_cols >= 0, nat_src, -1).reshape(-1)
     pick1 = jnp.concatenate(
         [
             rows_at(first_at(src, 0), PAD),
             rows_at(first_at(slots, 0), PAD),
-            rows_at(first_at(src, 1), PAIR),
         ]
     )
     pick1 = hot(pick1, Y * Z * 4 * PAIR)
+    pick_p = hot(rows_at(first_at(nat_src, 1), PAIR), Y * Z * 4 * PAIR)
+    near_p = call(neighbour_kernel, shape(Y, LOCAL * NBR * PAIR, BLOCK), "vv")(got, pick_p)
+    near_p = [near_p[0]] + [
+        lax.ppermute(near_p[d], "y", [(i, (i - d) % Y) for i in range(Y)]) for d in range(1, Y)
+    ]
     at_z = rows_at(place_z, PAD)
     pick_z = hot(at_z, Z * HELD * PAIR)
     put_z = (jnp.arange(Z * HELD * PAIR, dtype=jnp.int32)[:, None] == at_z[None, :]).astype(BF16)
@@ -296,41 +329,44 @@
     msg_z = shape(Z, HELD * PAIR, BLOCK)
     held = shape(HELD * PAIR, BLOCK, dtype=F32)
     sums = shape(WIDE, BLOCK, dtype=F32)
-    out = (msg_z, held, shape(HELD * PAD, BLOCK, dtype=F32), shape(Y, LOCAL * NBR * PAIR, BLOCK))
-    msg, solved, q, near_p = call(
-        level1_kernel, out, "svv" + "h", [near_scratch] + held_scratch
-    )(level, got, pick1, w)
+    out = (msg_z, held, shape(HELD * PAD, BLOCK, dtype=F32))
+    msg, solved, q = call(
+        level1_kernel, out, "svv" + "h" * 7, [near_scratch] + held_scratch
+    )(level, got, pick1, *ws)
     got = lax.all_to_all(msg, "z", 0, 0, tiled=True)
-    near_p = lax.all_to_all(near_p, "y", 0, 0, tiled=True)
     msg, solved = call(
-        level2_kernel, (msg_z, held), "svv" + "h" + "vv", [near_scratch] + held_scratch
-    )(level, got, pick_z, w, q, solved)
+        level2_kernel, (msg_z, held), "svv" + "h" * 7 + "vv", [near_scratch] + held_scratch
+    )(level, got, pick_z, *ws, q, solved)
     got = lax.all_to_all(msg, "z", 0, 0, tiled=True)
     msg, solved, before = call(
         level3_kernel,
         (msg_z, held, sums),
-        "svv" + "h" + "vvv",
+        "svv" + "h" * 7 + "vvv",
         [near_scratch, pad_scratch] + held_scratch,
-    )(level, got, pick_z, w, q, solved, put_z)
+    )(level, got, pick_z, *ws, q, solved, put_z)
     got = lax.all_to_all(msg, "z", 0, 0, tiled=True)
     msg, t, before = call(
         back2_kernel,
         (msg_z, held, sums),
-        "sv" + "h" + "vvv",
+        "sv" + "h" * 7 + "vvv",
         [near_scratch, pad_scratch] + held_scratch,
-    )(level, got, w, solved, before, put_z)
+    )(level, got, *ws, solved, before, put_z)
     got = lax.all_to_all(msg, "z", 0, 0, tiled=True)
     msg, t = call(
         back1_kernel,
         (shape(Y * Z, 2 * group, BLOCK // 2), held),
-        "sv" + "h" + "vvvv",
+        "sv" + "h" * 7 + "vvvv",
         [near_scratch, pad_scratch] + held_scratch,
-    )(level, got, w, t, before, put_last, own_last)
+    )(level, got, *ws, t, before, put_last, own_last)
     got = lax.all_to_all(msg, ROWS, 0, 0, tiled=True)
     mine = (my * Z + mz) * LOCAL + local_iota
     first = (rows_of(mine) < width).astype(jnp.int32)
     out = (shape(LOCAL, COUNT, BLOCK), shape(LOCAL, NBR + 1, BLOCK, BLOCK))
-    return call(final_kernel, out, "svvvvv")(first, got, q_own, probes, inverses, near_p)
+    column = jnp.arange(COUNT, dtype=jnp.int32)
+    turn = (((column + PAIR * my) % COUNT)[:, None] == column[None, :]).astype(BF16)
+    return call(final_kernel, out, "svvvvvvvvv")(
+        first, got, q_own, probes, inverses, turn, *near_p
+    )
 
 
 def solution(mesh):

time: 191 us -> 167 us (0.87)
  waiting for transfers between devices: 97.5 us -> 66.9 us
  starting transfers between devices: 53.5 us -> 72.7 us
  between operations: 14.3 us -> 1.07 us
  Pallas kernels: 17.9 us -> 20.3 us
    ppermute x0 -> x9, starting transfers between devices: none -> 28.1 us  [the longest x3 11.5 us: along(): return lax.ppermute(w_send, 'y', [(i, (i + step) % Y) for i in range(Y)])]
    all_to_all x2, waiting for transfers between devices: 32 us -> 12 us  [body(): got = lax.all_to_all(msg, ROWS, 0, 0, tiled=True)]
    all_gather x1 -> x0, waiting for transfers between devices: 6.97 us -> none  [body(): w = lax.all_gather(w_send, ('y', 'c'), axis=0, tiled=False)]
    all_to_all x4, starting transfers between devices: 25.6 us -> 19.1 us  [body(): got = lax.all_to_all(msg, 'z', 0, 0, tiled=True)]
    all_to_all x4, waiting for transfers between devices: 55.2 us -> 51 us  [body(): got = lax.all_to_all(msg, 'z', 0, 0, tiled=True)]
    ppermute x0 -> x9, waiting for transfers between devices: none -> 3.89 us  [the longest x3 3.87 us: body(): lax.ppermute(near_p[d], 'y', [(i, (i - d) % Y) for i in range(Y)])]
    all_to_all x1 -> x0, waiting for transfers between devices: 3.3 us -> none  [body(): near_p = lax.all_to_all(near_p, 'y', 0, 0, tiled=True)]
    all_to_all x1 -> x0, starting transfers between devices: 3.26 us -> none  [body(): near_p = lax.all_to_all(near_p, 'y', 0, 0, tiled=True)]
  transfers between devices with their start and end apart: 8 -> 15, of which waited for: 8 -> 8; matrix products, arithmetic and copies ran while one was open for 3% -> 3% of each run, Pallas kernels for 1% -> 0%
where the time goes in v3:
time: 167 us; the launch traced here: 166 us
  starting transfers between devices  72.7 us (44%)
  waiting for transfers between devices  66.9 us (40%)
  Pallas kernels  20.3 us (12%)
  other arithmetic  3.03 us (2%)
  local copies, waits for them, and re-layouts  2.17 us (1%)
    all_to_all x4, waiting for transfers between devices, body(): got = lax.all_to_all(msg, 'z', 0, 0, tiled=True)  51 us
    all_to_all x2, starting transfers between devices, body(): got = lax.all_to_all(msg, ROWS, 0, 0, tiled=True)  25.4 us
    all_to_all x4, starting transfers between devices, body(): got = lax.all_to_all(msg, 'z', 0, 0, tiled=True)  19.1 us
    all_to_all x2, waiting for transfers between devices, body(): got = lax.all_to_all(msg, ROWS, 0, 0, tiled=True)  12 us
    ppermute x3, starting transfers between devices, along(): return lax.ppermute(w_send, 'y', [(i, (i + step) % Y) for i in range(Y)])  11.5 us
    ppermute x3, starting transfers between devices, body(): lax.ppermute(near_p[d], 'y', [(i, (i - d) % Y) for i in range(Y)])  10.3 us
    ppermute x3, starting transfers between devices, body(): w_other = [lax.ppermute(v, 'c', [(0, 1), (1, 0)]) for v in w_mine]  6.25 us
    pallas_call x1, Pallas kernels, body(): call(level3_kernel, (msg_z, held, sums), 'svv' + 'h' * 7 + 'vvv', [near_s...  4.31 us
  transfers between devices with their start and end apart: 15, of which 8 were waited for; matrix products, arithmetic and copies ran while one was open for 3% of the time, Pallas kernels for 0%

profile of v3, /device:TPU:6, one launch (start us, length us, event | category | flops | bytes accessed | tf_op | source)
XLA Modules:
  0.0 166.1 jit_solution(17628810815289734113)
XLA Ops:
  0.7 2.8 %shard_map.68 = (bf16[2,8,256]{2,1,0:T(8,128)(2,1)}, bf16[64,8,256]{2,1,0:T(8,128)(2,1)}, bf16[2,4,256,256]{3,2,1,0:T(8,128)(2,1)}, bf16[4,256,256]{2,1,0:T(8,128)(2,1)}) custom-call(s32[1]{0:T(128)} %bitcast.core_ref, bf16[2,8,256]{2,1,0:T(8,128)(2,1)} %probes_ref.3, bf16[2,256,256]{2,1,0:T(8,128)(2,1)} %inv_ref.3, bf16[2,4,256,256]{3,2,1,0:T(8,128)(2,1)} %factor_ref.1), custom_call_target="tpu_custom_call" | custom-call | tf_op jit(solution)/shard_map/pallas_call | solution.py:245
  3.5 3.5 %collective-permute-start = (bf16[4,256,256]{2,1,0:T(8,128)(2,1)}, bf16[4,256,256]{2,1,0:T(8,128)(2,1)S(1)}, u32[]{:S(2)}, u32[]{:S(2)}) collective-permute-start(bf16[4,256,256]{2,1,0:T(8,128)(2,1)} %get-tuple-element.20), channel_id=1, source_target_pairs={{0,128},{128,256},{256,384},{384,0},{1,129},{129,257},{257,385},{3... | collective-permute-start | bytes 1572872 | tf_op jit(solution)/shard_map/ppermute | solution.py:249
  7.0 4.8 %collective-permute-start.1 = (bf16[4,256,256]{2,1,0:T(8,128)(2,1)}, bf16[4,256,256]{2,1,0:T(8,128)(2,1)S(1)}, u32[]{:S(2)}, u32[]{:S(2)}) collective-permute-start(bf16[4,256,256]{2,1,0:T(8,128)(2,1)} %get-tuple-element.20), channel_id=1, source_target_pairs={{0,256},{128,384},{256,0},{384,128},{1,257},{129,385},{257,1},{385... | collective-permute-start | bytes 1572872 | tf_op jit(solution)/shard_map/ppermute | solution.py:249
  11.8 3.3 %collective-permute-start.2 = (bf16[4,256,256]{2,1,0:T(8,128)(2,1)}, bf16[4,256,256]{2,1,0:T(8,128)(2,1)S(1)}, u32[]{:S(2)}, u32[]{:S(2)}) collective-permute-start(bf16[4,256,256]{2,1,0:T(8,128)(2,1)} %get-tuple-element.20), channel_id=1, source_target_pairs={{0,384},{128,0},{256,128},{384,256},{1,385},{129,1},{257,129},{385... | collective-permute-start | bytes 1572872 | tf_op jit(solution)/shard_map/ppermute | solution.py:249
  15.0 16.2 %all-to-all-start = ((bf16[64,8,256]{2,1,0:T(8,128)(2,1)}), bf16[64,8,256]{2,1,0:T(8,128)(2,1)S(1)}, u32[]{:S(2)}, u32[]{:S(2)}) async-start(bf16[64,8,256]{2,1,0:T(8,128)(2,1)} %get-tuple-element.18), calls=%async_computation | async-start | bytes 524288 | tf_op jit(solution)/shard_map/all_to_all | solution.py:252
  31.4 0.1 add.420
  31.5 0.1 add.454
  31.6 0.2 select_reduce_fusion.4
  31.8 0.1 iota_compare_fusion.10
  31.9 0.2 select_reduce_fusion.1
  32.1 0.1 copy.15
  32.2 0.3 select_reduce_fusion
  32.5 0.1 copy.16
  32.6 0.1 reduce_sum.72
  32.6 0.1 reduce_sum.70
  32.8 0.1 add_select_fusion.5
  32.9 0.1 add_select_fusion.1
  33.0 0.1 select_n.335
  33.0 0.1 select_n.340
  33.1 0.1 select_n.352
  33.2 0.1 add_select_fusion.4
  33.3 0.1 select_n.355
  33.4 1.9 %collective-permute-start.3 = (bf16[4,256,256]{2,1,0:T(8,128)(2,1)S(1)}, bf16[4,256,256]{2,1,0:T(8,128)(2,1)S(1)}, u32[]{:S(2)}, u32[]{:S(2)}) collective-permute-start(bf16[4,256,256]{2,1,0:T(8,128)(2,1)S(1)} %collective-permute-done.w1_ref), channel_id=1, source_target_pairs={{0,1},{1,0},{2,3},{3,2},{4,5},{5,4},{6,7},{7,6},{8,9},{9,8},{10,11... | collective-permute-start | bytes 1572872 | tf_op jit(solution)/shard_map/ppermute | solution.py:253
  35.3 2.4 %collective-permute-start.4 = (bf16[4,256,256]{2,1,0:T(8,128)(2,1)S(1)}, bf16[4,256,256]{2,1,0:T(8,128)(2,1)}, u32[]{:S(2)}, u32[]{:S(2)}) collective-permute-start(bf16[4,256,256]{2,1,0:T(8,128)(2,1)S(1)} %collective-permute-done.1.w2_ref), channel_id=1, source_target_pairs={{0,1},{1,0},{2,3},{3,2},{4,5},{5,4},{6,7},{7,6},{8,9},{9,8},{10,11... | collective-permute-start | bytes 1572872 | tf_op jit(solution)/shard_map/ppermute | solution.py:253
  37.8 1.9 %collective-permute-start.5 = (bf16[4,256,256]{2,1,0:T(8,128)(2,1)S(1)}, bf16[4,256,256]{2,1,0:T(8,128)(2,1)}, u32[]{:S(2)}, u32[]{:S(2)}) collective-permute-start(bf16[4,256,256]{2,1,0:T(8,128)(2,1)S(1)} %collective-permute-done.2.w3_ref), channel_id=1, source_target_pairs={{0,1},{1,0},{2,3},{3,2},{4,5},{5,4},{6,7},{7,6},{8,9},{9,8},{10,11... | collective-permute-start | bytes 1572872 | tf_op jit(solution)/shard_map/ppermute | solution.py:253
  39.7 0.1 iota_compare_fusion.2
  39.8 0.1 fusion.pick_ref
  39.9 11.5 %all-to-all-done.got_ref = bf16[64,8,256]{2,1,0:T(8,128)(2,1)S(1)} async-done(((bf16[64,8,256]{2,1,0:T(8,128)(2,1)}), bf16[64,8,256]{2,1,0:T(8,128)(2,1)S(1)}, u32[]{:S(2)}, u32[]{:S(2)}) %all-to-all-start) | async-done | bytes 262176 | tf_op jit(solution)/shard_map/all_to_all | solution.py:252
  51.5 0.8 copy-done.4
  52.2 3.1 %shard_map.69 = (bf16[16,16,256]{2,1,0:T(8,128)(2,1)}, f32[16,256]{1,0:T(8,128)S(1)}, f32[64,256]{1,0:T(8,128)S(1)}) custom-call(s32[8]{0:T(128)S(1)} %get-tuple-element.42.level_ref, bf16[64,8,256]{2,1,0:T(8,128)(2,1)S(1)} %all-to-all-done.got_ref, bf16[320,512]{1,0:T(8,128)(2,1)S(1)} %fusion.pick_ref, bf16[2,4,256,256]{3,2,1,0:T(8,128)(2,1)} %get-tuple-element.19.w0_ref, ...), custom_call_target="tpu_custom_call" | custom-call | tf_op jit(solution)/shard_map/pallas_call | solution.py:333
  55.3 4.6 %all-to-all-start.1 = ((bf16[16,16,256]{2,1,0:T(8,128)(2,1)}), bf16[16,16,256]{2,1,0:T(8,128)(2,1)S(1)}, u32[]{:S(2)}, u32[]{:S(2)}) async-start(bf16[16,16,256]{2,1,0:T(8,128)(2,1)} %get-tuple-element.21), calls=%async_computation.1 | async-start | bytes 262144 | tf_op jit(solution)/shard_map/all_to_all | solution.py:336
  60.0 0.1 select_n.347
  60.1 0.1 iota_compare_fusion.1
  60.2 0.1 fusion.2
  60.3 13.2 %all-to-all-done.1.got_ref = bf16[16,16,256]{2,1,0:T(8,128)(2,1)S(1)} async-done(((bf16[16,16,256]{2,1,0:T(8,128)(2,1)}), bf16[16,16,256]{2,1,0:T(8,128)(2,1)S(1)}, u32[]{:S(2)}, u32[]{:S(2)}) %all-to-all-start.1) | async-done | bytes 131104 | tf_op jit(solution)/shard_map/all_to_all | solution.py:336
  73.5 1.5 shard_map.70
  75.0 5.2 %all-to-all-start.2 = ((bf16[16,16,256]{2,1,0:T(8,128)(2,1)}), bf16[16,16,256]{2,1,0:T(8,128)(2,1)S(1)}, u32[]{:S(2)}, u32[]{:S(2)}) async-start(bf16[16,16,256]{2,1,0:T(8,128)(2,1)} %get-tuple-element.24), calls=%async_computation.2 | async-start | bytes 262144 | tf_op jit(solution)/shard_map/all_to_all | solution.py:340
  80.3 0.1 iota_compare_fusion.6
  80.4 0.9 add_convert_fusion.put_ref
  81.3 12.2 %all-to-all-done.2.got_ref = bf16[16,16,256]{2,1,0:T(8,128)(2,1)S(1)} async-done(((bf16[16,16,256]{2,1,0:T(8,128)(2,1)}), bf16[16,16,256]{2,1,0:T(8,128)(2,1)S(1)}, u32[]{:S(2)}, u32[]{:S(2)}) %all-to-all-start.2) | async-done | bytes 131104 | tf_op jit(solution)/shard_map/all_to_all | solution.py:340
  93.5 4.3 %shard_map.71 = (bf16[16,16,256]{2,1,0:T(8,128)(2,1)}, f32[16,256]{1,0:T(8,128)S(1)}, f32[256,256]{1,0:T(8,128)S(1)}) custom-call(s32[8]{0:T(128)S(1)} %get-tuple-element.42.level_ref, bf16[16,16,256]{2,1,0:T(8,128)(2,1)S(1)} %all-to-all-done.2.got_ref, bf16[256,256]{1,0:T(8,128)(2,1)S(1)} %get-tuple-element.52.pick_ref, ...), custom_call_target="tpu_custom_call" | custom-call | tf_op jit(solution)/shard_map/pallas_call | solution.py:341
  97.8 3.8 %all-to-all-start.3 = ((bf16[16,16,256]{2,1,0:T(8,128)(2,1)}), bf16[16,16,256]{2,1,0:T(8,128)(2,1)S(1)}, u32[]{:S(2)}, u32[]{:S(2)}) async-start(bf16[16,16,256]{2,1,0:T(8,128)(2,1)} %get-tuple-element.26), calls=%async_computation.3 | async-start | bytes 262144 | tf_op jit(solution)/shard_map/all_to_all | solution.py:347
  101.7 0.1 copy.18
  101.7 0.1 select_n.361
  101.8 0.1 add_select_fusion
  101.9 12.9 %all-to-all-done.3.got_ref = bf16[16,16,256]{2,1,0:T(8,128)(2,1)S(1)} async-done(((bf16[16,16,256]{2,1,0:T(8,128)(2,1)}), bf16[16,16,256]{2,1,0:T(8,128)(2,1)S(1)}, u32[]{:S(2)}, u32[]{:S(2)}) %all-to-all-start.3) | async-done | bytes 131104 | tf_op jit(solution)/shard_map/all_to_all | solution.py:347
  114.9 1.7 %shard_map.72 = (bf16[16,16,256]{2,1,0:T(8,128)(2,1)}, f32[16,256]{1,0:T(8,128)S(1)}, f32[256,256]{1,0:T(8,128)S(1)}) custom-call(s32[8]{0:T(128)S(1)} %get-tuple-element.42.level_ref, bf16[16,16,256]{2,1,0:T(8,128)(2,1)S(1)} %all-to-all-done.3.got_ref, bf16[2,4,256,256]{3,2,1,0:T(8,128)(2,1)} %get-tuple-element.19.w0_ref, ...), custom_call_target="tpu_custom_call" | custom-call | tf_op jit(solution)/shard_map/pallas_call | solution.py:348
  116.5 5.4 %all-to-all-start.4 = ((bf16[16,16,256]{2,1,0:T(8,128)(2,1)}), bf16[16,16,256]{2,1,0:T(8,128)(2,1)S(1)}, u32[]{:S(2)}, u32[]{:S(2)}) async-start(bf16[16,16,256]{2,1,0:T(8,128)(2,1)} %get-tuple-element.29), calls=%async_computation.4 | async-start | bytes 262144 | tf_op jit(solution)/shard_map/all_to_all | solution.py:354
  122.0 0.2 copy.17.own_ref
  122.1 0.1 select_n.366
  122.2 0.1 fusion.4.turn_ref
  122.3 0.1 fusion.3.pick_ref
  122.4 12.6 %all-to-all-done.4.got_ref = bf16[16,16,256]{2,1,0:T(8,128)(2,1)S(1)} async-done(((bf16[16,16,256]{2,1,0:T(8,128)(2,1)}), bf16[16,16,256]{2,1,0:T(8,128)(2,1)S(1)}, u32[]{:S(2)}, u32[]{:S(2)}) %all-to-all-start.4) | async-done | bytes 131104 | tf_op jit(solution)/shard_map/all_to_all | solution.py:354
  135.0 3.9 %shard_map.73 = (bf16[64,8,128]{2,1,0:T(8,128)(2,1)}, f32[16,256]{1,0:T(8,128)}) custom-call(s32[8]{0:T(128)S(1)} %get-tuple-element.42.level_ref, bf16[16,16,256]{2,1,0:T(8,128)(2,1)S(1)} %all-to-all-done.4.got_ref, bf16[2,4,256,256]{3,2,1,0:T(8,128)(2,1)} %get-tuple-element.19.w0_ref, bf16[4,256,256]{2,1,0:T(8,128)(2,1)S(1)} %collective-permute-done.w1_ref, ...), custom_call_target="tpu_custom_call" | custom-call | tf_op jit(solution)/shard_map/pallas_call | solution.py:355
  138.9 9.2 %all-to-all-start.5 = ((bf16[64,8,128]{2,1,0:T(8,128)(2,1)}), bf16[64,8,128]{2,1,0:T(8,128)(2,1)S(1)}, u32[]{:S(2)}, u32[]{:S(2)}) async-start(bf16[64,8,128]{2,1,0:T(8,128)(2,1)} %get-tuple-element.32), calls=%async_computation.5 | async-start | bytes 262144 | tf_op jit(solution)/shard_map/all_to_all | solution.py:361
  148.2 0.2 fusion.5
  148.3 0.2 shard_map.74
  148.5 4.9 %collective-permute-start.6 = (bf16[16,256]{1,0:T(8,128)(2,1)S(1)}, bf16[16,256]{1,0:T(8,128)(2,1)S(1)}, u32[]{:S(2)}, u32[]{:S(2)}) collective-permute-start(bf16[16,256]{1,0:T(8,128)(2,1)S(1)} %get-tuple-element.49), channel_id=1, source_target_pairs={{0,384},{128,0},{256,128},{384,256},{1,385},{129,1},{257,129},{385... | collective-permute-start | bytes 24584 | tf_op jit(solution)/shard_map/ppermute | solution.py:301
  153.4 2.6 %collective-permute-start.7 = (bf16[16,256]{1,0:T(8,128)(2,1)S(1)}, bf16[16,256]{1,0:T(8,128)(2,1)S(1)}, u32[]{:S(2)}, u32[]{:S(2)}) collective-permute-start(bf16[16,256]{1,0:T(8,128)(2,1)S(1)} %get-tuple-element.48), channel_id=1, source_target_pairs={{0,256},{128,384},{256,0},{384,128},{1,257},{129,385},{257,1},{385... | collective-permute-start | bytes 24584 | tf_op jit(solution)/shard_map/ppermute | solution.py:301
  156.0 2.9 %collective-permute-start.8 = (bf16[16,256]{1,0:T(8,128)(2,1)S(1)}, bf16[16,256]{1,0:T(8,128)(2,1)S(1)}, u32[]{:S(2)}, u32[]{:S(2)}) collective-permute-start(bf16[16,256]{1,0:T(8,128)(2,1)S(1)} %get-tuple-element.47), channel_id=1, source_target_pairs={{0,128},{128,256},{256,384},{384,0},{1,129},{129,257},{257,385},{3... | collective-permute-start | bytes 24584 | tf_op jit(solution)/shard_map/ppermute | solution.py:301
  158.9 1.6 collective-permute-done.7.near2_ref
  160.5 2.3 %collective-permute-done.8.near3_ref = bf16[16,256]{1,0:T(8,128)(2,1)S(1)} collective-permute-done((bf16[16,256]{1,0:T(8,128)(2,1)S(1)}, bf16[16,256]{1,0:T(8,128)(2,1)S(1)}, u32[]{:S(2)}, u32[]{:S(2)}) %collective-permute-start.8) | collective-permute-done | bytes 8224 | tf_op jit(solution)/shard_map/ppermute | solution.py:301
  162.8 0.5 all-to-all-done.5.got_ref
  163.3 2.8 %shard_map.75 = (bf16[2,8,256]{2,1,0:T(8,128)(2,1)}, bf16[2,5,256,256]{3,2,1,0:T(8,128)(2,1)}) custom-call(s32[2]{0:T(128)S(1)} %compare_convert_fusion.first_ref, bf16[64,8,128]{2,1,0:T(8,128)(2,1)S(1)} %all-to-all-done.5.got_ref, bf16[2,8,256]{2,1,0:T(8,128)(2,1)S(1)} %copy-done.2, bf16[2,8,256]{2,1,0:T(8,128)(2,1)S(1)} %copy-done.1, ...), custom_call_target="tpu_custom_call" | custom-call | tf_op jit(solution)/shard_map/pallas_call | solution.py:367
  (39 shorter events, 0.3 us)
Async XLA Ops:
  0.6 30.9 %copy-start.5 = (s32[128]{0:T(128)S(1)}, s32[128]{0:T(128)}, u32[]{:S(2)}) copy-start(s32[128]{0:T(128)} %param.9) | copy-start | bytes 1540
  0.6 31.2 %copy-start.6 = (s32[128,4]{0,1:T(4,128)S(1)}, s32[128,4]{0,1:T(4,128)}, u32[]{:S(2)}) copy-start(s32[128,4]{0,1:T(4,128)} %param.8) | copy-start | bytes 6148
  3.5 29.9 %collective-permute-start = (bf16[4,256,256]{2,1,0:T(8,128)(2,1)}, bf16[4,256,256]{2,1,0:T(8,128)(2,1)S(1)}, u32[]{:S(2)}, u32[]{:S(2)}) collective-permute-start(bf16[4,256,256]{2,1,0:T(8,128)(2,1)} %get-tuple-element.20), channel_id=1, source_target_pairs={{0,128},{128,256},{256,384},{384,0},{1,129},{129,257},{257,385},{3... | collective-permute-start | bytes 1572872 | tf_op jit(solution)/shard_map/ppermute | solution.py:249
  7.0 28.4 %collective-permute-start.1 = (bf16[4,256,256]{2,1,0:T(8,128)(2,1)}, bf16[4,256,256]{2,1,0:T(8,128)(2,1)S(1)}, u32[]{:S(2)}, u32[]{:S(2)}) collective-permute-start(bf16[4,256,256]{2,1,0:T(8,128)(2,1)} %get-tuple-element.20), channel_id=1, source_target_pairs={{0,256},{128,384},{256,0},{384,128},{1,257},{129,385},{257,1},{385... | collective-permute-start | bytes 1572872 | tf_op jit(solution)/shard_map/ppermute | solution.py:249
  11.8 26.0 %collective-permute-start.2 = (bf16[4,256,256]{2,1,0:T(8,128)(2,1)}, bf16[4,256,256]{2,1,0:T(8,128)(2,1)S(1)}, u32[]{:S(2)}, u32[]{:S(2)}) collective-permute-start(bf16[4,256,256]{2,1,0:T(8,128)(2,1)} %get-tuple-element.20), channel_id=1, source_target_pairs={{0,384},{128,0},{256,128},{384,256},{1,385},{129,1},{257,129},{385... | collective-permute-start | bytes 1572872 | tf_op jit(solution)/shard_map/ppermute | solution.py:249
  15.0 36.4 %all-to-all-start = ((bf16[64,8,256]{2,1,0:T(8,128)(2,1)}), bf16[64,8,256]{2,1,0:T(8,128)(2,1)S(1)}, u32[]{:S(2)}, u32[]{:S(2)}) async-start(bf16[64,8,256]{2,1,0:T(8,128)(2,1)} %get-tuple-element.18), calls=%async_computation | async-start | bytes 524288 | tf_op jit(solution)/shard_map/all_to_all | solution.py:252
  33.4 18.1 %collective-permute-start.3 = (bf16[4,256,256]{2,1,0:T(8,128)(2,1)S(1)}, bf16[4,256,256]{2,1,0:T(8,128)(2,1)S(1)}, u32[]{:S(2)}, u32[]{:S(2)}) collective-permute-start(bf16[4,256,256]{2,1,0:T(8,128)(2,1)S(1)} %collective-permute-done.w1_ref), channel_id=1, source_target_pairs={{0,1},{1,0},{2,3},{3,2},{4,5},{5,4},{6,7},{7,6},{8,9},{9,8},{10,11... | collective-permute-start | bytes 1572872 | tf_op jit(solution)/shard_map/ppermute | solution.py:253
  35.3 16.1 %collective-permute-start.4 = (bf16[4,256,256]{2,1,0:T(8,128)(2,1)S(1)}, bf16[4,256,256]{2,1,0:T(8,128)(2,1)}, u32[]{:S(2)}, u32[]{:S(2)}) collective-permute-start(bf16[4,256,256]{2,1,0:T(8,128)(2,1)S(1)} %collective-permute-done.1.w2_ref), channel_id=1, source_target_pairs={{0,1},{1,0},{2,3},{3,2},{4,5},{5,4},{6,7},{7,6},{8,9},{9,8},{10,11... | collective-permute-start | bytes 1572872 | tf_op jit(solution)/shard_map/ppermute | solution.py:253
  37.7 13.7 %copy-start.3 = (bf16[4,256,256]{2,1,0:T(8,128)(2,1)}, bf16[4,256,256]{2,1,0:T(8,128)(2,1)S(1)}, u32[]{:S(2)}) copy-start(bf16[4,256,256]{2,1,0:T(8,128)(2,1)S(1)} %collective-permute-done.2.w3_ref) | copy-start | bytes 1572868
  37.8 13.7 %collective-permute-start.5 = (bf16[4,256,256]{2,1,0:T(8,128)(2,1)S(1)}, bf16[4,256,256]{2,1,0:T(8,128)(2,1)}, u32[]{:S(2)}, u32[]{:S(2)}) collective-permute-start(bf16[4,256,256]{2,1,0:T(8,128)(2,1)S(1)} %collective-permute-done.2.w3_ref), channel_id=1, source_target_pairs={{0,1},{1,0},{2,3},{3,2},{4,5},{5,4},{6,7},{7,6},{8,9},{9,8},{10,11... | collective-permute-start | bytes 1572872 | tf_op jit(solution)/shard_map/ppermute | solution.py:253
  51.4 0.8 copy-start.4
  55.3 18.1 %all-to-all-start.1 = ((bf16[16,16,256]{2,1,0:T(8,128)(2,1)}), bf16[16,16,256]{2,1,0:T(8,128)(2,1)S(1)}, u32[]{:S(2)}, u32[]{:S(2)}) async-start(bf16[16,16,256]{2,1,0:T(8,128)(2,1)} %get-tuple-element.21), calls=%async_computation.1 | async-start | bytes 262144 | tf_op jit(solution)/shard_map/all_to_all | solution.py:336
  75.0 18.5 %all-to-all-start.2 = ((bf16[16,16,256]{2,1,0:T(8,128)(2,1)}), bf16[16,16,256]{2,1,0:T(8,128)(2,1)S(1)}, u32[]{:S(2)}, u32[]{:S(2)}) async-start(bf16[16,16,256]{2,1,0:T(8,128)(2,1)} %get-tuple-element.24), calls=%async_computation.2 | async-start | bytes 262144 | tf_op jit(solution)/shard_map/all_to_all | solution.py:340
  97.8 17.0 %all-to-all-start.3 = ((bf16[16,16,256]{2,1,0:T(8,128)(2,1)}), bf16[16,16,256]{2,1,0:T(8,128)(2,1)S(1)}, u32[]{:S(2)}, u32[]{:S(2)}) async-start(bf16[16,16,256]{2,1,0:T(8,128)(2,1)} %get-tuple-element.26), calls=%async_computation.3 | async-start | bytes 262144 | tf_op jit(solution)/shard_map/all_to_all | solution.py:347
  116.5 18.5 %all-to-all-start.4 = ((bf16[16,16,256]{2,1,0:T(8,128)(2,1)}), bf16[16,16,256]{2,1,0:T(8,128)(2,1)S(1)}, u32[]{:S(2)}, u32[]{:S(2)}) async-start(bf16[16,16,256]{2,1,0:T(8,128)(2,1)} %get-tuple-element.29), calls=%async_computation.4 | async-start | bytes 262144 | tf_op jit(solution)/shard_map/all_to_all | solution.py:354
  135.0 28.3 %copy-start = (bf16[2,256,256]{2,1,0:T(8,128)(2,1)S(1)}, bf16[2,256,256]{2,1,0:T(8,128)(2,1)}, u32[]{:S(2)}) copy-start(bf16[2,256,256]{2,1,0:T(8,128)(2,1)} %inv_ref.3) | copy-start | bytes 786436
  135.0 28.3 %copy-start.1 = (bf16[2,8,256]{2,1,0:T(8,128)(2,1)S(1)}, bf16[2,8,256]{2,1,0:T(8,128)(2,1)}, u32[]{:S(2)}) copy-start(bf16[2,8,256]{2,1,0:T(8,128)(2,1)} %probes_ref.3) | copy-start | bytes 24580
  135.0 28.3 %copy-start.2 = (bf16[2,8,256]{2,1,0:T(8,128)(2,1)S(1)}, bf16[2,8,256]{2,1,0:T(8,128)(2,1)}, u32[]{:S(2)}) copy-start(bf16[2,8,256]{2,1,0:T(8,128)(2,1)} %get-tuple-element.33.q_ref) | copy-start | bytes 24580
  138.9 24.3 %all-to-all-start.5 = ((bf16[64,8,128]{2,1,0:T(8,128)(2,1)}), bf16[64,8,128]{2,1,0:T(8,128)(2,1)S(1)}, u32[]{:S(2)}, u32[]{:S(2)}) async-start(bf16[64,8,128]{2,1,0:T(8,128)(2,1)} %get-tuple-element.32), calls=%async_computation.5 | async-start | bytes 262144 | tf_op jit(solution)/shard_map/all_to_all | solution.py:361
  148.5 10.4 %collective-permute-start.6 = (bf16[16,256]{1,0:T(8,128)(2,1)S(1)}, bf16[16,256]{1,0:T(8,128)(2,1)S(1)}, u32[]{:S(2)}, u32[]{:S(2)}) collective-permute-start(bf16[16,256]{1,0:T(8,128)(2,1)S(1)} %get-tuple-element.49), channel_id=1, source_target_pairs={{0,384},{128,0},{256,128},{384,256},{1,385},{129,1},{257,129},{385... | collective-permute-start | bytes 24584 | tf_op jit(solution)/shard_map/ppermute | solution.py:301
  153.4 7.1 %collective-permute-start.7 = (bf16[16,256]{1,0:T(8,128)(2,1)S(1)}, bf16[16,256]{1,0:T(8,128)(2,1)S(1)}, u32[]{:S(2)}, u32[]{:S(2)}) collective-permute-start(bf16[16,256]{1,0:T(8,128)(2,1)S(1)} %get-tuple-element.48), channel_id=1, source_target_pairs={{0,256},{128,384},{256,0},{384,128},{1,257},{129,385},{257,1},{385... | collective-permute-start | bytes 24584 | tf_op jit(solution)/shard_map/ppermute | solution.py:301
  156.0 6.8 %collective-permute-start.8 = (bf16[16,256]{1,0:T(8,128)(2,1)S(1)}, bf16[16,256]{1,0:T(8,128)(2,1)S(1)}, u32[]{:S(2)}, u32[]{:S(2)}) collective-permute-start(bf16[16,256]{1,0:T(8,128)(2,1)S(1)} %get-tuple-element.47), channel_id=1, source_target_pairs={{0,128},{128,256},{256,384},{384,0},{1,129},{129,257},{257,385},{3... | collective-permute-start | bytes 24584 | tf_op jit(solution)/shard_map/ppermute | solution.py:301

commit v4 on v3

--- a/solution.py
+++ b/solution.py
@@ -42,6 +42,19 @@
     if dims is None:
         return jnp.dot(a, b, preferred_element_type=F32)
     return lax.dot_general(a, b, dims, preferred_element_type=F32)
+
+
+def late(value):
+    whole = pl.BlockSpec(memory_space=pltpu.HBM)
+    return pl.pallas_call(
+        lambda value_ref, same_ref: None,
+        out_shape=shape(*value.shape),
+        in_specs=[whole],
+        out_specs=whole,
+        input_output_aliases={0: 0},
+        compiler_params=pltpu.CompilerParams(vmem_limit_bytes=52 * 2**20),
+        cost_estimate=pl.CostEstimate(flops=20000000000, bytes_accessed=2**20, transcendentals=0),
+    )(value)
 
 
 def start_kernel(core_ref, probes_ref, inv_ref, factor_ref, q_ref, msg_ref, w_ref, send_ref, p_ref, d_ref, l_ref, sems):
@@ -78,10 +91,7 @@
     waits = []
     for r in range(HELD):
         d, slot = r // LOCAL, r % LOCAL
-        if d == 0:
-            source = w_refs[0].at[slot]
-        else:
-            source = w_refs[slot * (Y - 1) + d]
+        source = w_refs[d].at[slot] if d < Y - 1 else w_refs[d + slot]
         copy = pltpu.make_async_copy(source, held_ref.at[r], sems.at[r])
 
         @pl.when(level_ref[r] == lev)
@@ -138,8 +148,8 @@
     near_ref[...] = dot(pick_ref[...], got).astype(BF16).reshape(near_ref.shape)
 
 
-def level1_kernel(level_ref, got_ref, pick_ref, w0_ref, w1_ref, w2_ref, w3_ref, w4_ref, w5_ref, w6_ref, msg_ref, solved_ref, q_ref, near_ref, held_ref, sems):
-    waits = load_rows(level_ref, 1, (w0_ref, w1_ref, w2_ref, w3_ref, w4_ref, w5_ref, w6_ref), held_ref, sems)
+def level1_kernel(level_ref, got_ref, pick_ref, w0_ref, w1_ref, w2_ref, w3_ref, w4_ref, msg_ref, solved_ref, q_ref, near_ref, held_ref, sems):
+    waits = load_rows(level_ref, 1, (w0_ref, w1_ref, w2_ref, w3_ref, w4_ref), held_ref, sems)
     got = got_ref[...].reshape(Y * Z * 4 * PAIR, BLOCK)
     near_ref[...] = dot(pick_ref[:WIDE], got)
     q_ref[...] = dot(pick_ref[WIDE : WIDE + HELD * PAD], got)
@@ -149,8 +159,8 @@
     broadcast_to_z(solved_ref[...].astype(BF16), msg_ref)
 
 
-def level2_kernel(level_ref, got_ref, pick_ref, w0_ref, w1_ref, w2_ref, w3_ref, w4_ref, w5_ref, w6_ref, q_ref, old_ref, msg_ref, solved_ref, near_ref, held_ref, sems):
-    waits = load_rows(level_ref, 2, (w0_ref, w1_ref, w2_ref, w3_ref, w4_ref, w5_ref, w6_ref), held_ref, sems)
+def level2_kernel(level_ref, got_ref, pick_ref, w0_ref, w1_ref, w2_ref, w3_ref, w4_ref, q_ref, old_ref, _a, _b, _c, _d, msg_ref, solved_ref, near_ref, held_ref, sems):
+    waits = load_rows(level_ref, 2, (w0_ref, w1_ref, w2_ref, w3_ref, w4_ref), held_ref, sems)
     near_ref[...] = dot(pick_ref[...], got_ref[...].reshape(Z * HELD * PAIR, BLOCK))
     solved_ref[...] = old_ref[...]
     forward_rows(level_ref, 2, waits, near_ref, q_ref, held_ref, solved_ref)
@@ -158,9 +168,9 @@
 
 
 def level3_kernel(
-    level_ref, got_ref, pick_ref, w0_ref, w1_ref, w2_ref, w3_ref, w4_ref, w5_ref, w6_ref, q_ref, old_ref, put_ref,
+    level_ref, got_ref, pick_ref, w0_ref, w1_ref, w2_ref, w3_ref, w4_ref, q_ref, old_ref, put_ref,
     msg_ref, solved_ref, terms_ref, near_ref, pad_ref, held_ref, sems):
-    waits = load_rows(level_ref, 3, (w0_ref, w1_ref, w2_ref, w3_ref, w4_ref, w5_ref, w6_ref), held_ref, sems)
+    waits = load_rows(level_ref, 3, (w0_ref, w1_ref, w2_ref, w3_ref, w4_ref), held_ref, sems)
     near_ref[...] = dot(pick_ref[...], got_ref[...].reshape(Z * HELD * PAIR, BLOCK))
     solved_ref[...] = old_ref[...]
     forward_rows(level_ref, 3, waits, near_ref, q_ref, held_ref, solved_ref)
@@ -181,9 +191,9 @@
 
 
 def back2_kernel(
-    level_ref, got_ref, w0_ref, w1_ref, w2_ref, w3_ref, w4_ref, w5_ref, w6_ref, old_ref, before_ref, put_ref,
+    level_ref, got_ref, w0_ref, w1_ref, w2_ref, w3_ref, w4_ref, old_ref, before_ref, put_ref,
     msg_ref, t_ref, sums_ref, terms_ref, pad_ref, held_ref, sems):
-    waits = load_rows(level_ref, 2, (w0_ref, w1_ref, w2_ref, w3_ref, w4_ref, w5_ref, w6_ref), held_ref, sems)
+    waits = load_rows(level_ref, 2, (w0_ref, w1_ref, w2_ref, w3_ref, w4_ref), held_ref, sems)
     finish_rows(level_ref, 2, got_ref, old_ref, t_ref)
     backward_rows(level_ref, 2, waits, t_ref, pad_ref, held_ref, terms_ref)
     sums_ref[...] = before_ref[...] + terms_ref[...]
@@ -192,8 +202,8 @@
 
 
 def back1_kernel(
-    level_ref, got_ref, w0_ref, w1_ref, w2_ref, w3_ref, w4_ref, w5_ref, w6_ref, old_ref, before_ref, put_ref, own_ref, msg_ref, t_ref, terms_ref, pad_ref, held_ref, sems):
-    waits = load_rows(level_ref, 1, (w0_ref, w1_ref, w2_ref, w3_ref, w4_ref, w5_ref, w6_ref), held_ref, sems)
+    level_ref, got_ref, w0_ref, w1_ref, w2_ref, w3_ref, w4_ref, old_ref, before_ref, put_ref, own_ref, msg_ref, t_ref, terms_ref, pad_ref, held_ref, sems):
+    waits = load_rows(level_ref, 1, (w0_ref, w1_ref, w2_ref, w3_ref, w4_ref), held_ref, sems)
     finish_rows(level_ref, 1, got_ref, old_ref, t_ref)
     backward_rows(level_ref, 1, waits, t_ref, pad_ref, held_ref, terms_ref)
     sums = before_ref[...] + terms_ref[...]
@@ -245,21 +255,24 @@
     q_own, msg, w_own, w_send = call(start_kernel, out, "shhh", scratch, room=60)(
         core, probes, inverses, factor
     )
-    def along(step):
-        return lax.ppermute(w_send, "y", [(i, (i + step) % Y) for i in range(Y)])
-
-    w_mine = [along(step) for step in (1, 2, 3)]
+    ring = [(2 * i, 2 * ((i + 1) % Y)) for i in range(Y)]
+    ring += [(2 * i + 1, 2 * ((i - 1) % Y) + 1) for i in range(Y)]
+    w_near = lax.ppermute(w_own, ("y", "c"), ring)
+    w_far = lax.ppermute(w_send, "y", [(i, (i + 2) % Y) for i in range(Y)])
     got = lax.all_to_all(msg, ROWS, 0, 0, tiled=True)
-    w_other = [lax.ppermute(v, "c", [(0, 1), (1, 0)]) for v in w_mine]
-    ws = [w_own, *w_mine, *w_other]
+    swap = [(0, 1), (1, 0)]
+    ws = [w_own, w_near, late(lax.ppermute(w_near, "c", swap)), w_far, lax.ppermute(w_far, "c", swap)]
 
     def rows_of(slots):
         return jnp.sum(jnp.where(owner[None, :] == slots[:, None], iota[None, :], 0), axis=1)
 
     local_iota = jnp.arange(LOCAL, dtype=jnp.int32)
-    held_y = (my - jnp.arange(Y, dtype=jnp.int32)) % Y
+    way = 1 - 2 * lax.axis_index("c")
+    held_y = (my + way * jnp.array([0, -1, 1, 2], jnp.int32)) % Y
+    held_flip = jnp.array([0, 0, 1, 0], jnp.int32)
     core = lax.axis_index("c")
-    slots = (LOCAL * (held_y * Z + mz))[:, None] + (core + local_iota[None, :]) % LOCAL
+    flip = core + held_flip[:, None] + local_iota[None, :]
+    slots = (LOCAL * (held_y * Z + mz))[:, None] + flip % LOCAL
     slots = slots.reshape(-1)
     rows = rows_of(slots)
     level = rows // width
@@ -269,8 +282,9 @@
     src = jnp.where(cols >= 0, src, -1).reshape(-1)
     dev = src // LOCAL
     bad = -(2**20)
-    turn = (my - dev // Z) % Y
-    place_z = jnp.where(src >= 0, (dev % Z) * HELD + turn * LOCAL + (src - core) % LOCAL, bad)
+    turn = (way * (dev // Z - my)) % Y
+    turn = jnp.where(turn == 3, 1, jnp.where(turn == 0, 0, turn + 1))
+    place_z = jnp.where(src >= 0, (dev % Z) * HELD + turn * LOCAL + (src - core - (turn == 2)) % LOCAL, bad)
 
     def rows_at(place, pad, stride=PAIR):
         col = jnp.arange(pad, dtype=jnp.int32)
@@ -283,7 +297,7 @@
     def first_at(slot, kind):
         return jnp.where(slot >= 0, (slot // LOCAL) * 4 + kind * LOCAL + slot % LOCAL, bad)
 
-    natural = (held_y[:, None] * Z + mz) * LOCAL + local_iota[None, :]
+    natural = (((my - jnp.arange(Y, dtype=jnp.int32)) % Y)[:, None] * Z + mz) * LOCAL + local_iota[None, :]
     nat_rows = rows_of(natural.reshape(-1))
     nat_cols = jnp.sum(jnp.where(nat_rows[:, None, None] == iota[None, :, None], pattern[None], 0), axis=1)
     nat_src = jnp.sum(jnp.where(nat_cols[..., None] == iota, owner, 0), axis=-1)
@@ -331,31 +345,31 @@
     sums = shape(WIDE, BLOCK, dtype=F32)
     out = (msg_z, held, shape(HELD * PAD, BLOCK, dtype=F32))
     msg, solved, q = call(
-        level1_kernel, out, "svv" + "h" * 7, [near_scratch] + held_scratch
+        level1_kernel, out, "svv" + "h" * 5, [near_scratch] + held_scratch
     )(level, got, pick1, *ws)
     got = lax.all_to_all(msg, "z", 0, 0, tiled=True)
     msg, solved = call(
-        level2_kernel, (msg_z, held), "svv" + "h" * 7 + "vv", [near_scratch] + held_scratch
-    )(level, got, pick_z, *ws, q, solved)
+        level2_kernel, (msg_z, held), "svv" + "h" * 5 + "vvhhhh", [near_scratch] + held_scratch
+    )(level, got, pick_z, *ws, q, solved, put_z, put_last, own_last, pick_p)
     got = lax.all_to_all(msg, "z", 0, 0, tiled=True)
     msg, solved, before = call(
         level3_kernel,
         (msg_z, held, sums),
-        "svv" + "h" * 7 + "vvv",
+        "svv" + "h" * 5 + "vvv",
         [near_scratch, pad_scratch] + held_scratch,
     )(level, got, pick_z, *ws, q, solved, put_z)
     got = lax.all_to_all(msg, "z", 0, 0, tiled=True)
     msg, t, before = call(
         back2_kernel,
         (msg_z, held, sums),
-        "sv" + "h" * 7 + "vvv",
+        "sv" + "h" * 5 + "vvv",
         [near_scratch, pad_scratch] + held_scratch,
     )(level, got, *ws, solved, before, put_z)
     got = lax.all_to_all(msg, "z", 0, 0, tiled=True)
     msg, t = call(
         back1_kernel,
         (shape(Y * Z, 2 * group, BLOCK // 2), held),
-        "sv" + "h" * 7 + "vvvv",
+        "sv" + "h" * 5 + "vvvv",
         [near_scratch, pad_scratch] + held_scratch,
     )(level, got, *ws, t, before, put_last, own_last)
     got = lax.all_to_all(msg, ROWS, 0, 0, tiled=True)

time: 167 us -> 167 us (level)
  blocking collectives: 0 us -> 35.3 us
  waiting for transfers between devices: 66.9 us -> 43.1 us
  starting transfers between devices: 72.7 us -> 60.6 us
    all_to_all x0 -> x2, blocking collectives: none -> 35.3 us  [body(): got = lax.all_to_all(msg, 'z', 0, 0, tiled=True)]
    all_to_all x4 -> x2, waiting for transfers between devices: 51 us -> 27.1 us  [body(): got = lax.all_to_all(msg, 'z', 0, 0, tiled=True)]
    all_to_all x4 -> x2, starting transfers between devices: 19.1 us -> 10.1 us  [body(): got = lax.all_to_all(msg, 'z', 0, 0, tiled=True)]
    ppermute x6 -> x4, starting transfers between devices: 17.8 us -> 12.6 us  [the longest x1 4.81 us: body(): w_far = lax.ppermute(w_send, 'y', [(i, (i + 2) % Y) for i in range(Y)])]
    all_to_all x2, starting transfers between devices: 25.4 us -> 27.6 us  [body(): got = lax.all_to_all(msg, ROWS, 0, 0, tiled=True)]
    pallas_call x4 -> x5, Pallas kernels: 10.6 us -> 10.9 us  [the longest x1 3.68 us: body(): call(level3_kernel, (msg_z, held, sums), 'svv' + 'h' * 5 + 'vvv', [near_s...]
  transfers between devices with their start and end apart: 15 -> 11, of which waited for: 8 -> 6; matrix products, arithmetic and copies ran while one was open for 3% -> 3% of each run, Pallas kernels for 0% -> 0%
where the time goes in v4:
time: 167 us; the launch traced here: 166 us
  starting transfers between devices  60.6 us (36%)
  waiting for transfers between devices  43.1 us (26%)
  blocking collectives  35.3 us (21%)
  Pallas kernels  20.2 us (12%)
  other arithmetic  3.32 us (2%)
  local copies, waits for them, and re-layouts  2.64 us (2%)
    all_to_all x2, blocking collectives, body(): got = lax.all_to_all(msg, 'z', 0, 0, tiled=True)  35.3 us
    all_to_all x2, starting transfers between devices, body(): got = lax.all_to_all(msg, ROWS, 0, 0, tiled=True)  27.6 us
    all_to_all x2, waiting for transfers between devices, body(): got = lax.all_to_all(msg, 'z', 0, 0, tiled=True)  27.1 us
    all_to_all x2, waiting for transfers between devices, body(): got = lax.all_to_all(msg, ROWS, 0, 0, tiled=True)  12.2 us
    ppermute x3, starting transfers between devices, body(): lax.ppermute(near_p[d], 'y', [(i, (i - d) % Y) for i in range(Y)])  10.3 us
    all_to_all x2, starting transfers between devices, body(): got = lax.all_to_all(msg, 'z', 0, 0, tiled=True)  10.1 us
    ppermute x1, starting transfers between devices, body(): w_far = lax.ppermute(w_send, 'y', [(i, (i + 2) % Y) for i in range(Y)])  4.81 us
    ppermute x3, waiting for transfers between devices, body(): lax.ppermute(near_p[d], 'y', [(i, (i - d) % Y) for i in range(Y)])  3.87 us
  transfers between devices with their start and end apart: 11, of which 6 were waited for; matrix products, arithmetic and copies ran while one was open for 3% of the time, Pallas kernels for 0%

profile of v4, /device:TPU:6, one launch (start us, length us, event | category | flops | bytes accessed | tf_op | source)
XLA Modules:
  0.0 166.2 jit_solution(15144152597615921428)
XLA Ops:
  0.7 2.8 %shard_map.86 = (bf16[2,8,256]{2,1,0:T(8,128)(2,1)}, bf16[64,8,256]{2,1,0:T(8,128)(2,1)}, bf16[2,4,256,256]{3,2,1,0:T(8,128)(2,1)}, bf16[4,256,256]{2,1,0:T(8,128)(2,1)}) custom-call(s32[1]{0:T(128)} %bitcast.core_ref, bf16[2,8,256]{2,1,0:T(8,128)(2,1)} %probes_ref.3, bf16[2,256,256]{2,1,0:T(8,128)(2,1)} %inv_ref.3, bf16[2,4,256,256]{3,2,1,0:T(8,128)(2,1)} %factor_ref.1), custom_call_target="tpu_custom_call" | custom-call | tf_op jit(solution)/shard_map/pallas_call | solution.py:255
  3.5 3.5 %collective-permute-start = (bf16[2,4,256,256]{3,2,1,0:T(8,128)(2,1)}, bf16[2,4,256,256]{3,2,1,0:T(8,128)(2,1)}, u32[]{:S(2)}, u32[]{:S(2)}) collective-permute-start(bf16[2,4,256,256]{3,2,1,0:T(8,128)(2,1)} %get-tuple-element.19.w0_ref), channel_id=1, source_target_pairs={{0,128},{128,256},{256,384},{384,0},{1,385},{129,1},{257,129},{385... | collective-permute-start | bytes 3145736 | tf_op jit(solution)/shard_map/ppermute | solution.py:260
  7.0 4.8 %collective-permute-start.2 = (bf16[4,256,256]{2,1,0:T(8,128)(2,1)}, bf16[4,256,256]{2,1,0:T(8,128)(2,1)S(1)}, u32[]{:S(2)}, u32[]{:S(2)}) collective-permute-start(bf16[4,256,256]{2,1,0:T(8,128)(2,1)} %get-tuple-element.20), channel_id=1, source_target_pairs={{0,256},{128,384},{256,0},{384,128},{1,257},{129,385},{257,1},{385... | collective-permute-start | bytes 1572872 | tf_op jit(solution)/shard_map/ppermute | solution.py:261
  11.8 16.9 %all-to-all-start = ((bf16[64,8,256]{2,1,0:T(8,128)(2,1)}), bf16[64,8,256]{2,1,0:T(8,128)(2,1)S(1)}, u32[]{:S(2)}, u32[]{:S(2)}) async-start(bf16[64,8,256]{2,1,0:T(8,128)(2,1)} %get-tuple-element.18), calls=%async_computation | async-start | bytes 524288 | tf_op jit(solution)/shard_map/all_to_all | solution.py:262
  28.8 0.1 add.460
  28.9 0.1 iota_add_fusion.1
  29.0 0.1 add.466
  29.2 0.1 add.502
  29.3 0.2 select_reduce_fusion.4
  29.5 0.1 iota_compare_fusion.12
  29.6 0.1 iota_compare_fusion.11
  29.7 0.2 select_reduce_fusion.1
  29.9 0.1 copy.14
  30.0 0.3 select_reduce_fusion
  30.3 0.1 copy.15
  30.3 0.1 reduce_sum.72
  30.4 0.1 reduce_sum.70
  30.6 0.1 add_select_fusion.1
  30.7 0.1 select_n.378
  30.8 0.1 copy.17
  30.8 0.1 select_n.387
  31.0 0.1 add_select_fusion.4
  31.0 0.1 select_n.381
  31.1 0.1 add_select_fusion.5
  31.2 0.1 iota_compare_fusion.2
  31.3 0.1 iota_compare_fusion.1
  31.4 2.1 %collective-permute-start.1 = (bf16[2,4,256,256]{3,2,1,0:T(8,128)(2,1)}, bf16[2,4,256,256]{3,2,1,0:T(8,128)(2,1)S(1)}, u32[]{:S(2)}, u32[]{:S(2)}) collective-permute-start(bf16[2,4,256,256]{3,2,1,0:T(8,128)(2,1)} %collective-permute-done.w1_ref), channel_id=1, source_target_pairs={{0,1},{1,0},{2,3},{3,2},{4,5},{5,4},{6,7},{7,6},{8,9},{9,8},{10,11... | collective-permute-start | bytes 3145736 | tf_op jit(solution)/shard_map/ppermute | solution.py:264
  33.5 0.9 add_convert_fusion._b.put_ref
  34.4 0.1 select_n.359
  34.5 0.1 select_n.364
  34.5 0.1 iota_compare_fusion.7
  34.6 0.1 iota_compare_fusion.6
  34.7 0.1 add_select_fusion
  34.8 0.1 fusion.pick_ref
  34.9 2.2 %collective-permute-start.3 = (bf16[4,256,256]{2,1,0:T(8,128)(2,1)S(1)}, bf16[4,256,256]{2,1,0:T(8,128)(2,1)S(1)}, u32[]{:S(2)}, u32[]{:S(2)}) collective-permute-start(bf16[4,256,256]{2,1,0:T(8,128)(2,1)S(1)} %collective-permute-done.2.w3_ref), channel_id=1, source_target_pairs={{0,1},{1,0},{2,3},{3,2},{4,5},{5,4},{6,7},{7,6},{8,9},{9,8},{10,11... | collective-permute-start | bytes 1572872 | tf_op jit(solution)/shard_map/ppermute | solution.py:264
  37.2 1.0 copy-done
  38.2 11.7 %all-to-all-done.got_ref = bf16[64,8,256]{2,1,0:T(8,128)(2,1)S(1)} async-done(((bf16[64,8,256]{2,1,0:T(8,128)(2,1)}), bf16[64,8,256]{2,1,0:T(8,128)(2,1)S(1)}, u32[]{:S(2)}, u32[]{:S(2)}) %all-to-all-start) | async-done | bytes 262176 | tf_op jit(solution)/shard_map/all_to_all | solution.py:262
  49.8 2.6 %shard_map.88 = (bf16[16,16,256]{2,1,0:T(8,128)(2,1)}, f32[16,256]{1,0:T(8,128)S(1)}, f32[64,256]{1,0:T(8,128)S(1)}) custom-call(s32[8]{0:T(128)S(1)} %get-tuple-element.42.level_ref, bf16[64,8,256]{2,1,0:T(8,128)(2,1)S(1)} %all-to-all-done.got_ref, bf16[320,512]{1,0:T(8,128)(2,1)S(1)} %fusion.pick_ref, bf16[2,4,256,256]{3,2,1,0:T(8,128)(2,1)} %get-tuple-element.19.w0_ref, ...), custom_call_target="tpu_custom_call" | custom-call | tf_op jit(solution)/shard_map/pallas_call | solution.py:347
  52.4 5.7 %all-to-all-start.1 = ((bf16[16,16,256]{2,1,0:T(8,128)(2,1)}), bf16[16,16,256]{2,1,0:T(8,128)(2,1)S(1)}, u32[]{:S(2)}, u32[]{:S(2)}) async-start(bf16[16,16,256]{2,1,0:T(8,128)(2,1)} %get-tuple-element.21), calls=%async_computation.1 | async-start | bytes 262144 | tf_op jit(solution)/shard_map/all_to_all | solution.py:350
  58.2 0.1 select_n.373
  58.3 0.1 select_n.392
  58.4 0.3 copy.16
  58.7 0.1 fusion.3._d.pick_ref
  58.8 0.1 fusion.2
  58.9 14.0 %all-to-all-done.1.got_ref = bf16[16,16,256]{2,1,0:T(8,128)(2,1)S(1)} async-done(((bf16[16,16,256]{2,1,0:T(8,128)(2,1)}), bf16[16,16,256]{2,1,0:T(8,128)(2,1)S(1)}, u32[]{:S(2)}, u32[]{:S(2)}) %all-to-all-start.1) | async-done | bytes 131104 | tf_op jit(solution)/shard_map/all_to_all | solution.py:350
  72.9 1.9 %shard_map.89 = (bf16[16,16,256]{2,1,0:T(8,128)(2,1)S(1)}, f32[16,256]{1,0:T(8,128)S(1)}) custom-call(s32[8]{0:T(128)S(1)} %get-tuple-element.42.level_ref, bf16[16,16,256]{2,1,0:T(8,128)(2,1)S(1)} %all-to-all-done.1.got_ref, bf16[256,256]{1,0:T(8,128)(2,1)S(1)} %get-tuple-element.52.pick_ref, bf16[2,4,256,256]{3,2,1,0:T(8,128)(2,1)} %get-tuple-element.19.w0_ref, ...), custom_call_target="tpu_custom_call" | custom-call | tf_op jit(solution)/shard_map/pallas_call | solution.py:351
  74.9 18.4 %all_to_all.30.got_ref = bf16[16,16,256]{2,1,0:T(8,128)(2,1)S(1)} all-to-all(bf16[16,16,256]{2,1,0:T(8,128)(2,1)S(1)} %get-tuple-element.24), channel_id=1, replica_groups=mesh['y'=4,'z'=16,'x'=4,'c'=2] {'z'}, dimensions={0} | all-to-all | bytes 262144 | tf_op jit(solution)/shard_map/all_to_all | solution.py:354
  93.3 3.7 %shard_map.90 = (bf16[16,16,256]{2,1,0:T(8,128)(2,1)S(1)}, f32[16,256]{1,0:T(8,128)S(1)}, f32[256,256]{1,0:T(8,128)S(1)}) custom-call(s32[8]{0:T(128)S(1)} %get-tuple-element.42.level_ref, bf16[16,16,256]{2,1,0:T(8,128)(2,1)S(1)} %all_to_all.30.got_ref, bf16[256,256]{1,0:T(8,128)(2,1)S(1)} %get-tuple-element.52.pick_ref, ...), custom_call_target="tpu_custom_call" | custom-call | tf_op jit(solution)/shard_map/pallas_call | solution.py:355
  97.0 16.9 %all_to_all.31.got_ref = bf16[16,16,256]{2,1,0:T(8,128)(2,1)S(1)} all-to-all(bf16[16,16,256]{2,1,0:T(8,128)(2,1)S(1)} %get-tuple-element.26), channel_id=1, replica_groups=mesh['y'=4,'z'=16,'x'=4,'c'=2] {'z'}, dimensions={0} | all-to-all | bytes 262144 | tf_op jit(solution)/shard_map/all_to_all | solution.py:361
  113.9 2.7 %shard_map.91 = (bf16[16,16,256]{2,1,0:T(8,128)(2,1)}, f32[16,256]{1,0:T(8,128)S(1)}, f32[256,256]{1,0:T(8,128)S(1)}) custom-call(s32[8]{0:T(128)S(1)} %get-tuple-element.42.level_ref, bf16[16,16,256]{2,1,0:T(8,128)(2,1)S(1)} %all_to_all.31.got_ref, bf16[2,4,256,256]{3,2,1,0:T(8,128)(2,1)} %get-tuple-element.19.w0_ref, ...), custom_call_target="tpu_custom_call" | custom-call | tf_op jit(solution)/shard_map/pallas_call | solution.py:362
  116.6 4.3 %all-to-all-start.4 = ((bf16[16,16,256]{2,1,0:T(8,128)(2,1)}), bf16[16,16,256]{2,1,0:T(8,128)(2,1)S(1)}, u32[]{:S(2)}, u32[]{:S(2)}) async-start(bf16[16,16,256]{2,1,0:T(8,128)(2,1)} %get-tuple-element.29), calls=%async_computation.4 | async-start | bytes 262144 | tf_op jit(solution)/shard_map/all_to_all | solution.py:368
  121.0 0.1 fusion.4.turn_ref
  121.0 13.0 %all-to-all-done.4.got_ref = bf16[16,16,256]{2,1,0:T(8,128)(2,1)S(1)} async-done(((bf16[16,16,256]{2,1,0:T(8,128)(2,1)}), bf16[16,16,256]{2,1,0:T(8,128)(2,1)S(1)}, u32[]{:S(2)}, u32[]{:S(2)}) %all-to-all-start.4) | async-done | bytes 131104 | tf_op jit(solution)/shard_map/all_to_all | solution.py:368
  134.1 3.5 %shard_map.92 = (bf16[64,8,128]{2,1,0:T(8,128)(2,1)}, f32[16,256]{1,0:T(8,128)}) custom-call(s32[8]{0:T(128)S(1)} %get-tuple-element.42.level_ref, bf16[16,16,256]{2,1,0:T(8,128)(2,1)S(1)} %all-to-all-done.4.got_ref, bf16[2,4,256,256]{3,2,1,0:T(8,128)(2,1)} %get-tuple-element.19.w0_ref, bf16[2,4,256,256]{3,2,1,0:T(8,128)(2,1)} %collective-permute-done.w1_ref, ...), custom_call_target="tpu_custom_call" | custom-call | tf_op jit(solution)/shard_map/pallas_call | solution.py:369
  137.6 10.7 %all-to-all-start.5 = ((bf16[64,8,128]{2,1,0:T(8,128)(2,1)}), bf16[64,8,128]{2,1,0:T(8,128)(2,1)S(1)}, u32[]{:S(2)}, u32[]{:S(2)}) async-start(bf16[64,8,128]{2,1,0:T(8,128)(2,1)} %get-tuple-element.32), calls=%async_computation.5 | async-start | bytes 262144 | tf_op jit(solution)/shard_map/all_to_all | solution.py:375
  148.3 0.2 fusion.5
  148.5 0.2 shard_map.93
  148.7 4.9 %collective-permute-start.4 = (bf16[16,256]{1,0:T(8,128)(2,1)S(1)}, bf16[16,256]{1,0:T(8,128)(2,1)S(1)}, u32[]{:S(2)}, u32[]{:S(2)}) collective-permute-start(bf16[16,256]{1,0:T(8,128)(2,1)S(1)} %get-tuple-element.49), channel_id=1, source_target_pairs={{0,384},{128,0},{256,128},{384,256},{1,385},{129,1},{257,129},{385... | collective-permute-start | bytes 24584 | tf_op jit(solution)/shard_map/ppermute | solution.py:315
  153.6 2.6 %collective-permute-start.5 = (bf16[16,256]{1,0:T(8,128)(2,1)S(1)}, bf16[16,256]{1,0:T(8,128)(2,1)S(1)}, u32[]{:S(2)}, u32[]{:S(2)}) collective-permute-start(bf16[16,256]{1,0:T(8,128)(2,1)S(1)} %get-tuple-element.48), channel_id=1, source_target_pairs={{0,256},{128,384},{256,0},{384,128},{1,257},{129,385},{257,1},{385... | collective-permute-start | bytes 24584 | tf_op jit(solution)/shard_map/ppermute | solution.py:315
  156.2 2.9 %collective-permute-start.6 = (bf16[16,256]{1,0:T(8,128)(2,1)S(1)}, bf16[16,256]{1,0:T(8,128)(2,1)S(1)}, u32[]{:S(2)}, u32[]{:S(2)}) collective-permute-start(bf16[16,256]{1,0:T(8,128)(2,1)S(1)} %get-tuple-element.47), channel_id=1, source_target_pairs={{0,128},{128,256},{256,384},{384,0},{1,129},{129,257},{257,385},{3... | collective-permute-start | bytes 24584 | tf_op jit(solution)/shard_map/ppermute | solution.py:315
  159.0 1.6 collective-permute-done.5.near2_ref
  160.7 2.3 %collective-permute-done.6.near3_ref = bf16[16,256]{1,0:T(8,128)(2,1)S(1)} collective-permute-done((bf16[16,256]{1,0:T(8,128)(2,1)S(1)}, bf16[16,256]{1,0:T(8,128)(2,1)S(1)}, u32[]{:S(2)}, u32[]{:S(2)}) %collective-permute-start.6) | collective-permute-done | bytes 8224 | tf_op jit(solution)/shard_map/ppermute | solution.py:315
  162.9 0.5 all-to-all-done.5.got_ref
  163.4 2.8 %shard_map.94 = (bf16[2,8,256]{2,1,0:T(8,128)(2,1)}, bf16[2,5,256,256]{3,2,1,0:T(8,128)(2,1)}) custom-call(s32[2]{0:T(128)S(1)} %compare_convert_fusion.1.first_ref, bf16[64,8,128]{2,1,0:T(8,128)(2,1)S(1)} %all-to-all-done.5.got_ref, bf16[2,8,256]{2,1,0:T(8,128)(2,1)S(1)} %copy-done.3, bf16[2,8,256]{2,1,0:T(8,128)(2,1)S(1)} %copy-done.2, ...), custom_call_target="tpu_custom_call" | custom-call | tf_op jit(solution)/shard_map/pallas_call | solution.py:381
  (43 shorter events, 0.4 us)
Async XLA Ops:
  0.6 28.1 %copy-start.6 = (s32[4]{0:T(128)S(1)}, s32[4]{0:T(128)}, u32[]{:S(2)}) copy-start(s32[4]{0:T(128)} %constant.199.clone) | copy-start | bytes 52
  0.6 28.3 %copy-start.7 = (s32[4]{0:T(128)S(1)}, s32[4]{0:T(128)}, u32[]{:S(2)}) copy-start(s32[4]{0:T(128)} %constant.200.clone) | copy-start | bytes 52
  0.7 28.6 %copy-start.4 = (s32[128]{0:T(128)S(1)}, s32[128]{0:T(128)}, u32[]{:S(2)}) copy-start(s32[128]{0:T(128)} %param.11) | copy-start | bytes 1540
  0.7 29.0 %copy-start.5 = (s32[128,4]{0,1:T(4,128)S(1)}, s32[128,4]{0,1:T(4,128)}, u32[]{:S(2)}) copy-start(s32[128,4]{0,1:T(4,128)} %param.10) | copy-start | bytes 6148
  3.5 27.9 %collective-permute-start = (bf16[2,4,256,256]{3,2,1,0:T(8,128)(2,1)}, bf16[2,4,256,256]{3,2,1,0:T(8,128)(2,1)}, u32[]{:S(2)}, u32[]{:S(2)}) collective-permute-start(bf16[2,4,256,256]{3,2,1,0:T(8,128)(2,1)} %get-tuple-element.19.w0_ref), channel_id=1, source_target_pairs={{0,128},{128,256},{256,384},{384,0},{1,385},{129,1},{257,129},{385... | collective-permute-start | bytes 3145736 | tf_op jit(solution)/shard_map/ppermute | solution.py:260
  7.0 27.9 %collective-permute-start.2 = (bf16[4,256,256]{2,1,0:T(8,128)(2,1)}, bf16[4,256,256]{2,1,0:T(8,128)(2,1)S(1)}, u32[]{:S(2)}, u32[]{:S(2)}) collective-permute-start(bf16[4,256,256]{2,1,0:T(8,128)(2,1)} %get-tuple-element.20), channel_id=1, source_target_pairs={{0,256},{128,384},{256,0},{384,128},{1,257},{129,385},{257,1},{385... | collective-permute-start | bytes 1572872 | tf_op jit(solution)/shard_map/ppermute | solution.py:261
  11.8 38.0 %all-to-all-start = ((bf16[64,8,256]{2,1,0:T(8,128)(2,1)}), bf16[64,8,256]{2,1,0:T(8,128)(2,1)S(1)}, u32[]{:S(2)}, u32[]{:S(2)}) async-start(bf16[64,8,256]{2,1,0:T(8,128)(2,1)} %get-tuple-element.18), calls=%async_computation | async-start | bytes 524288 | tf_op jit(solution)/shard_map/all_to_all | solution.py:262
  31.4 5.8 %collective-permute-start.1 = (bf16[2,4,256,256]{3,2,1,0:T(8,128)(2,1)}, bf16[2,4,256,256]{3,2,1,0:T(8,128)(2,1)S(1)}, u32[]{:S(2)}, u32[]{:S(2)}) collective-permute-start(bf16[2,4,256,256]{3,2,1,0:T(8,128)(2,1)} %collective-permute-done.w1_ref), channel_id=1, source_target_pairs={{0,1},{1,0},{2,3},{3,2},{4,5},{5,4},{6,7},{7,6},{8,9},{9,8},{10,11... | collective-permute-start | bytes 3145736 | tf_op jit(solution)/shard_map/ppermute | solution.py:264
  34.9 14.9 %collective-permute-start.3 = (bf16[4,256,256]{2,1,0:T(8,128)(2,1)S(1)}, bf16[4,256,256]{2,1,0:T(8,128)(2,1)S(1)}, u32[]{:S(2)}, u32[]{:S(2)}) collective-permute-start(bf16[4,256,256]{2,1,0:T(8,128)(2,1)S(1)} %collective-permute-done.2.w3_ref), channel_id=1, source_target_pairs={{0,1},{1,0},{2,3},{3,2},{4,5},{5,4},{6,7},{7,6},{8,9},{9,8},{10,11... | collective-permute-start | bytes 1572872 | tf_op jit(solution)/shard_map/ppermute | solution.py:264
  37.2 1.0 copy-start
  52.4 20.5 %all-to-all-start.1 = ((bf16[16,16,256]{2,1,0:T(8,128)(2,1)}), bf16[16,16,256]{2,1,0:T(8,128)(2,1)S(1)}, u32[]{:S(2)}, u32[]{:S(2)}) async-start(bf16[16,16,256]{2,1,0:T(8,128)(2,1)} %get-tuple-element.21), calls=%async_computation.1 | async-start | bytes 262144 | tf_op jit(solution)/shard_map/all_to_all | solution.py:350
  116.6 17.4 %all-to-all-start.4 = ((bf16[16,16,256]{2,1,0:T(8,128)(2,1)}), bf16[16,16,256]{2,1,0:T(8,128)(2,1)S(1)}, u32[]{:S(2)}, u32[]{:S(2)}) async-start(bf16[16,16,256]{2,1,0:T(8,128)(2,1)} %get-tuple-element.29), calls=%async_computation.4 | async-start | bytes 262144 | tf_op jit(solution)/shard_map/all_to_all | solution.py:368
  134.1 29.4 %copy-start.1 = (bf16[2,256,256]{2,1,0:T(8,128)(2,1)S(1)}, bf16[2,256,256]{2,1,0:T(8,128)(2,1)}, u32[]{:S(2)}) copy-start(bf16[2,256,256]{2,1,0:T(8,128)(2,1)} %inv_ref.3) | copy-start | bytes 786436
  134.1 29.4 %copy-start.2 = (bf16[2,8,256]{2,1,0:T(8,128)(2,1)S(1)}, bf16[2,8,256]{2,1,0:T(8,128)(2,1)}, u32[]{:S(2)}) copy-start(bf16[2,8,256]{2,1,0:T(8,128)(2,1)} %probes_ref.3) | copy-start | bytes 24580
  134.1 29.4 %copy-start.3 = (bf16[2,8,256]{2,1,0:T(8,128)(2,1)S(1)}, bf16[2,8,256]{2,1,0:T(8,128)(2,1)}, u32[]{:S(2)}) copy-start(bf16[2,8,256]{2,1,0:T(8,128)(2,1)} %get-tuple-element.33.q_ref) | copy-start | bytes 24580
  137.6 25.8 %all-to-all-start.5 = ((bf16[64,8,128]{2,1,0:T(8,128)(2,1)}), bf16[64,8,128]{2,1,0:T(8,128)(2,1)S(1)}, u32[]{:S(2)}, u32[]{:S(2)}) async-start(bf16[64,8,128]{2,1,0:T(8,128)(2,1)} %get-tuple-element.32), calls=%async_computation.5 | async-start | bytes 262144 | tf_op jit(solution)/shard_map/all_to_all | solution.py:375
  148.7 10.4 %collective-permute-start.4 = (bf16[16,256]{1,0:T(8,128)(2,1)S(1)}, bf16[16,256]{1,0:T(8,128)(2,1)S(1)}, u32[]{:S(2)}, u32[]{:S(2)}) collective-permute-start(bf16[16,256]{1,0:T(8,128)(2,1)S(1)} %get-tuple-element.49), channel_id=1, source_target_pairs={{0,384},{128,0},{256,128},{384,256},{1,385},{129,1},{257,129},{385... | collective-permute-start | bytes 24584 | tf_op jit(solution)/shard_map/ppermute | solution.py:315
  153.6 7.1 %collective-permute-start.5 = (bf16[16,256]{1,0:T(8,128)(2,1)S(1)}, bf16[16,256]{1,0:T(8,128)(2,1)S(1)}, u32[]{:S(2)}, u32[]{:S(2)}) collective-permute-start(bf16[16,256]{1,0:T(8,128)(2,1)S(1)} %get-tuple-element.48), channel_id=1, source_target_pairs={{0,256},{128,384},{256,0},{384,128},{1,257},{129,385},{257,1},{385... | collective-permute-start | bytes 24584 | tf_op jit(solution)/shard_map/ppermute | solution.py:315
  156.2 6.8 %collective-permute-start.6 = (bf16[16,256]{1,0:T(8,128)(2,1)S(1)}, bf16[16,256]{1,0:T(8,128)(2,1)S(1)}, u32[]{:S(2)}, u32[]{:S(2)}) collective-permute-start(bf16[16,256]{1,0:T(8,128)(2,1)S(1)} %get-tuple-element.47), channel_id=1, source_target_pairs={{0,128},{128,256},{256,384},{384,0},{1,129},{129,257},{257,385},{3... | collective-permute-start | bytes 24584 | tf_op jit(solution)/shard_map/ppermute | solution.py:315

commit v5 on v4

--- a/solution.py
+++ b/solution.py
@@ -143,9 +143,9 @@
         msg_ref[z] = value
 
 
-def neighbour_kernel(got_ref, pick_ref, near_ref):
+def neighbour_kernel(got_ref, pick_ref, _, near_ref):
     got = got_ref[...].reshape(Y * Z * 4 * PAIR, BLOCK)
-    near_ref[...] = dot(pick_ref[...], got).astype(BF16).reshape(near_ref.shape)
+    near_ref[...] = dot(pick_ref[...], got).astype(BF16)
 
 
 def level1_kernel(level_ref, got_ref, pick_ref, w0_ref, w1_ref, w2_ref, w3_ref, w4_ref, msg_ref, solved_ref, q_ref, near_ref, held_ref, sems):
@@ -310,10 +310,15 @@
     )
     pick1 = hot(pick1, Y * Z * 4 * PAIR)
     pick_p = hot(rows_at(first_at(nat_src, 1), PAIR), Y * Z * 4 * PAIR)
-    near_p = call(neighbour_kernel, shape(Y, LOCAL * NBR * PAIR, BLOCK), "vv")(got, pick_p)
-    near_p = [near_p[0]] + [
-        lax.ppermute(near_p[d], "y", [(i, (i - d) % Y) for i in range(Y)]) for d in range(1, Y)
-    ]
+    got_first = got
+
+    def neighbours(d, since):
+        rows = LOCAL * NBR * PAIR
+        near = call(neighbour_kernel, shape(rows, BLOCK), "vvh")(
+            got_first, pick_p[d * rows : (d + 1) * rows], since
+        )
+        return lax.ppermute(near, "y", [(i, (i - d) % Y) for i in range(Y)]) if d else near
+
     at_z = rows_at(place_z, PAD)
     pick_z = hot(at_z, Z * HELD * PAIR)
     put_z = (jnp.arange(Z * HELD * PAIR, dtype=jnp.int32)[:, None] == at_z[None, :]).astype(BF16)
@@ -348,9 +353,10 @@
         level1_kernel, out, "svv" + "h" * 5, [near_scratch] + held_scratch
     )(level, got, pick1, *ws)
     got = lax.all_to_all(msg, "z", 0, 0, tiled=True)
+    near1 = neighbours(1, solved)
     msg, solved = call(
         level2_kernel, (msg_z, held), "svv" + "h" * 5 + "vvhhhh", [near_scratch] + held_scratch
-    )(level, got, pick_z, *ws, q, solved, put_z, put_last, own_last, pick_p)
+    )(level, got, pick_z, *ws, q, solved, put_z, put_last, own_last, near1)
     got = lax.all_to_all(msg, "z", 0, 0, tiled=True)
     msg, solved, before = call(
         level3_kernel,
@@ -379,7 +385,7 @@
     column = jnp.arange(COUNT, dtype=jnp.int32)
     turn = (((column + PAIR * my) % COUNT)[:, None] == column[None, :]).astype(BF16)
     return call(final_kernel, out, "svvvvvvvvv")(
-        first, got, q_own, probes, inverses, turn, *near_p
+        first, got, q_own, probes, inverses, turn, neighbours(0, t), near1, neighbours(2, t), neighbours(3, t)
     )
 
 

time: 167 us -> 167 us (level)
  blocking collectives: 35.3 us -> 38 us
  waiting for transfers between devices: 43.1 us -> 41.1 us
    all_to_all x2, waiting for transfers between devices: 27.1 us -> 21.1 us  [body(): got = lax.all_to_all(msg, 'z', 0, 0, tiled=True)]
    all_to_all x2, waiting for transfers between devices: 12.2 us -> 16.6 us  [body(): got = lax.all_to_all(msg, ROWS, 0, 0, tiled=True)]
    all_to_all x2, starting transfers between devices: 27.6 us -> 24.4 us  [body(): got = lax.all_to_all(msg, ROWS, 0, 0, tiled=True)]
    all_to_all x2, blocking collectives: 35.3 us -> 38 us  [body(): got = lax.all_to_all(msg, 'z', 0, 0, tiled=True)]
    ppermute x3, starting transfers between devices: 10.3 us -> 12.9 us  [neighbours(): lax.ppermute(near, 'y', [(i, (i - d) % Y) for i in range(Y)])]
  transfers between devices with their start and end apart: 11 -> 11, of which waited for: 6 -> 7; matrix products, arithmetic and copies ran while one was open for 3% -> 3% of each run, Pallas kernels for 0% -> 0%
where the time goes in v5:
time: 167 us; the launch traced here: 166 us
  starting transfers between devices  59.2 us (35%)
  waiting for transfers between devices  41.1 us (25%)
  blocking collectives  38 us (23%)
  Pallas kernels  21.1 us (13%)
  other arithmetic  3.32 us (2%)
  local copies, waits for them, and re-layouts  2.64 us (2%)
    all_to_all x2, blocking collectives, body(): got = lax.all_to_all(msg, 'z', 0, 0, tiled=True)  38 us
    all_to_all x2, starting transfers between devices, body(): got = lax.all_to_all(msg, ROWS, 0, 0, tiled=True)  24.4 us
    all_to_all x2, waiting for transfers between devices, body(): got = lax.all_to_all(msg, 'z', 0, 0, tiled=True)  21.1 us
    all_to_all x2, waiting for transfers between devices, body(): got = lax.all_to_all(msg, ROWS, 0, 0, tiled=True)  16.6 us
    ppermute x3, starting transfers between devices, neighbours(): lax.ppermute(near, 'y', [(i, (i - d) % Y) for i in range(Y)])  12.9 us
    all_to_all x2, starting transfers between devices, body(): got = lax.all_to_all(msg, 'z', 0, 0, tiled=True)  9.65 us
    ppermute x1, starting transfers between devices, body(): w_far = lax.ppermute(w_send, 'y', [(i, (i + 2) % Y) for i in range(Y)])  4.81 us
    pallas_call x1, Pallas kernels, body(): call(back1_kernel, (shape(Y * Z, 2 * group, BLOCK // 2), held), 'sv' + 'h...  3.9 us
  transfers between devices with their start and end apart: 11, of which 7 were waited for; matrix products, arithmetic and copies ran while one was open for 3% of the time, Pallas kernels for 0%

profile of v5, /device:TPU:6, one launch (start us, length us, event | category | flops | bytes accessed | tf_op | source)
XLA Modules:
  0.0 166.4 jit_solution(13641710620057155922)
XLA Ops:
  0.7 2.8 %shard_map.86 = (bf16[2,8,256]{2,1,0:T(8,128)(2,1)}, bf16[64,8,256]{2,1,0:T(8,128)(2,1)}, bf16[2,4,256,256]{3,2,1,0:T(8,128)(2,1)}, bf16[4,256,256]{2,1,0:T(8,128)(2,1)}) custom-call(s32[1]{0:T(128)} %bitcast.core_ref, bf16[2,8,256]{2,1,0:T(8,128)(2,1)} %probes_ref.3, bf16[2,256,256]{2,1,0:T(8,128)(2,1)} %inv_ref.3, bf16[2,4,256,256]{3,2,1,0:T(8,128)(2,1)} %factor_ref.1), custom_call_target="tpu_custom_call" | custom-call | tf_op jit(solution)/shard_map/pallas_call | solution.py:255
  3.5 3.5 %collective-permute-start = (bf16[2,4,256,256]{3,2,1,0:T(8,128)(2,1)}, bf16[2,4,256,256]{3,2,1,0:T(8,128)(2,1)}, u32[]{:S(2)}, u32[]{:S(2)}) collective-permute-start(bf16[2,4,256,256]{3,2,1,0:T(8,128)(2,1)} %get-tuple-element.20.w0_ref), channel_id=1, source_target_pairs={{0,128},{128,256},{256,384},{384,0},{1,385},{129,1},{257,129},{385... | collective-permute-start | bytes 3145736 | tf_op jit(solution)/shard_map/ppermute | solution.py:260
  7.0 4.8 %collective-permute-start.2 = (bf16[4,256,256]{2,1,0:T(8,128)(2,1)}, bf16[4,256,256]{2,1,0:T(8,128)(2,1)S(1)}, u32[]{:S(2)}, u32[]{:S(2)}) collective-permute-start(bf16[4,256,256]{2,1,0:T(8,128)(2,1)} %get-tuple-element.21), channel_id=1, source_target_pairs={{0,256},{128,384},{256,0},{384,128},{1,257},{129,385},{257,1},{385... | collective-permute-start | bytes 1572872 | tf_op jit(solution)/shard_map/ppermute | solution.py:261
  11.8 16.9 %all-to-all-start = ((bf16[64,8,256]{2,1,0:T(8,128)(2,1)}), bf16[64,8,256]{2,1,0:T(8,128)(2,1)S(1)}, u32[]{:S(2)}, u32[]{:S(2)}) async-start(bf16[64,8,256]{2,1,0:T(8,128)(2,1)} %get-tuple-element.19), calls=%async_computation | async-start | bytes 524288 | tf_op jit(solution)/shard_map/all_to_all | solution.py:262
  28.8 0.1 add.460
  28.9 0.1 iota_add_fusion.1
  29.0 0.1 add.466
  29.2 0.1 add.502
  29.3 0.2 select_reduce_fusion.4
  29.5 0.1 iota_compare_fusion.12
  29.7 0.2 select_reduce_fusion.1
  29.9 0.1 copy.14
  30.0 0.3 select_reduce_fusion
  30.3 0.1 copy.15
  30.3 0.1 reduce_sum.72
  30.4 0.1 reduce_sum.70
  30.5 0.1 copy.17
  30.6 0.1 select_n.387
  30.7 0.1 add_select_fusion
  30.8 0.1 select_n.392
  31.0 0.1 add_select_fusion.1
  31.0 0.1 select_n.378
  31.2 0.1 select_n.381
  31.4 0.1 iota_compare_fusion.7
  31.4 0.1 fusion.3
  31.5 1.9 %collective-permute-start.1 = (bf16[2,4,256,256]{3,2,1,0:T(8,128)(2,1)}, bf16[2,4,256,256]{3,2,1,0:T(8,128)(2,1)S(1)}, u32[]{:S(2)}, u32[]{:S(2)}) collective-permute-start(bf16[2,4,256,256]{3,2,1,0:T(8,128)(2,1)} %collective-permute-done.w1_ref), channel_id=1, source_target_pairs={{0,1},{1,0},{2,3},{3,2},{4,5},{5,4},{6,7},{7,6},{8,9},{9,8},{10,11... | collective-permute-start | bytes 3145736 | tf_op jit(solution)/shard_map/ppermute | solution.py:264
  33.5 0.1 select_n.359
  33.6 0.1 select_n.364
  33.7 0.1 iota_compare_fusion.2
  33.8 0.1 iota_compare_fusion.1
  33.9 0.1 fusion.pick_ref
  34.0 0.3 collective-permute-done.2.w3_ref
  34.3 2.1 %collective-permute-start.3 = (bf16[4,256,256]{2,1,0:T(8,128)(2,1)S(1)}, bf16[4,256,256]{2,1,0:T(8,128)(2,1)S(1)}, u32[]{:S(2)}, u32[]{:S(2)}) collective-permute-start(bf16[4,256,256]{2,1,0:T(8,128)(2,1)S(1)} %collective-permute-done.2.w3_ref), channel_id=1, source_target_pairs={{0,1},{1,0},{2,3},{3,2},{4,5},{5,4},{6,7},{7,6},{8,9},{9,8},{10,11... | collective-permute-start | bytes 1572872 | tf_op jit(solution)/shard_map/ppermute | solution.py:264
  36.4 1.0 copy-done
  37.4 12.4 %all-to-all-done.got_ref = bf16[64,8,256]{2,1,0:T(8,128)(2,1)S(1)} async-done(((bf16[64,8,256]{2,1,0:T(8,128)(2,1)}), bf16[64,8,256]{2,1,0:T(8,128)(2,1)S(1)}, u32[]{:S(2)}, u32[]{:S(2)}) %all-to-all-start) | async-done | bytes 262176 | tf_op jit(solution)/shard_map/all_to_all | solution.py:262
  49.8 3.1 %shard_map.88 = (bf16[16,16,256]{2,1,0:T(8,128)(2,1)}, f32[16,256]{1,0:T(8,128)S(1)}, f32[64,256]{1,0:T(8,128)S(1)}) custom-call(s32[8]{0:T(128)S(1)} %get-tuple-element.44.level_ref, bf16[64,8,256]{2,1,0:T(8,128)(2,1)S(1)} %all-to-all-done.got_ref, bf16[320,512]{1,0:T(8,128)(2,1)S(1)} %fusion.pick_ref, bf16[2,4,256,256]{3,2,1,0:T(8,128)(2,1)} %get-tuple-element.20.w0_ref, ...), custom_call_target="tpu_custom_call" | custom-call | tf_op jit(solution)/shard_map/pallas_call | solution.py:352
  52.9 5.2 %all-to-all-start.1 = ((bf16[16,16,256]{2,1,0:T(8,128)(2,1)}), bf16[16,16,256]{2,1,0:T(8,128)(2,1)S(1)}, u32[]{:S(2)}, u32[]{:S(2)}) async-start(bf16[16,16,256]{2,1,0:T(8,128)(2,1)} %get-tuple-element.22), calls=%async_computation.1 | async-start | bytes 262144 | tf_op jit(solution)/shard_map/all_to_all | solution.py:355
  58.1 0.1 iota_compare_fusion.6
  58.2 0.1 select_n.373
  58.3 0.9 add_convert_fusion._b.put_ref
  59.2 0.1 fusion.2
  59.3 0.1 shard_map.89
  59.5 4.6 %collective-permute-start.4 = (bf16[16,256]{1,0:T(8,128)(2,1)S(1)}, bf16[16,256]{1,0:T(8,128)(2,1)S(1)}, u32[]{:S(2)}, u32[]{:S(2)}) collective-permute-start(bf16[16,256]{1,0:T(8,128)(2,1)S(1)} %shard_map.89), channel_id=1, source_target_pairs={{0,384},{128,0},{256,128},{384,256},{1,385},{129,1},{257,129},{385... | collective-permute-start | bytes 24584 | tf_op jit(solution)/shard_map/ppermute | solution.py:320
  64.1 0.3 copy.16
  64.4 1.0 collective-permute-done.4._d.near1_ref
  65.4 7.4 %all-to-all-done.1.got_ref = bf16[16,16,256]{2,1,0:T(8,128)(2,1)S(1)} async-done(((bf16[16,16,256]{2,1,0:T(8,128)(2,1)}), bf16[16,16,256]{2,1,0:T(8,128)(2,1)S(1)}, u32[]{:S(2)}, u32[]{:S(2)}) %all-to-all-start.1) | async-done | bytes 131104 | tf_op jit(solution)/shard_map/all_to_all | solution.py:355
  72.9 2.2 %shard_map.90 = (bf16[16,16,256]{2,1,0:T(8,128)(2,1)S(1)}, f32[16,256]{1,0:T(8,128)S(1)}) custom-call(s32[8]{0:T(128)S(1)} %get-tuple-element.44.level_ref, bf16[16,16,256]{2,1,0:T(8,128)(2,1)S(1)} %all-to-all-done.1.got_ref, bf16[256,256]{1,0:T(8,128)(2,1)S(1)} %get-tuple-element.54.pick_ref, bf16[2,4,256,256]{3,2,1,0:T(8,128)(2,1)} %get-tuple-element.20.w0_ref, ...), custom_call_target="tpu_custom_call" | custom-call | tf_op jit(solution)/shard_map/pallas_call | solution.py:357
  75.0 19.5 %all_to_all.30.got_ref = bf16[16,16,256]{2,1,0:T(8,128)(2,1)S(1)} all-to-all(bf16[16,16,256]{2,1,0:T(8,128)(2,1)S(1)} %get-tuple-element.25), channel_id=1, replica_groups=mesh['y'=4,'z'=16,'x'=4,'c'=2] {'z'}, dimensions={0} | all-to-all | bytes 262144 | tf_op jit(solution)/shard_map/all_to_all | solution.py:360
  94.5 2.8 %shard_map.91 = (bf16[16,16,256]{2,1,0:T(8,128)(2,1)S(1)}, f32[16,256]{1,0:T(8,128)S(1)}, f32[256,256]{1,0:T(8,128)S(1)}) custom-call(s32[8]{0:T(128)S(1)} %get-tuple-element.44.level_ref, bf16[16,16,256]{2,1,0:T(8,128)(2,1)S(1)} %all_to_all.30.got_ref, bf16[256,256]{1,0:T(8,128)(2,1)S(1)} %get-tuple-element.54.pick_ref, ...), custom_call_target="tpu_custom_call" | custom-call | tf_op jit(solution)/shard_map/pallas_call | solution.py:361
  97.3 18.5 %all_to_all.31.got_ref = bf16[16,16,256]{2,1,0:T(8,128)(2,1)S(1)} all-to-all(bf16[16,16,256]{2,1,0:T(8,128)(2,1)S(1)} %get-tuple-element.27), channel_id=1, replica_groups=mesh['y'=4,'z'=16,'x'=4,'c'=2] {'z'}, dimensions={0} | all-to-all | bytes 262144 | tf_op jit(solution)/shard_map/all_to_all | solution.py:367
  115.9 2.9 %shard_map.92 = (bf16[16,16,256]{2,1,0:T(8,128)(2,1)}, f32[16,256]{1,0:T(8,128)S(1)}, f32[256,256]{1,0:T(8,128)S(1)}) custom-call(s32[8]{0:T(128)S(1)} %get-tuple-element.44.level_ref, bf16[16,16,256]{2,1,0:T(8,128)(2,1)S(1)} %all_to_all.31.got_ref, bf16[2,4,256,256]{3,2,1,0:T(8,128)(2,1)} %get-tuple-element.20.w0_ref, ...), custom_call_target="tpu_custom_call" | custom-call | tf_op jit(solution)/shard_map/pallas_call | solution.py:368
  118.8 4.5 %all-to-all-start.4 = ((bf16[16,16,256]{2,1,0:T(8,128)(2,1)}), bf16[16,16,256]{2,1,0:T(8,128)(2,1)S(1)}, u32[]{:S(2)}, u32[]{:S(2)}) async-start(bf16[16,16,256]{2,1,0:T(8,128)(2,1)} %get-tuple-element.30), calls=%async_computation.4 | async-start | bytes 262144 | tf_op jit(solution)/shard_map/all_to_all | solution.py:374
  123.3 0.2 fusion.5
  123.5 13.6 %all-to-all-done.4.got_ref = bf16[16,16,256]{2,1,0:T(8,128)(2,1)S(1)} async-done(((bf16[16,16,256]{2,1,0:T(8,128)(2,1)}), bf16[16,16,256]{2,1,0:T(8,128)(2,1)S(1)}, u32[]{:S(2)}, u32[]{:S(2)}) %all-to-all-start.4) | async-done | bytes 131104 | tf_op jit(solution)/shard_map/all_to_all | solution.py:374
  137.1 3.9 %shard_map.93 = (bf16[64,8,128]{2,1,0:T(8,128)(2,1)}, f32[16,256]{1,0:T(8,128)S(1)}) custom-call(s32[8]{0:T(128)S(1)} %get-tuple-element.44.level_ref, bf16[16,16,256]{2,1,0:T(8,128)(2,1)S(1)} %all-to-all-done.4.got_ref, bf16[2,4,256,256]{3,2,1,0:T(8,128)(2,1)} %get-tuple-element.20.w0_ref, bf16[2,4,256,256]{3,2,1,0:T(8,128)(2,1)} %collective-permute-done.w1_ref, ...), custom_call_target="tpu_custom_call" | custom-call | tf_op jit(solution)/shard_map/pallas_call | solution.py:375
  141.0 7.5 %all-to-all-start.5 = ((bf16[64,8,128]{2,1,0:T(8,128)(2,1)}), bf16[64,8,128]{2,1,0:T(8,128)(2,1)S(1)}, u32[]{:S(2)}, u32[]{:S(2)}) async-start(bf16[64,8,128]{2,1,0:T(8,128)(2,1)} %get-tuple-element.33), calls=%async_computation.5 | async-start | bytes 262144 | tf_op jit(solution)/shard_map/all_to_all | solution.py:381
  148.6 0.1 shard_map.96
  148.7 3.5 %collective-permute-start.6 = (bf16[16,256]{1,0:T(8,128)(2,1)S(1)}, bf16[16,256]{1,0:T(8,128)(2,1)S(1)}, u32[]{:S(2)}, u32[]{:S(2)}) collective-permute-start(bf16[16,256]{1,0:T(8,128)(2,1)S(1)} %shard_map.96), channel_id=1, source_target_pairs={{0,128},{128,256},{256,384},{384,0},{1,129},{129,257},{257,385},{3... | collective-permute-start | bytes 24584 | tf_op jit(solution)/shard_map/ppermute | solution.py:320
  152.2 0.1 shard_map.95
  152.4 4.8 %collective-permute-start.5 = (bf16[16,256]{1,0:T(8,128)(2,1)S(1)}, bf16[16,256]{1,0:T(8,128)(2,1)S(1)}, u32[]{:S(2)}, u32[]{:S(2)}) collective-permute-start(bf16[16,256]{1,0:T(8,128)(2,1)S(1)} %shard_map.95), channel_id=1, source_target_pairs={{0,256},{128,384},{256,0},{384,128},{1,257},{129,385},{257,1},{385... | collective-permute-start | bytes 24584 | tf_op jit(solution)/shard_map/ppermute | solution.py:320
  157.2 0.1 shard_map.94.near0_ref
  157.3 2.1 %collective-permute-done.5.near2_ref = bf16[16,256]{1,0:T(8,128)(2,1)S(1)} collective-permute-done((bf16[16,256]{1,0:T(8,128)(2,1)S(1)}, bf16[16,256]{1,0:T(8,128)(2,1)S(1)}, u32[]{:S(2)}, u32[]{:S(2)}) %collective-permute-start.5) | collective-permute-done | bytes 8224 | tf_op jit(solution)/shard_map/ppermute | solution.py:320
  159.4 4.2 %all-to-all-done.5.got_ref = bf16[64,8,128]{2,1,0:T(8,128)(2,1)S(1)} async-done(((bf16[64,8,128]{2,1,0:T(8,128)(2,1)}), bf16[64,8,128]{2,1,0:T(8,128)(2,1)S(1)}, u32[]{:S(2)}, u32[]{:S(2)}) %all-to-all-start.5) | async-done | bytes 131104 | tf_op jit(solution)/shard_map/all_to_all | solution.py:381
  163.6 2.8 %shard_map.97 = (bf16[2,8,256]{2,1,0:T(8,128)(2,1)}, bf16[2,5,256,256]{3,2,1,0:T(8,128)(2,1)}) custom-call(s32[2]{0:T(128)S(1)} %compare_convert_fusion.1.first_ref, bf16[64,8,128]{2,1,0:T(8,128)(2,1)S(1)} %all-to-all-done.5.got_ref, bf16[2,8,256]{2,1,0:T(8,128)(2,1)S(1)} %copy-done.3, bf16[2,8,256]{2,1,0:T(8,128)(2,1)S(1)} %copy-done.2, ...), custom_call_target="tpu_custom_call" | custom-call | tf_op jit(solution)/shard_map/pallas_call | solution.py:387
  (46 shorter events, 0.7 us)
Async XLA Ops:
  0.6 28.1 %copy-start.6 = (s32[4]{0:T(128)S(1)}, s32[4]{0:T(128)}, u32[]{:S(2)}) copy-start(s32[4]{0:T(128)} %constant.199.clone) | copy-start | bytes 52
  0.6 28.3 %copy-start.7 = (s32[4]{0:T(128)S(1)}, s32[4]{0:T(128)}, u32[]{:S(2)}) copy-start(s32[4]{0:T(128)} %constant.200.clone) | copy-start | bytes 52
  0.7 28.6 %copy-start.4 = (s32[128]{0:T(128)S(1)}, s32[128]{0:T(128)}, u32[]{:S(2)}) copy-start(s32[128]{0:T(128)} %param.11) | copy-start | bytes 1540
  0.7 29.0 %copy-start.5 = (s32[128,4]{0,1:T(4,128)S(1)}, s32[128,4]{0,1:T(4,128)}, u32[]{:S(2)}) copy-start(s32[128,4]{0,1:T(4,128)} %param.10) | copy-start | bytes 6148
  3.5 28.0 %collective-permute-start = (bf16[2,4,256,256]{3,2,1,0:T(8,128)(2,1)}, bf16[2,4,256,256]{3,2,1,0:T(8,128)(2,1)}, u32[]{:S(2)}, u32[]{:S(2)}) collective-permute-start(bf16[2,4,256,256]{3,2,1,0:T(8,128)(2,1)} %get-tuple-element.20.w0_ref), channel_id=1, source_target_pairs={{0,128},{128,256},{256,384},{384,0},{1,385},{129,1},{257,129},{385... | collective-permute-start | bytes 3145736 | tf_op jit(solution)/shard_map/ppermute | solution.py:260
  7.0 27.3 %collective-permute-start.2 = (bf16[4,256,256]{2,1,0:T(8,128)(2,1)}, bf16[4,256,256]{2,1,0:T(8,128)(2,1)S(1)}, u32[]{:S(2)}, u32[]{:S(2)}) collective-permute-start(bf16[4,256,256]{2,1,0:T(8,128)(2,1)} %get-tuple-element.21), channel_id=1, source_target_pairs={{0,256},{128,384},{256,0},{384,128},{1,257},{129,385},{257,1},{385... | collective-permute-start | bytes 1572872 | tf_op jit(solution)/shard_map/ppermute | solution.py:261
  11.8 38.0 %all-to-all-start = ((bf16[64,8,256]{2,1,0:T(8,128)(2,1)}), bf16[64,8,256]{2,1,0:T(8,128)(2,1)S(1)}, u32[]{:S(2)}, u32[]{:S(2)}) async-start(bf16[64,8,256]{2,1,0:T(8,128)(2,1)} %get-tuple-element.19), calls=%async_computation | async-start | bytes 524288 | tf_op jit(solution)/shard_map/all_to_all | solution.py:262
  31.5 4.9 %collective-permute-start.1 = (bf16[2,4,256,256]{3,2,1,0:T(8,128)(2,1)}, bf16[2,4,256,256]{3,2,1,0:T(8,128)(2,1)S(1)}, u32[]{:S(2)}, u32[]{:S(2)}) collective-permute-start(bf16[2,4,256,256]{3,2,1,0:T(8,128)(2,1)} %collective-permute-done.w1_ref), channel_id=1, source_target_pairs={{0,1},{1,0},{2,3},{3,2},{4,5},{5,4},{6,7},{7,6},{8,9},{9,8},{10,11... | collective-permute-start | bytes 3145736 | tf_op jit(solution)/shard_map/ppermute | solution.py:264
  34.3 15.6 %collective-permute-start.3 = (bf16[4,256,256]{2,1,0:T(8,128)(2,1)S(1)}, bf16[4,256,256]{2,1,0:T(8,128)(2,1)S(1)}, u32[]{:S(2)}, u32[]{:S(2)}) collective-permute-start(bf16[4,256,256]{2,1,0:T(8,128)(2,1)S(1)} %collective-permute-done.2.w3_ref), channel_id=1, source_target_pairs={{0,1},{1,0},{2,3},{3,2},{4,5},{5,4},{6,7},{7,6},{8,9},{9,8},{10,11... | collective-permute-start | bytes 1572872 | tf_op jit(solution)/shard_map/ppermute | solution.py:264
  36.4 1.0 copy-start
  52.9 19.9 %all-to-all-start.1 = ((bf16[16,16,256]{2,1,0:T(8,128)(2,1)}), bf16[16,16,256]{2,1,0:T(8,128)(2,1)S(1)}, u32[]{:S(2)}, u32[]{:S(2)}) async-start(bf16[16,16,256]{2,1,0:T(8,128)(2,1)} %get-tuple-element.22), calls=%async_computation.1 | async-start | bytes 262144 | tf_op jit(solution)/shard_map/all_to_all | solution.py:355
  59.5 5.9 %collective-permute-start.4 = (bf16[16,256]{1,0:T(8,128)(2,1)S(1)}, bf16[16,256]{1,0:T(8,128)(2,1)S(1)}, u32[]{:S(2)}, u32[]{:S(2)}) collective-permute-start(bf16[16,256]{1,0:T(8,128)(2,1)S(1)} %shard_map.89), channel_id=1, source_target_pairs={{0,384},{128,0},{256,128},{384,256},{1,385},{129,1},{257,129},{385... | collective-permute-start | bytes 24584 | tf_op jit(solution)/shard_map/ppermute | solution.py:320
  118.8 18.3 %all-to-all-start.4 = ((bf16[16,16,256]{2,1,0:T(8,128)(2,1)}), bf16[16,16,256]{2,1,0:T(8,128)(2,1)S(1)}, u32[]{:S(2)}, u32[]{:S(2)}) async-start(bf16[16,16,256]{2,1,0:T(8,128)(2,1)} %get-tuple-element.30), calls=%async_computation.4 | async-start | bytes 262144 | tf_op jit(solution)/shard_map/all_to_all | solution.py:374
  137.1 26.5 %copy-start.2 = (bf16[2,8,256]{2,1,0:T(8,128)(2,1)S(1)}, bf16[2,8,256]{2,1,0:T(8,128)(2,1)}, u32[]{:S(2)}) copy-start(bf16[2,8,256]{2,1,0:T(8,128)(2,1)} %probes_ref.3) | copy-start | bytes 24580
  137.1 26.5 %copy-start.3 = (bf16[2,8,256]{2,1,0:T(8,128)(2,1)S(1)}, bf16[2,8,256]{2,1,0:T(8,128)(2,1)}, u32[]{:S(2)}) copy-start(bf16[2,8,256]{2,1,0:T(8,128)(2,1)} %get-tuple-element.34.q_ref) | copy-start | bytes 24580
  141.0 22.6 %copy-start.1 = (bf16[2,256,256]{2,1,0:T(8,128)(2,1)S(1)}, bf16[2,256,256]{2,1,0:T(8,128)(2,1)}, u32[]{:S(2)}) copy-start(bf16[2,256,256]{2,1,0:T(8,128)(2,1)} %inv_ref.3) | copy-start | bytes 786436
  141.0 22.6 %all-to-all-start.5 = ((bf16[64,8,128]{2,1,0:T(8,128)(2,1)}), bf16[64,8,128]{2,1,0:T(8,128)(2,1)S(1)}, u32[]{:S(2)}, u32[]{:S(2)}) async-start(bf16[64,8,128]{2,1,0:T(8,128)(2,1)} %get-tuple-element.33), calls=%async_computation.5 | async-start | bytes 262144 | tf_op jit(solution)/shard_map/all_to_all | solution.py:381
  148.7 8.6 %collective-permute-start.6 = (bf16[16,256]{1,0:T(8,128)(2,1)S(1)}, bf16[16,256]{1,0:T(8,128)(2,1)S(1)}, u32[]{:S(2)}, u32[]{:S(2)}) collective-permute-start(bf16[16,256]{1,0:T(8,128)(2,1)S(1)} %shard_map.96), channel_id=1, source_target_pairs={{0,128},{128,256},{256,384},{384,0},{1,129},{129,257},{257,385},{3... | collective-permute-start | bytes 24584 | tf_op jit(solution)/shard_map/ppermute | solution.py:320
  152.4 7.0 %collective-permute-start.5 = (bf16[16,256]{1,0:T(8,128)(2,1)S(1)}, bf16[16,256]{1,0:T(8,128)(2,1)S(1)}, u32[]{:S(2)}, u32[]{:S(2)}) collective-permute-start(bf16[16,256]{1,0:T(8,128)(2,1)S(1)} %shard_map.95), channel_id=1, source_target_pairs={{0,256},{128,384},{256,0},{384,128},{1,257},{129,385},{257,1},{385... | collective-permute-start | bytes 24584 | tf_op jit(solution)/shard_map/ppermute | solution.py:320

commit v6 on v5

--- a/solution.py
+++ b/solution.py
@@ -209,8 +209,16 @@
     sums = before_ref[...] + terms_ref[...]
     t = t_ref[...].astype(BF16)
     half = BLOCK // 2
-    left = scatter(put_ref[0], sums[:, :half]) + dot(own_ref[0], t[:, :half])
-    right = scatter(put_ref[1], sums[:, half:]) + dot(own_ref[1], t[:, half:])
+    group = LOCAL * PAIR
+    size = Y * Z * 2 * group
+
+    def hot(at, h):
+        rows = lax.broadcasted_iota(jnp.int32, (size, at.shape[1]), 0)
+        return jnp.where(rows == at + h * group, 1.0, 0.0).astype(BF16)
+
+    put_at, own_at = put_ref[...], own_ref[...]
+    left = scatter(hot(put_at, 0), sums[:, :half]) + dot(hot(own_at, 0), t[:, :half])
+    right = scatter(hot(put_at, 1), sums[:, half:]) + dot(hot(own_at, 1), t[:, half:])
     msg_ref[...] = (left + right).astype(BF16).reshape(msg_ref.shape)
 
 
@@ -328,16 +336,8 @@
     def last_at(slot, good):
         return jnp.where(good, (slot // LOCAL) * (2 * LOCAL) + slot % LOCAL, bad)
 
-    size = Y * Z * 2 * group
-    last_rows = jnp.arange(size, dtype=jnp.int32)
-    put_at = rows_at(last_at(src, level_of_src == 0), PAD)
-    own_at = rows_at(last_at(slots, level > 0), PAIR)
-    put_last = jnp.stack(
-        [(last_rows[:, None] == (put_at + h * group)[None, :]) for h in range(2)]
-    ).astype(BF16)
-    own_last = jnp.stack(
-        [(last_rows[:, None] == (own_at + h * group)[None, :]) for h in range(2)]
-    ).astype(BF16)
+    put_last = rows_at(last_at(src, level_of_src == 0), PAD).reshape(1, -1)
+    own_last = rows_at(last_at(slots, level > 0), PAIR).reshape(1, -1)
 
     near_scratch = pltpu.VMEM((WIDE, BLOCK), F32)
     held_scratch = [

time: 167 us -> 166 us (level)
  starting transfers between devices: 59.2 us -> 61.2 us
  transfers between devices with their start and end apart: 11 -> 11, of which waited for: 7 -> 6; matrix products, arithmetic and copies ran while one was open for 3% -> 2% of each run, Pallas kernels for 0% -> 0%
where the time goes in v6:
time: 166 us; the launch traced here: 165 us
  starting transfers between devices  61.2 us (37%)
  waiting for transfers between devices  41.1 us (25%)
  blocking collectives  36.9 us (22%)
  Pallas kernels  20.6 us (12%)
  local copies, waits for them, and re-layouts  2.37 us (1%)
  other arithmetic  2.04 us (1%)
    all_to_all x2, blocking collectives, body(): got = lax.all_to_all(msg, 'z', 0, 0, tiled=True)  36.9 us
    all_to_all x2, starting transfers between devices, body(): got = lax.all_to_all(msg, ROWS, 0, 0, tiled=True)  25.4 us
    all_to_all x2, waiting for transfers between devices, body(): got = lax.all_to_all(msg, 'z', 0, 0, tiled=True)  21.1 us
    all_to_all x2, waiting for transfers between devices, body(): got = lax.all_to_all(msg, ROWS, 0, 0, tiled=True)  16.8 us
    ppermute x3, starting transfers between devices, neighbours(): lax.ppermute(near, 'y', [(i, (i - d) % Y) for i in range(Y)])  13.1 us
    all_to_all x2, starting transfers between devices, body(): got = lax.all_to_all(msg, 'z', 0, 0, tiled=True)  9.76 us
    ppermute x1, starting transfers between devices, body(): w_far = lax.ppermute(w_send, 'y', [(i, (i + 2) % Y) for i in range(Y)])  4.81 us
    pallas_call x1, Pallas kernels, body(): call(level3_kernel, (msg_z, held, sums), 'svv' + 'h' * 5 + 'vvv', [near_s...  3.66 us
  transfers between devices with their start and end apart: 11, of which 6 were waited for; matrix products, arithmetic and copies ran while one was open for 2% of the time, Pallas kernels for 0%

profile of v6, /device:TPU:6, one launch (start us, length us, event | category | flops | bytes accessed | tf_op | source)
XLA Modules:
  0.0 165.2 jit_solution(15825461217541407859)
XLA Ops:
  0.7 2.8 %shard_map.86 = (bf16[2,8,256]{2,1,0:T(8,128)(2,1)}, bf16[64,8,256]{2,1,0:T(8,128)(2,1)}, bf16[2,4,256,256]{3,2,1,0:T(8,128)(2,1)}, bf16[4,256,256]{2,1,0:T(8,128)(2,1)}) custom-call(s32[1]{0:T(128)} %bitcast.core_ref, bf16[2,8,256]{2,1,0:T(8,128)(2,1)} %probes_ref.3, bf16[2,256,256]{2,1,0:T(8,128)(2,1)} %inv_ref.3, bf16[2,4,256,256]{3,2,1,0:T(8,128)(2,1)} %factor_ref.1), custom_call_target="tpu_custom_call" | custom-call | tf_op jit(solution)/shard_map/pallas_call | solution.py:263
  3.5 3.5 %collective-permute-start = (bf16[2,4,256,256]{3,2,1,0:T(8,128)(2,1)}, bf16[2,4,256,256]{3,2,1,0:T(8,128)(2,1)}, u32[]{:S(2)}, u32[]{:S(2)}) collective-permute-start(bf16[2,4,256,256]{3,2,1,0:T(8,128)(2,1)} %get-tuple-element.20.w0_ref), channel_id=1, source_target_pairs={{0,128},{128,256},{256,384},{384,0},{1,385},{129,1},{257,129},{385... | collective-permute-start | bytes 3145736 | tf_op jit(solution)/shard_map/ppermute | solution.py:268
  7.0 4.8 %collective-permute-start.2 = (bf16[4,256,256]{2,1,0:T(8,128)(2,1)}, bf16[4,256,256]{2,1,0:T(8,128)(2,1)S(1)}, u32[]{:S(2)}, u32[]{:S(2)}) collective-permute-start(bf16[4,256,256]{2,1,0:T(8,128)(2,1)} %get-tuple-element.21), channel_id=1, source_target_pairs={{0,256},{128,384},{256,0},{384,128},{1,257},{129,385},{257,1},{385... | collective-permute-start | bytes 1572872 | tf_op jit(solution)/shard_map/ppermute | solution.py:269
  11.8 16.9 %all-to-all-start = ((bf16[64,8,256]{2,1,0:T(8,128)(2,1)}), bf16[64,8,256]{2,1,0:T(8,128)(2,1)S(1)}, u32[]{:S(2)}, u32[]{:S(2)}) async-start(bf16[64,8,256]{2,1,0:T(8,128)(2,1)} %get-tuple-element.19), calls=%async_computation | async-start | bytes 524288 | tf_op jit(solution)/shard_map/all_to_all | solution.py:270
  28.8 0.1 add.440
  28.8 0.1 add.441
  28.9 0.1 iota_add_fusion.1
  29.0 0.1 add.447
  29.1 0.1 iota_add_fusion
  29.1 0.1 add.480
  29.3 0.2 select_reduce_fusion.4
  29.5 0.1 iota_compare_fusion.8
  29.6 0.1 iota_compare_fusion.7
  29.6 0.2 select_reduce_fusion.1
  29.9 0.1 copy.12
  29.9 0.3 select_reduce_fusion
  30.2 0.1 copy.13
  30.3 0.1 reduce_sum.72
  30.4 0.1 reduce_sum.70
  30.6 0.1 add_select_fusion.5
  30.7 0.1 add_select_fusion.1
  30.7 2.7 %collective-permute-start.1 = (bf16[2,4,256,256]{3,2,1,0:T(8,128)(2,1)}, bf16[2,4,256,256]{3,2,1,0:T(8,128)(2,1)S(1)}, u32[]{:S(2)}, u32[]{:S(2)}) collective-permute-start(bf16[2,4,256,256]{3,2,1,0:T(8,128)(2,1)} %collective-permute-done.w1_ref), channel_id=1, source_target_pairs={{0,1},{1,0},{2,3},{3,2},{4,5},{5,4},{6,7},{7,6},{8,9},{9,8},{10,11... | collective-permute-start | bytes 3145736 | tf_op jit(solution)/shard_map/ppermute | solution.py:272
  33.5 0.1 select_n.357
  33.6 0.1 select_n.362
  33.6 0.1 copy.14
  33.7 0.1 select_n.385
  33.8 0.1 add_select_fusion
  33.9 0.1 select_n.390
  34.0 0.1 fusion.3
  34.1 0.1 fusion.pick_ref
  34.2 0.0 collective-permute-done.2.w3_ref
  34.3 1.9 %collective-permute-start.3 = (bf16[4,256,256]{2,1,0:T(8,128)(2,1)S(1)}, bf16[4,256,256]{2,1,0:T(8,128)(2,1)S(1)}, u32[]{:S(2)}, u32[]{:S(2)}) collective-permute-start(bf16[4,256,256]{2,1,0:T(8,128)(2,1)S(1)} %collective-permute-done.2.w3_ref), channel_id=1, source_target_pairs={{0,1},{1,0},{2,3},{3,2},{4,5},{5,4},{6,7},{7,6},{8,9},{9,8},{10,11... | collective-permute-start | bytes 1572872 | tf_op jit(solution)/shard_map/ppermute | solution.py:272
  36.2 1.0 copy-done
  37.2 12.6 %all-to-all-done.got_ref = bf16[64,8,256]{2,1,0:T(8,128)(2,1)S(1)} async-done(((bf16[64,8,256]{2,1,0:T(8,128)(2,1)}), bf16[64,8,256]{2,1,0:T(8,128)(2,1)S(1)}, u32[]{:S(2)}, u32[]{:S(2)}) %all-to-all-start) | async-done | bytes 262176 | tf_op jit(solution)/shard_map/all_to_all | solution.py:270
  49.8 2.8 %shard_map.88 = (bf16[16,16,256]{2,1,0:T(8,128)(2,1)}, f32[16,256]{1,0:T(8,128)S(1)}, f32[64,256]{1,0:T(8,128)S(1)}) custom-call(s32[8]{0:T(128)S(1)} %get-tuple-element.44.level_ref, bf16[64,8,256]{2,1,0:T(8,128)(2,1)S(1)} %all-to-all-done.got_ref, bf16[320,512]{1,0:T(8,128)(2,1)S(1)} %fusion.pick_ref, bf16[2,4,256,256]{3,2,1,0:T(8,128)(2,1)} %get-tuple-element.20.w0_ref, ...), custom_call_target="tpu_custom_call" | custom-call | tf_op jit(solution)/shard_map/pallas_call | solution.py:352
  52.7 5.4 %all-to-all-start.1 = ((bf16[16,16,256]{2,1,0:T(8,128)(2,1)}), bf16[16,16,256]{2,1,0:T(8,128)(2,1)S(1)}, u32[]{:S(2)}, u32[]{:S(2)}) async-start(bf16[16,16,256]{2,1,0:T(8,128)(2,1)} %get-tuple-element.22), calls=%async_computation.1 | async-start | bytes 262144 | tf_op jit(solution)/shard_map/all_to_all | solution.py:355
  58.2 0.1 select_n.371
  58.2 0.1 fusion.2
  58.4 0.1 shard_map.89
  58.5 4.9 %collective-permute-start.4 = (bf16[16,256]{1,0:T(8,128)(2,1)S(1)}, bf16[16,256]{1,0:T(8,128)(2,1)S(1)}, u32[]{:S(2)}, u32[]{:S(2)}) collective-permute-start(bf16[16,256]{1,0:T(8,128)(2,1)S(1)} %shard_map.89), channel_id=1, source_target_pairs={{0,384},{128,0},{256,128},{384,256},{1,385},{129,1},{257,129},{385... | collective-permute-start | bytes 24584 | tf_op jit(solution)/shard_map/ppermute | solution.py:328
  63.4 0.1 add_select_fusion.4
  63.5 0.1 select_n.376._b.put_ref
  63.5 0.1 select_n.379._c.own_ref
  63.6 1.1 collective-permute-done.4._d.near1_ref
  64.7 8.1 %all-to-all-done.1.got_ref = bf16[16,16,256]{2,1,0:T(8,128)(2,1)S(1)} async-done(((bf16[16,16,256]{2,1,0:T(8,128)(2,1)}), bf16[16,16,256]{2,1,0:T(8,128)(2,1)S(1)}, u32[]{:S(2)}, u32[]{:S(2)}) %all-to-all-start.1) | async-done | bytes 131104 | tf_op jit(solution)/shard_map/all_to_all | solution.py:355
  72.9 1.9 %shard_map.90 = (bf16[16,16,256]{2,1,0:T(8,128)(2,1)S(1)}, f32[16,256]{1,0:T(8,128)S(1)}) custom-call(s32[8]{0:T(128)S(1)} %get-tuple-element.44.level_ref, bf16[16,16,256]{2,1,0:T(8,128)(2,1)S(1)} %all-to-all-done.1.got_ref, bf16[256,256]{1,0:T(8,128)(2,1)S(1)} %get-tuple-element.54.pick_ref, bf16[2,4,256,256]{3,2,1,0:T(8,128)(2,1)} %get-tuple-element.20.w0_ref, ...), custom_call_target="tpu_custom_call" | custom-call | tf_op jit(solution)/shard_map/pallas_call | solution.py:357
  74.8 19.5 %all_to_all.30.got_ref = bf16[16,16,256]{2,1,0:T(8,128)(2,1)S(1)} all-to-all(bf16[16,16,256]{2,1,0:T(8,128)(2,1)S(1)} %get-tuple-element.25), channel_id=1, replica_groups=mesh['y'=4,'z'=16,'x'=4,'c'=2] {'z'}, dimensions={0} | all-to-all | bytes 262144 | tf_op jit(solution)/shard_map/all_to_all | solution.py:360
  94.3 3.7 %shard_map.91 = (bf16[16,16,256]{2,1,0:T(8,128)(2,1)S(1)}, f32[16,256]{1,0:T(8,128)S(1)}, f32[256,256]{1,0:T(8,128)S(1)}) custom-call(s32[8]{0:T(128)S(1)} %get-tuple-element.44.level_ref, bf16[16,16,256]{2,1,0:T(8,128)(2,1)S(1)} %all_to_all.30.got_ref, bf16[256,256]{1,0:T(8,128)(2,1)S(1)} %get-tuple-element.54.pick_ref, ...), custom_call_target="tpu_custom_call" | custom-call | tf_op jit(solution)/shard_map/pallas_call | solution.py:361
  97.9 17.4 %all_to_all.31.got_ref = bf16[16,16,256]{2,1,0:T(8,128)(2,1)S(1)} all-to-all(bf16[16,16,256]{2,1,0:T(8,128)(2,1)S(1)} %get-tuple-element.27), channel_id=1, replica_groups=mesh['y'=4,'z'=16,'x'=4,'c'=2] {'z'}, dimensions={0} | all-to-all | bytes 262144 | tf_op jit(solution)/shard_map/all_to_all | solution.py:367
  115.4 2.7 %shard_map.92 = (bf16[16,16,256]{2,1,0:T(8,128)(2,1)}, f32[16,256]{1,0:T(8,128)S(1)}, f32[256,256]{1,0:T(8,128)S(1)}) custom-call(s32[8]{0:T(128)S(1)} %get-tuple-element.44.level_ref, bf16[16,16,256]{2,1,0:T(8,128)(2,1)S(1)} %all_to_all.31.got_ref, bf16[2,4,256,256]{3,2,1,0:T(8,128)(2,1)} %get-tuple-element.20.w0_ref, ...), custom_call_target="tpu_custom_call" | custom-call | tf_op jit(solution)/shard_map/pallas_call | solution.py:368
  118.1 4.3 %all-to-all-start.4 = ((bf16[16,16,256]{2,1,0:T(8,128)(2,1)}), bf16[16,16,256]{2,1,0:T(8,128)(2,1)S(1)}, u32[]{:S(2)}, u32[]{:S(2)}) async-start(bf16[16,16,256]{2,1,0:T(8,128)(2,1)} %get-tuple-element.30), calls=%async_computation.4 | async-start | bytes 262144 | tf_op jit(solution)/shard_map/all_to_all | solution.py:374
  122.5 0.2 fusion.5
  122.6 12.9 %all-to-all-done.4.got_ref = bf16[16,16,256]{2,1,0:T(8,128)(2,1)S(1)} async-done(((bf16[16,16,256]{2,1,0:T(8,128)(2,1)}), bf16[16,16,256]{2,1,0:T(8,128)(2,1)S(1)}, u32[]{:S(2)}, u32[]{:S(2)}) %all-to-all-start.4) | async-done | bytes 131104 | tf_op jit(solution)/shard_map/all_to_all | solution.py:374
  135.6 3.2 %shard_map.93 = (bf16[64,8,128]{2,1,0:T(8,128)(2,1)}, f32[16,256]{1,0:T(8,128)S(1)}) custom-call(s32[8]{0:T(128)S(1)} %get-tuple-element.44.level_ref, bf16[16,16,256]{2,1,0:T(8,128)(2,1)S(1)} %all-to-all-done.4.got_ref, bf16[2,4,256,256]{3,2,1,0:T(8,128)(2,1)} %get-tuple-element.20.w0_ref, bf16[2,4,256,256]{3,2,1,0:T(8,128)(2,1)} %collective-permute-done.w1_ref, ...), custom_call_target="tpu_custom_call" | custom-call | tf_op jit(solution)/shard_map/pallas_call | solution.py:375
  138.8 8.5 %all-to-all-start.5 = ((bf16[64,8,128]{2,1,0:T(8,128)(2,1)}), bf16[64,8,128]{2,1,0:T(8,128)(2,1)S(1)}, u32[]{:S(2)}, u32[]{:S(2)}) async-start(bf16[64,8,128]{2,1,0:T(8,128)(2,1)} %get-tuple-element.33), calls=%async_computation.5 | async-start | bytes 262144 | tf_op jit(solution)/shard_map/all_to_all | solution.py:381
  147.3 0.1 fusion.4.turn_ref
  147.4 0.1 shard_map.96
  147.5 3.5 %collective-permute-start.6 = (bf16[16,256]{1,0:T(8,128)(2,1)S(1)}, bf16[16,256]{1,0:T(8,128)(2,1)S(1)}, u32[]{:S(2)}, u32[]{:S(2)}) collective-permute-start(bf16[16,256]{1,0:T(8,128)(2,1)S(1)} %shard_map.96), channel_id=1, source_target_pairs={{0,128},{128,256},{256,384},{384,0},{1,129},{129,257},{257,385},{3... | collective-permute-start | bytes 24584 | tf_op jit(solution)/shard_map/ppermute | solution.py:328
  151.0 0.1 shard_map.95
  151.2 4.8 %collective-permute-start.5 = (bf16[16,256]{1,0:T(8,128)(2,1)S(1)}, bf16[16,256]{1,0:T(8,128)(2,1)S(1)}, u32[]{:S(2)}, u32[]{:S(2)}) collective-permute-start(bf16[16,256]{1,0:T(8,128)(2,1)S(1)} %shard_map.95), channel_id=1, source_target_pairs={{0,256},{128,384},{256,0},{384,128},{1,257},{129,385},{257,1},{385... | collective-permute-start | bytes 24584 | tf_op jit(solution)/shard_map/ppermute | solution.py:328
  156.0 0.1 shard_map.94.near0_ref
  156.1 2.1 %collective-permute-done.5.near2_ref = bf16[16,256]{1,0:T(8,128)(2,1)S(1)} collective-permute-done((bf16[16,256]{1,0:T(8,128)(2,1)S(1)}, bf16[16,256]{1,0:T(8,128)(2,1)S(1)}, u32[]{:S(2)}, u32[]{:S(2)}) %collective-permute-start.5) | collective-permute-done | bytes 8224 | tf_op jit(solution)/shard_map/ppermute | solution.py:328
  158.2 4.2 %all-to-all-done.5.got_ref = bf16[64,8,128]{2,1,0:T(8,128)(2,1)S(1)} async-done(((bf16[64,8,128]{2,1,0:T(8,128)(2,1)}), bf16[64,8,128]{2,1,0:T(8,128)(2,1)S(1)}, u32[]{:S(2)}, u32[]{:S(2)}) %all-to-all-start.5) | async-done | bytes 131104 | tf_op jit(solution)/shard_map/all_to_all | solution.py:381
  162.4 2.8 %shard_map.97 = (bf16[2,8,256]{2,1,0:T(8,128)(2,1)}, bf16[2,5,256,256]{3,2,1,0:T(8,128)(2,1)}) custom-call(s32[2]{0:T(128)S(1)} %compare_convert_fusion.1.first_ref, bf16[64,8,128]{2,1,0:T(8,128)(2,1)S(1)} %all-to-all-done.5.got_ref, bf16[2,8,256]{2,1,0:T(8,128)(2,1)S(1)} %copy-done.3, bf16[2,8,256]{2,1,0:T(8,128)(2,1)S(1)} %copy-done.2, ...), custom_call_target="tpu_custom_call" | custom-call | tf_op jit(solution)/shard_map/pallas_call | solution.py:387
  (36 shorter events, 0.2 us)
Async XLA Ops:
  0.6 28.1 %copy-start.6 = (s32[4]{0:T(128)S(1)}, s32[4]{0:T(128)}, u32[]{:S(2)}) copy-start(s32[4]{0:T(128)} %constant.197.clone) | copy-start | bytes 52
  0.6 28.3 %copy-start.7 = (s32[4]{0:T(128)S(1)}, s32[4]{0:T(128)}, u32[]{:S(2)}) copy-start(s32[4]{0:T(128)} %constant.198.clone) | copy-start | bytes 52
  0.7 28.6 %copy-start.4 = (s32[128]{0:T(128)S(1)}, s32[128]{0:T(128)}, u32[]{:S(2)}) copy-start(s32[128]{0:T(128)} %param.11) | copy-start | bytes 1540
  0.7 29.0 %copy-start.5 = (s32[128,4]{0,1:T(4,128)S(1)}, s32[128,4]{0,1:T(4,128)}, u32[]{:S(2)}) copy-start(s32[128,4]{0,1:T(4,128)} %param.10) | copy-start | bytes 6148
  3.5 27.2 %collective-permute-start = (bf16[2,4,256,256]{3,2,1,0:T(8,128)(2,1)}, bf16[2,4,256,256]{3,2,1,0:T(8,128)(2,1)}, u32[]{:S(2)}, u32[]{:S(2)}) collective-permute-start(bf16[2,4,256,256]{3,2,1,0:T(8,128)(2,1)} %get-tuple-element.20.w0_ref), channel_id=1, source_target_pairs={{0,128},{128,256},{256,384},{384,0},{1,385},{129,1},{257,129},{385... | collective-permute-start | bytes 3145736 | tf_op jit(solution)/shard_map/ppermute | solution.py:268
  7.0 27.3 %collective-permute-start.2 = (bf16[4,256,256]{2,1,0:T(8,128)(2,1)}, bf16[4,256,256]{2,1,0:T(8,128)(2,1)S(1)}, u32[]{:S(2)}, u32[]{:S(2)}) collective-permute-start(bf16[4,256,256]{2,1,0:T(8,128)(2,1)} %get-tuple-element.21), channel_id=1, source_target_pairs={{0,256},{128,384},{256,0},{384,128},{1,257},{129,385},{257,1},{385... | collective-permute-start | bytes 1572872 | tf_op jit(solution)/shard_map/ppermute | solution.py:269
  11.8 38.0 %all-to-all-start = ((bf16[64,8,256]{2,1,0:T(8,128)(2,1)}), bf16[64,8,256]{2,1,0:T(8,128)(2,1)S(1)}, u32[]{:S(2)}, u32[]{:S(2)}) async-start(bf16[64,8,256]{2,1,0:T(8,128)(2,1)} %get-tuple-element.19), calls=%async_computation | async-start | bytes 524288 | tf_op jit(solution)/shard_map/all_to_all | solution.py:270
  30.7 5.4 %collective-permute-start.1 = (bf16[2,4,256,256]{3,2,1,0:T(8,128)(2,1)}, bf16[2,4,256,256]{3,2,1,0:T(8,128)(2,1)S(1)}, u32[]{:S(2)}, u32[]{:S(2)}) collective-permute-start(bf16[2,4,256,256]{3,2,1,0:T(8,128)(2,1)} %collective-permute-done.w1_ref), channel_id=1, source_target_pairs={{0,1},{1,0},{2,3},{3,2},{4,5},{5,4},{6,7},{7,6},{8,9},{9,8},{10,11... | collective-permute-start | bytes 3145736 | tf_op jit(solution)/shard_map/ppermute | solution.py:272
  34.3 15.6 %collective-permute-start.3 = (bf16[4,256,256]{2,1,0:T(8,128)(2,1)S(1)}, bf16[4,256,256]{2,1,0:T(8,128)(2,1)S(1)}, u32[]{:S(2)}, u32[]{:S(2)}) collective-permute-start(bf16[4,256,256]{2,1,0:T(8,128)(2,1)S(1)} %collective-permute-done.2.w3_ref), channel_id=1, source_target_pairs={{0,1},{1,0},{2,3},{3,2},{4,5},{5,4},{6,7},{7,6},{8,9},{9,8},{10,11... | collective-permute-start | bytes 1572872 | tf_op jit(solution)/shard_map/ppermute | solution.py:272
  36.2 1.0 copy-start
  52.7 20.2 %all-to-all-start.1 = ((bf16[16,16,256]{2,1,0:T(8,128)(2,1)}), bf16[16,16,256]{2,1,0:T(8,128)(2,1)S(1)}, u32[]{:S(2)}, u32[]{:S(2)}) async-start(bf16[16,16,256]{2,1,0:T(8,128)(2,1)} %get-tuple-element.22), calls=%async_computation.1 | async-start | bytes 262144 | tf_op jit(solution)/shard_map/all_to_all | solution.py:355
  58.5 6.2 %collective-permute-start.4 = (bf16[16,256]{1,0:T(8,128)(2,1)S(1)}, bf16[16,256]{1,0:T(8,128)(2,1)S(1)}, u32[]{:S(2)}, u32[]{:S(2)}) collective-permute-start(bf16[16,256]{1,0:T(8,128)(2,1)S(1)} %shard_map.89), channel_id=1, source_target_pairs={{0,384},{128,0},{256,128},{384,256},{1,385},{129,1},{257,129},{385... | collective-permute-start | bytes 24584 | tf_op jit(solution)/shard_map/ppermute | solution.py:328
  118.1 17.5 %all-to-all-start.4 = ((bf16[16,16,256]{2,1,0:T(8,128)(2,1)}), bf16[16,16,256]{2,1,0:T(8,128)(2,1)S(1)}, u32[]{:S(2)}, u32[]{:S(2)}) async-start(bf16[16,16,256]{2,1,0:T(8,128)(2,1)} %get-tuple-element.30), calls=%async_computation.4 | async-start | bytes 262144 | tf_op jit(solution)/shard_map/all_to_all | solution.py:374
  135.6 26.8 %copy-start.2 = (bf16[2,8,256]{2,1,0:T(8,128)(2,1)S(1)}, bf16[2,8,256]{2,1,0:T(8,128)(2,1)}, u32[]{:S(2)}) copy-start(bf16[2,8,256]{2,1,0:T(8,128)(2,1)} %probes_ref.3) | copy-start | bytes 24580
  135.6 26.8 %copy-start.3 = (bf16[2,8,256]{2,1,0:T(8,128)(2,1)S(1)}, bf16[2,8,256]{2,1,0:T(8,128)(2,1)}, u32[]{:S(2)}) copy-start(bf16[2,8,256]{2,1,0:T(8,128)(2,1)} %get-tuple-element.34.q_ref) | copy-start | bytes 24580
  138.8 23.6 %copy-start.1 = (bf16[2,256,256]{2,1,0:T(8,128)(2,1)S(1)}, bf16[2,256,256]{2,1,0:T(8,128)(2,1)}, u32[]{:S(2)}) copy-start(bf16[2,256,256]{2,1,0:T(8,128)(2,1)} %inv_ref.3) | copy-start | bytes 786436
  138.8 23.6 %all-to-all-start.5 = ((bf16[64,8,128]{2,1,0:T(8,128)(2,1)}), bf16[64,8,128]{2,1,0:T(8,128)(2,1)S(1)}, u32[]{:S(2)}, u32[]{:S(2)}) async-start(bf16[64,8,128]{2,1,0:T(8,128)(2,1)} %get-tuple-element.33), calls=%async_computation.5 | async-start | bytes 262144 | tf_op jit(solution)/shard_map/all_to_all | solution.py:381
  147.5 8.6 %collective-permute-start.6 = (bf16[16,256]{1,0:T(8,128)(2,1)S(1)}, bf16[16,256]{1,0:T(8,128)(2,1)S(1)}, u32[]{:S(2)}, u32[]{:S(2)}) collective-permute-start(bf16[16,256]{1,0:T(8,128)(2,1)S(1)} %shard_map.96), channel_id=1, source_target_pairs={{0,128},{128,256},{256,384},{384,0},{1,129},{129,257},{257,385},{3... | collective-permute-start | bytes 24584 | tf_op jit(solution)/shard_map/ppermute | solution.py:328
  151.2 7.0 %collective-permute-start.5 = (bf16[16,256]{1,0:T(8,128)(2,1)S(1)}, bf16[16,256]{1,0:T(8,128)(2,1)S(1)}, u32[]{:S(2)}, u32[]{:S(2)}) collective-permute-start(bf16[16,256]{1,0:T(8,128)(2,1)S(1)} %shard_map.95), channel_id=1, source_target_pairs={{0,256},{128,384},{256,0},{384,128},{1,257},{129,385},{257,1},{385... | collective-permute-start | bytes 24584 | tf_op jit(solution)/shard_map/ppermute | solution.py:328

commit v7 on v6

--- a/solution.py
+++ b/solution.py
@@ -134,8 +134,7 @@
 
 def scatter(place, terms):
     high = terms.astype(BF16)
-    low = (terms - high.astype(F32)).astype(BF16)
-    return dot(place, high) + dot(place, low)
+    return dot(place, high)
 
 
 def broadcast_to_z(value, msg_ref):

time: 166 us -> 166 us (level)
  no operation moved by 1% of the time
where the time goes in v7:
time: 166 us
  starting transfers between devices  61.7 us (37%)
  waiting for transfers between devices  41.9 us (25%)
  blocking collectives  38 us (23%)
  Pallas kernels  19.4 us (12%)
  local copies, waits for them, and re-layouts  2.37 us (1%)
  other arithmetic  2.04 us (1%)
    all_to_all x2, blocking collectives, body(): got = lax.all_to_all(msg, 'z', 0, 0, tiled=True)  38 us
    all_to_all x2, starting transfers between devices, body(): got = lax.all_to_all(msg, ROWS, 0, 0, tiled=True)  25.2 us
    all_to_all x2, waiting for transfers between devices, body(): got = lax.all_to_all(msg, 'z', 0, 0, tiled=True)  21.8 us
    all_to_all x2, waiting for transfers between devices, body(): got = lax.all_to_all(msg, ROWS, 0, 0, tiled=True)  16.8 us
    ppermute x3, starting transfers between devices, neighbours(): lax.ppermute(near, 'y', [(i, (i - d) % Y) for i in range(Y)])  13.1 us
    all_to_all x2, starting transfers between devices, body(): got = lax.all_to_all(msg, 'z', 0, 0, tiled=True)  10.5 us
    ppermute x1, starting transfers between devices, body(): w_far = lax.ppermute(w_send, 'y', [(i, (i + 2) % Y) for i in range(Y)])  4.81 us
    ppermute x1, starting transfers between devices, body(): w_near = lax.ppermute(w_own, ('y', 'c'), ring)  3.49 us
  transfers between devices with their start and end apart: 11, of which 6 were waited for; matrix products, arithmetic and copies ran while one was open for 2% of the time, Pallas kernels for 0%

profile of v7, /device:TPU:6, one launch (start us, length us, event | category | flops | bytes accessed | tf_op | source)
XLA Modules:
  0.0 166.5 jit_solution(12018122359791295487)
XLA Ops:
  0.7 2.8 %shard_map.86 = (bf16[2,8,256]{2,1,0:T(8,128)(2,1)}, bf16[64,8,256]{2,1,0:T(8,128)(2,1)}, bf16[2,4,256,256]{3,2,1,0:T(8,128)(2,1)}, bf16[4,256,256]{2,1,0:T(8,128)(2,1)}) custom-call(s32[1]{0:T(128)} %bitcast.core_ref, bf16[2,8,256]{2,1,0:T(8,128)(2,1)} %probes_ref.3, bf16[2,256,256]{2,1,0:T(8,128)(2,1)} %inv_ref.3, bf16[2,4,256,256]{3,2,1,0:T(8,128)(2,1)} %factor_ref.1), custom_call_target="tpu_custom_call" | custom-call | tf_op jit(solution)/shard_map/pallas_call | solution.py:262
  3.5 3.5 %collective-permute-start = (bf16[2,4,256,256]{3,2,1,0:T(8,128)(2,1)}, bf16[2,4,256,256]{3,2,1,0:T(8,128)(2,1)}, u32[]{:S(2)}, u32[]{:S(2)}) collective-permute-start(bf16[2,4,256,256]{3,2,1,0:T(8,128)(2,1)} %get-tuple-element.20.w0_ref), channel_id=1, source_target_pairs={{0,128},{128,256},{256,384},{384,0},{1,385},{129,1},{257,129},{385... | collective-permute-start | bytes 3145736 | tf_op jit(solution)/shard_map/ppermute | solution.py:267
  7.0 4.8 %collective-permute-start.2 = (bf16[4,256,256]{2,1,0:T(8,128)(2,1)}, bf16[4,256,256]{2,1,0:T(8,128)(2,1)S(1)}, u32[]{:S(2)}, u32[]{:S(2)}) collective-permute-start(bf16[4,256,256]{2,1,0:T(8,128)(2,1)} %get-tuple-element.21), channel_id=1, source_target_pairs={{0,256},{128,384},{256,0},{384,128},{1,257},{129,385},{257,1},{385... | collective-permute-start | bytes 1572872 | tf_op jit(solution)/shard_map/ppermute | solution.py:268
  11.8 16.9 %all-to-all-start = ((bf16[64,8,256]{2,1,0:T(8,128)(2,1)}), bf16[64,8,256]{2,1,0:T(8,128)(2,1)S(1)}, u32[]{:S(2)}, u32[]{:S(2)}) async-start(bf16[64,8,256]{2,1,0:T(8,128)(2,1)} %get-tuple-element.19), calls=%async_computation | async-start | bytes 524288 | tf_op jit(solution)/shard_map/all_to_all | solution.py:269
  28.8 0.1 add.440
  28.8 0.1 add.441
  28.9 0.1 iota_add_fusion.1
  29.0 0.1 add.447
  29.1 0.1 iota_add_fusion
  29.1 0.1 add.480
  29.3 0.2 select_reduce_fusion.4
  29.5 0.1 iota_compare_fusion.8
  29.6 0.1 iota_compare_fusion.7
  29.6 0.2 select_reduce_fusion.1
  29.9 0.1 copy.12
  29.9 0.3 select_reduce_fusion
  30.2 0.1 copy.13
  30.3 0.1 reduce_sum.72
  30.4 0.1 reduce_sum.70
  30.6 0.1 add_select_fusion.5
  30.7 0.1 add_select_fusion.1
  30.7 2.7 %collective-permute-start.1 = (bf16[2,4,256,256]{3,2,1,0:T(8,128)(2,1)}, bf16[2,4,256,256]{3,2,1,0:T(8,128)(2,1)S(1)}, u32[]{:S(2)}, u32[]{:S(2)}) collective-permute-start(bf16[2,4,256,256]{3,2,1,0:T(8,128)(2,1)} %collective-permute-done.w1_ref), channel_id=1, source_target_pairs={{0,1},{1,0},{2,3},{3,2},{4,5},{5,4},{6,7},{7,6},{8,9},{9,8},{10,11... | collective-permute-start | bytes 3145736 | tf_op jit(solution)/shard_map/ppermute | solution.py:271
  33.5 0.1 select_n.357
  33.6 0.1 select_n.362
  33.6 0.1 copy.14
  33.7 0.1 select_n.385
  33.8 0.1 add_select_fusion
  33.9 0.1 select_n.390
  34.0 0.1 fusion.3
  34.1 0.1 fusion.pick_ref
  34.2 0.0 collective-permute-done.2.w3_ref
  34.3 1.9 %collective-permute-start.3 = (bf16[4,256,256]{2,1,0:T(8,128)(2,1)S(1)}, bf16[4,256,256]{2,1,0:T(8,128)(2,1)S(1)}, u32[]{:S(2)}, u32[]{:S(2)}) collective-permute-start(bf16[4,256,256]{2,1,0:T(8,128)(2,1)S(1)} %collective-permute-done.2.w3_ref), channel_id=1, source_target_pairs={{0,1},{1,0},{2,3},{3,2},{4,5},{5,4},{6,7},{7,6},{8,9},{9,8},{10,11... | collective-permute-start | bytes 1572872 | tf_op jit(solution)/shard_map/ppermute | solution.py:271
  36.2 1.0 copy-done
  37.2 12.6 %all-to-all-done.got_ref = bf16[64,8,256]{2,1,0:T(8,128)(2,1)S(1)} async-done(((bf16[64,8,256]{2,1,0:T(8,128)(2,1)}), bf16[64,8,256]{2,1,0:T(8,128)(2,1)S(1)}, u32[]{:S(2)}, u32[]{:S(2)}) %all-to-all-start) | async-done | bytes 262176 | tf_op jit(solution)/shard_map/all_to_all | solution.py:269
  49.8 2.8 %shard_map.88 = (bf16[16,16,256]{2,1,0:T(8,128)(2,1)}, f32[16,256]{1,0:T(8,128)S(1)}, f32[64,256]{1,0:T(8,128)S(1)}) custom-call(s32[8]{0:T(128)S(1)} %get-tuple-element.44.level_ref, bf16[64,8,256]{2,1,0:T(8,128)(2,1)S(1)} %all-to-all-done.got_ref, bf16[320,512]{1,0:T(8,128)(2,1)S(1)} %fusion.pick_ref, bf16[2,4,256,256]{3,2,1,0:T(8,128)(2,1)} %get-tuple-element.20.w0_ref, ...), custom_call_target="tpu_custom_call" | custom-call | tf_op jit(solution)/shard_map/pallas_call | solution.py:351
  52.7 6.2 %all-to-all-start.1 = ((bf16[16,16,256]{2,1,0:T(8,128)(2,1)}), bf16[16,16,256]{2,1,0:T(8,128)(2,1)S(1)}, u32[]{:S(2)}, u32[]{:S(2)}) async-start(bf16[16,16,256]{2,1,0:T(8,128)(2,1)} %get-tuple-element.22), calls=%async_computation.1 | async-start | bytes 262144 | tf_op jit(solution)/shard_map/all_to_all | solution.py:354
  58.9 0.1 select_n.371
  59.0 0.1 fusion.2
  59.1 0.1 shard_map.89
  59.3 4.9 %collective-permute-start.4 = (bf16[16,256]{1,0:T(8,128)(2,1)S(1)}, bf16[16,256]{1,0:T(8,128)(2,1)S(1)}, u32[]{:S(2)}, u32[]{:S(2)}) collective-permute-start(bf16[16,256]{1,0:T(8,128)(2,1)S(1)} %shard_map.89), channel_id=1, source_target_pairs={{0,384},{128,0},{256,128},{384,256},{1,385},{129,1},{257,129},{385... | collective-permute-start | bytes 24584 | tf_op jit(solution)/shard_map/ppermute | solution.py:327
  64.1 0.1 add_select_fusion.4
  64.2 0.1 select_n.376._b.put_ref
  64.3 0.1 select_n.379._c.own_ref
  64.4 1.1 collective-permute-done.4._d.near1_ref
  65.5 8.1 %all-to-all-done.1.got_ref = bf16[16,16,256]{2,1,0:T(8,128)(2,1)S(1)} async-done(((bf16[16,16,256]{2,1,0:T(8,128)(2,1)}), bf16[16,16,256]{2,1,0:T(8,128)(2,1)S(1)}, u32[]{:S(2)}, u32[]{:S(2)}) %all-to-all-start.1) | async-done | bytes 131104 | tf_op jit(solution)/shard_map/all_to_all | solution.py:354
  73.6 1.9 %shard_map.90 = (bf16[16,16,256]{2,1,0:T(8,128)(2,1)S(1)}, f32[16,256]{1,0:T(8,128)S(1)}) custom-call(s32[8]{0:T(128)S(1)} %get-tuple-element.44.level_ref, bf16[16,16,256]{2,1,0:T(8,128)(2,1)S(1)} %all-to-all-done.1.got_ref, bf16[256,256]{1,0:T(8,128)(2,1)S(1)} %get-tuple-element.54.pick_ref, bf16[2,4,256,256]{3,2,1,0:T(8,128)(2,1)} %get-tuple-element.20.w0_ref, ...), custom_call_target="tpu_custom_call" | custom-call | tf_op jit(solution)/shard_map/pallas_call | solution.py:356
  75.6 19.7 %all_to_all.30.got_ref = bf16[16,16,256]{2,1,0:T(8,128)(2,1)S(1)} all-to-all(bf16[16,16,256]{2,1,0:T(8,128)(2,1)S(1)} %get-tuple-element.25), channel_id=1, replica_groups=mesh['y'=4,'z'=16,'x'=4,'c'=2] {'z'}, dimensions={0} | all-to-all | bytes 262144 | tf_op jit(solution)/shard_map/all_to_all | solution.py:359
  95.3 2.8 %shard_map.91 = (bf16[16,16,256]{2,1,0:T(8,128)(2,1)S(1)}, f32[16,256]{1,0:T(8,128)S(1)}, f32[256,256]{1,0:T(8,128)S(1)}) custom-call(s32[8]{0:T(128)S(1)} %get-tuple-element.44.level_ref, bf16[16,16,256]{2,1,0:T(8,128)(2,1)S(1)} %all_to_all.30.got_ref, bf16[256,256]{1,0:T(8,128)(2,1)S(1)} %get-tuple-element.54.pick_ref, ...), custom_call_target="tpu_custom_call" | custom-call | tf_op jit(solution)/shard_map/pallas_call | solution.py:360
  98.1 18.3 %all_to_all.31.got_ref = bf16[16,16,256]{2,1,0:T(8,128)(2,1)S(1)} all-to-all(bf16[16,16,256]{2,1,0:T(8,128)(2,1)S(1)} %get-tuple-element.27), channel_id=1, replica_groups=mesh['y'=4,'z'=16,'x'=4,'c'=2] {'z'}, dimensions={0} | all-to-all | bytes 262144 | tf_op jit(solution)/shard_map/all_to_all | solution.py:366
  116.4 2.7 %shard_map.92 = (bf16[16,16,256]{2,1,0:T(8,128)(2,1)}, f32[16,256]{1,0:T(8,128)S(1)}, f32[256,256]{1,0:T(8,128)S(1)}) custom-call(s32[8]{0:T(128)S(1)} %get-tuple-element.44.level_ref, bf16[16,16,256]{2,1,0:T(8,128)(2,1)S(1)} %all_to_all.31.got_ref, bf16[2,4,256,256]{3,2,1,0:T(8,128)(2,1)} %get-tuple-element.20.w0_ref, ...), custom_call_target="tpu_custom_call" | custom-call | tf_op jit(solution)/shard_map/pallas_call | solution.py:367
  119.1 4.3 %all-to-all-start.4 = ((bf16[16,16,256]{2,1,0:T(8,128)(2,1)}), bf16[16,16,256]{2,1,0:T(8,128)(2,1)S(1)}, u32[]{:S(2)}, u32[]{:S(2)}) async-start(bf16[16,16,256]{2,1,0:T(8,128)(2,1)} %get-tuple-element.30), calls=%async_computation.4 | async-start | bytes 262144 | tf_op jit(solution)/shard_map/all_to_all | solution.py:373
  123.4 0.2 fusion.5
  123.6 13.6 %all-to-all-done.4.got_ref = bf16[16,16,256]{2,1,0:T(8,128)(2,1)S(1)} async-done(((bf16[16,16,256]{2,1,0:T(8,128)(2,1)}), bf16[16,16,256]{2,1,0:T(8,128)(2,1)S(1)}, u32[]{:S(2)}, u32[]{:S(2)}) %all-to-all-start.4) | async-done | bytes 131104 | tf_op jit(solution)/shard_map/all_to_all | solution.py:373
  137.2 3.0 %shard_map.93 = (bf16[64,8,128]{2,1,0:T(8,128)(2,1)}, f32[16,256]{1,0:T(8,128)S(1)}) custom-call(s32[8]{0:T(128)S(1)} %get-tuple-element.44.level_ref, bf16[16,16,256]{2,1,0:T(8,128)(2,1)S(1)} %all-to-all-done.4.got_ref, bf16[2,4,256,256]{3,2,1,0:T(8,128)(2,1)} %get-tuple-element.20.w0_ref, bf16[2,4,256,256]{3,2,1,0:T(8,128)(2,1)} %collective-permute-done.w1_ref, ...), custom_call_target="tpu_custom_call" | custom-call | tf_op jit(solution)/shard_map/pallas_call | solution.py:374
  140.3 8.3 %all-to-all-start.5 = ((bf16[64,8,128]{2,1,0:T(8,128)(2,1)}), bf16[64,8,128]{2,1,0:T(8,128)(2,1)S(1)}, u32[]{:S(2)}, u32[]{:S(2)}) async-start(bf16[64,8,128]{2,1,0:T(8,128)(2,1)} %get-tuple-element.33), calls=%async_computation.5 | async-start | bytes 262144 | tf_op jit(solution)/shard_map/all_to_all | solution.py:380
  148.6 0.1 fusion.4.turn_ref
  148.7 0.1 shard_map.96
  148.8 3.5 %collective-permute-start.6 = (bf16[16,256]{1,0:T(8,128)(2,1)S(1)}, bf16[16,256]{1,0:T(8,128)(2,1)S(1)}, u32[]{:S(2)}, u32[]{:S(2)}) collective-permute-start(bf16[16,256]{1,0:T(8,128)(2,1)S(1)} %shard_map.96), channel_id=1, source_target_pairs={{0,128},{128,256},{256,384},{384,0},{1,129},{129,257},{257,385},{3... | collective-permute-start | bytes 24584 | tf_op jit(solution)/shard_map/ppermute | solution.py:327
  152.3 0.1 shard_map.95
  152.4 4.8 %collective-permute-start.5 = (bf16[16,256]{1,0:T(8,128)(2,1)S(1)}, bf16[16,256]{1,0:T(8,128)(2,1)S(1)}, u32[]{:S(2)}, u32[]{:S(2)}) collective-permute-start(bf16[16,256]{1,0:T(8,128)(2,1)S(1)} %shard_map.95), channel_id=1, source_target_pairs={{0,256},{128,384},{256,0},{384,128},{1,257},{129,385},{257,1},{385... | collective-permute-start | bytes 24584 | tf_op jit(solution)/shard_map/ppermute | solution.py:327
  157.2 0.1 shard_map.94.near0_ref
  157.4 2.1 %collective-permute-done.5.near2_ref = bf16[16,256]{1,0:T(8,128)(2,1)S(1)} collective-permute-done((bf16[16,256]{1,0:T(8,128)(2,1)S(1)}, bf16[16,256]{1,0:T(8,128)(2,1)S(1)}, u32[]{:S(2)}, u32[]{:S(2)}) %collective-permute-start.5) | collective-permute-done | bytes 8224 | tf_op jit(solution)/shard_map/ppermute | solution.py:327
  159.5 4.2 %all-to-all-done.5.got_ref = bf16[64,8,128]{2,1,0:T(8,128)(2,1)S(1)} async-done(((bf16[64,8,128]{2,1,0:T(8,128)(2,1)}), bf16[64,8,128]{2,1,0:T(8,128)(2,1)S(1)}, u32[]{:S(2)}, u32[]{:S(2)}) %all-to-all-start.5) | async-done | bytes 131104 | tf_op jit(solution)/shard_map/all_to_all | solution.py:380
  163.7 2.8 %shard_map.97 = (bf16[2,8,256]{2,1,0:T(8,128)(2,1)}, bf16[2,5,256,256]{3,2,1,0:T(8,128)(2,1)}) custom-call(s32[2]{0:T(128)S(1)} %compare_convert_fusion.1.first_ref, bf16[64,8,128]{2,1,0:T(8,128)(2,1)S(1)} %all-to-all-done.5.got_ref, bf16[2,8,256]{2,1,0:T(8,128)(2,1)S(1)} %copy-done.3, bf16[2,8,256]{2,1,0:T(8,128)(2,1)S(1)} %copy-done.2, ...), custom_call_target="tpu_custom_call" | custom-call | tf_op jit(solution)/shard_map/pallas_call | solution.py:386
  (36 shorter events, 0.2 us)
Async XLA Ops:
  0.6 28.1 %copy-start.6 = (s32[4]{0:T(128)S(1)}, s32[4]{0:T(128)}, u32[]{:S(2)}) copy-start(s32[4]{0:T(128)} %constant.197.clone) | copy-start | bytes 52
  0.6 28.3 %copy-start.7 = (s32[4]{0:T(128)S(1)}, s32[4]{0:T(128)}, u32[]{:S(2)}) copy-start(s32[4]{0:T(128)} %constant.198.clone) | copy-start | bytes 52
  0.7 28.6 %copy-start.4 = (s32[128]{0:T(128)S(1)}, s32[128]{0:T(128)}, u32[]{:S(2)}) copy-start(s32[128]{0:T(128)} %param.11) | copy-start | bytes 1540
  0.7 29.0 %copy-start.5 = (s32[128,4]{0,1:T(4,128)S(1)}, s32[128,4]{0,1:T(4,128)}, u32[]{:S(2)}) copy-start(s32[128,4]{0,1:T(4,128)} %param.10) | copy-start | bytes 6148
  3.5 27.2 %collective-permute-start = (bf16[2,4,256,256]{3,2,1,0:T(8,128)(2,1)}, bf16[2,4,256,256]{3,2,1,0:T(8,128)(2,1)}, u32[]{:S(2)}, u32[]{:S(2)}) collective-permute-start(bf16[2,4,256,256]{3,2,1,0:T(8,128)(2,1)} %get-tuple-element.20.w0_ref), channel_id=1, source_target_pairs={{0,128},{128,256},{256,384},{384,0},{1,385},{129,1},{257,129},{385... | collective-permute-start | bytes 3145736 | tf_op jit(solution)/shard_map/ppermute | solution.py:267
  7.0 27.3 %collective-permute-start.2 = (bf16[4,256,256]{2,1,0:T(8,128)(2,1)}, bf16[4,256,256]{2,1,0:T(8,128)(2,1)S(1)}, u32[]{:S(2)}, u32[]{:S(2)}) collective-permute-start(bf16[4,256,256]{2,1,0:T(8,128)(2,1)} %get-tuple-element.21), channel_id=1, source_target_pairs={{0,256},{128,384},{256,0},{384,128},{1,257},{129,385},{257,1},{385... | collective-permute-start | bytes 1572872 | tf_op jit(solution)/shard_map/ppermute | solution.py:268
  11.8 38.0 %all-to-all-start = ((bf16[64,8,256]{2,1,0:T(8,128)(2,1)}), bf16[64,8,256]{2,1,0:T(8,128)(2,1)S(1)}, u32[]{:S(2)}, u32[]{:S(2)}) async-start(bf16[64,8,256]{2,1,0:T(8,128)(2,1)} %get-tuple-element.19), calls=%async_computation | async-start | bytes 524288 | tf_op jit(solution)/shard_map/all_to_all | solution.py:269
  30.7 5.4 %collective-permute-start.1 = (bf16[2,4,256,256]{3,2,1,0:T(8,128)(2,1)}, bf16[2,4,256,256]{3,2,1,0:T(8,128)(2,1)S(1)}, u32[]{:S(2)}, u32[]{:S(2)}) collective-permute-start(bf16[2,4,256,256]{3,2,1,0:T(8,128)(2,1)} %collective-permute-done.w1_ref), channel_id=1, source_target_pairs={{0,1},{1,0},{2,3},{3,2},{4,5},{5,4},{6,7},{7,6},{8,9},{9,8},{10,11... | collective-permute-start | bytes 3145736 | tf_op jit(solution)/shard_map/ppermute | solution.py:271
  34.3 15.6 %collective-permute-start.3 = (bf16[4,256,256]{2,1,0:T(8,128)(2,1)S(1)}, bf16[4,256,256]{2,1,0:T(8,128)(2,1)S(1)}, u32[]{:S(2)}, u32[]{:S(2)}) collective-permute-start(bf16[4,256,256]{2,1,0:T(8,128)(2,1)S(1)} %collective-permute-done.2.w3_ref), channel_id=1, source_target_pairs={{0,1},{1,0},{2,3},{3,2},{4,5},{5,4},{6,7},{7,6},{8,9},{9,8},{10,11... | collective-permute-start | bytes 1572872 | tf_op jit(solution)/shard_map/ppermute | solution.py:271
  36.2 1.0 copy-start
  52.7 20.9 %all-to-all-start.1 = ((bf16[16,16,256]{2,1,0:T(8,128)(2,1)}), bf16[16,16,256]{2,1,0:T(8,128)(2,1)S(1)}, u32[]{:S(2)}, u32[]{:S(2)}) async-start(bf16[16,16,256]{2,1,0:T(8,128)(2,1)} %get-tuple-element.22), calls=%async_computation.1 | async-start | bytes 262144 | tf_op jit(solution)/shard_map/all_to_all | solution.py:354
  59.3 6.2 %collective-permute-start.4 = (bf16[16,256]{1,0:T(8,128)(2,1)S(1)}, bf16[16,256]{1,0:T(8,128)(2,1)S(1)}, u32[]{:S(2)}, u32[]{:S(2)}) collective-permute-start(bf16[16,256]{1,0:T(8,128)(2,1)S(1)} %shard_map.89), channel_id=1, source_target_pairs={{0,384},{128,0},{256,128},{384,256},{1,385},{129,1},{257,129},{385... | collective-permute-start | bytes 24584 | tf_op jit(solution)/shard_map/ppermute | solution.py:327
  119.1 18.1 %all-to-all-start.4 = ((bf16[16,16,256]{2,1,0:T(8,128)(2,1)}), bf16[16,16,256]{2,1,0:T(8,128)(2,1)S(1)}, u32[]{:S(2)}, u32[]{:S(2)}) async-start(bf16[16,16,256]{2,1,0:T(8,128)(2,1)} %get-tuple-element.30), calls=%async_computation.4 | async-start | bytes 262144 | tf_op jit(solution)/shard_map/all_to_all | solution.py:373
  137.2 26.5 %copy-start.2 = (bf16[2,8,256]{2,1,0:T(8,128)(2,1)S(1)}, bf16[2,8,256]{2,1,0:T(8,128)(2,1)}, u32[]{:S(2)}) copy-start(bf16[2,8,256]{2,1,0:T(8,128)(2,1)} %probes_ref.3) | copy-start | bytes 24580
  137.2 26.5 %copy-start.3 = (bf16[2,8,256]{2,1,0:T(8,128)(2,1)S(1)}, bf16[2,8,256]{2,1,0:T(8,128)(2,1)}, u32[]{:S(2)}) copy-start(bf16[2,8,256]{2,1,0:T(8,128)(2,1)} %get-tuple-element.34.q_ref) | copy-start | bytes 24580
  140.3 23.4 %copy-start.1 = (bf16[2,256,256]{2,1,0:T(8,128)(2,1)S(1)}, bf16[2,256,256]{2,1,0:T(8,128)(2,1)}, u32[]{:S(2)}) copy-start(bf16[2,256,256]{2,1,0:T(8,128)(2,1)} %inv_ref.3) | copy-start | bytes 786436
  140.3 23.4 %all-to-all-start.5 = ((bf16[64,8,128]{2,1,0:T(8,128)(2,1)}), bf16[64,8,128]{2,1,0:T(8,128)(2,1)S(1)}, u32[]{:S(2)}, u32[]{:S(2)}) async-start(bf16[64,8,128]{2,1,0:T(8,128)(2,1)} %get-tuple-element.33), calls=%async_computation.5 | async-start | bytes 262144 | tf_op jit(solution)/shard_map/all_to_all | solution.py:380
  148.8 8.6 %collective-permute-start.6 = (bf16[16,256]{1,0:T(8,128)(2,1)S(1)}, bf16[16,256]{1,0:T(8,128)(2,1)S(1)}, u32[]{:S(2)}, u32[]{:S(2)}) collective-permute-start(bf16[16,256]{1,0:T(8,128)(2,1)S(1)} %shard_map.96), channel_id=1, source_target_pairs={{0,128},{128,256},{256,384},{384,0},{1,129},{129,257},{257,385},{3... | collective-permute-start | bytes 24584 | tf_op jit(solution)/shard_map/ppermute | solution.py:327
  152.4 7.0 %collective-permute-start.5 = (bf16[16,256]{1,0:T(8,128)(2,1)S(1)}, bf16[16,256]{1,0:T(8,128)(2,1)S(1)}, u32[]{:S(2)}, u32[]{:S(2)}) collective-permute-start(bf16[16,256]{1,0:T(8,128)(2,1)S(1)} %shard_map.95), channel_id=1, source_target_pairs={{0,256},{128,384},{256,0},{384,128},{1,257},{129,385},{257,1},{385... | collective-permute-start | bytes 24584 | tf_op jit(solution)/shard_map/ppermute | solution.py:327
